TPU v7x, 32 devices: a whole 2x2x4 slice. The times are simulated.
32 devices in a mesh: groups: 2 (over x), expert: 8 (over z, y), tensor: 2 (over core).
Axes of the slice: x: 2, y: 2, z: 4, core: 2. Of those that a mesh axis runs over, the one named last changes fastest.
Arguments:
- tokens: bfloat16 [4096, 3584], P(('groups', 'expert', 'tensor')), parts along dimension 0, may hold values from -6 to 6
- router_weight: bfloat16 [256, 3584], P('expert'), may hold values from -0.09375 to 0.09375
- gate_weight: bfloat16 [8, 3584, 1024], P('expert', None, 'tensor'), may hold values from -0.09375 to 0.09375
- up_weight: bfloat16 [8, 3584, 1024], P('expert', None, 'tensor'), may hold values from -0.09375 to 0.09375
- down_weight: bfloat16 [8, 1024, 3584], P('expert', 'tensor'), may hold values from -0.1875 to 0.1875
- policy_logits: float32 [4096, 256], P(('groups', 'expert', 'tensor')), parts along dimension 0, may hold values from -18 to 18
- expert_ids: int32 [4096, 8], P(('groups', 'expert', 'tensor')), parts along dimension 0, may hold values from 0 to 255, as said below
- slots: int32 [4096, 8], P(('groups', 'expert', 'tensor')), parts along dimension 0, may hold values from 0 to 8, as said below
- occupancy: int32 [8, 32], P('expert', 'groups'), parts along dimension 1, may hold values from 0 to 8, as said below
- env_mask: int32 [4096], P(('groups', 'expert', 'tensor')), parts along dimension 0, may hold values 0 or 1
Outputs:
- mixed: bfloat16 [4096, 3584], P(('groups', 'expert', 'tensor')), parts along dimension 0
- kl_terms: float32 [4096], P(('groups', 'expert', 'tensor')), parts along dimension 0
There are 2 independent parts, one for each index of `groups`. A program takes and returns all parts, laid end to end along the dimension named above; an argument that names none is the same for every part. Nothing has to cross between parts.
Inputs may be any that keep to these rules, and one draw needn't show every extreme that they name: `expert_ids`: each row holds 8 different expert numbers; numbers below 8 are the experts held in this window. For a choice of a window expert that is placed, its slot among the 8 slots of its source device and expert; the placed choices of one source and expert hold the slots 0, 1, 2 and so on in order of token, then choice; 8 marks a choice that is not placed (expert outside the window or buffer full). occupancy[e, s] is the number of placed choices of source device s for window expert e; some expert is full from every source.
All inputs are finite; a program needn't handle non-finite values. No bound on the sum of `env_mask` on one device may be relied on, other than what follows from the above.
Results may differ from a plain program's by a relative error of at most 0.0074.
Values may be sent and summed in bfloat16 or wider, within the bound.
No kernel may reach another device: no remote copies, remote signals or barrier semaphores. Data moves between devices by JAX's collectives and lax.ppermute only.
A program may use at most 64 MiB of HBM per device.

v0:
```python
import jax
import jax.numpy as jnp
from jax import lax
from jax.sharding import PartitionSpec as P

CAP = 8


def placements(expert_ids, slots, count, capacity):
    valid = (expert_ids < count) & (slots < capacity)
    return jnp.where(valid, expert_ids * capacity + slots, -1)


def select_matrix(place, width):
    columns = jnp.arange(width, dtype=jnp.int32)
    hits = place[:, :, None] == columns[None, None, :]
    return jnp.any(hits, axis=1).astype(jnp.bfloat16)


def weighted_matrix(place, weights, width):
    columns = jnp.arange(width, dtype=jnp.int32)
    hits = place[:, :, None] == columns[None, None, :]
    picked = jnp.where(hits, weights[:, :, None], jnp.zeros((), jnp.bfloat16))
    return jnp.sum(picked, axis=1)


def router_terms(logits, policy_logits, expert_ids, env_mask):
    scores = jax.nn.sigmoid(logits)
    chosen = jnp.take_along_axis(scores, expert_ids, axis=1)
    combine_weights = (2.5 * chosen / jnp.sum(chosen, axis=1, keepdims=True)).astype(jnp.bfloat16)
    log_p = jax.nn.log_sigmoid(logits) - jnp.log(jnp.sum(scores, axis=1, keepdims=True))
    policy = jax.nn.sigmoid(policy_logits)
    log_q = jax.nn.log_sigmoid(policy_logits) - jnp.log(jnp.sum(policy, axis=1, keepdims=True))
    keep = (1 - env_mask).astype(jnp.float32)
    kl_terms = keep * jnp.sum(jnp.exp(log_q) * (log_q - log_p), axis=1)
    return (combine_weights, kl_terms)


def per_device(
    tokens,
    router_weight,
    gate_weight,
    up_weight,
    down_weight,
    policy_logits,
    expert_ids,
    slots,
    occupancy,
    env_mask,
):
    experts = lax.axis_size("expert")
    pairs = lax.axis_size("tensor")
    model_width = tokens.shape[1]
    logits = lax.dot_general(
        tokens,
        lax.all_gather(router_weight, "expert", axis=0, tiled=True),
        (((1,), (1,)), ((), ())),
        preferred_element_type=jnp.float32,
    )
    combine_weights, kl_terms = router_terms(logits, policy_logits, expert_ids, env_mask)
    width = experts * CAP
    place = placements(expert_ids, slots, experts, CAP)
    matrix = select_matrix(place, width)
    outgoing = lax.dot_general(
        matrix, tokens, (((0,), (0,)), ((), ())), preferred_element_type=jnp.float32
    )
    outgoing = outgoing.astype(jnp.bfloat16).reshape(experts, CAP, model_width)
    w_gate = gate_weight[0]
    w_up = up_weight[0]
    w_down = down_weight[0]
    capacity_iota = jnp.arange(CAP, dtype=jnp.int32)
    arrived = lax.all_to_all(outgoing, "expert", split_axis=0, concat_axis=0, tiled=True)
    ordered = occupancy[0].reshape(experts, pairs).T.reshape(-1)
    alive = (capacity_iota[None, :] < ordered[:, None]).reshape(-1)
    rows = lax.all_gather(arrived.reshape(-1, model_width), "tensor", axis=0, tiled=True)
    gate = jnp.dot(rows, w_gate, preferred_element_type=jnp.float32)
    up = jnp.dot(rows, w_up, preferred_element_type=jnp.float32)
    hidden = jnp.where(alive[:, None], jax.nn.silu(gate) * up, jnp.zeros((), jnp.float32)).astype(
        jnp.bfloat16
    )
    rows = hidden
    partial_value = lax.optimization_barrier(
        jnp.dot(rows, w_down, preferred_element_type=jnp.float32).astype(jnp.bfloat16)
    )
    summed = lax.psum_scatter(
        partial_value.astype(jnp.float32).astype(jnp.bfloat16),
        "tensor",
        scatter_dimension=0,
        tiled=True,
    )
    returned = lax.all_to_all(
        summed.reshape(experts, CAP, model_width), "expert", split_axis=0, concat_axis=0, tiled=True
    )
    combine_matrix = weighted_matrix(place, combine_weights, width)
    mixed = jnp.dot(
        combine_matrix, returned.reshape(width, model_width), preferred_element_type=jnp.float32
    ).astype(jnp.bfloat16)
    return (mixed, kl_terms)


def solution(mesh):
    in_specs = (
        P(("groups", "expert", "tensor"), None),
        P("expert", None),
        P("expert", None, "tensor"),
        P("expert", None, "tensor"),
        P("expert", "tensor", None),
        P(("groups", "expert", "tensor"), None),
        P(("groups", "expert", "tensor"), None),
        P(("groups", "expert", "tensor"), None),
        P("expert", "groups"),
        P(("groups", "expert", "tensor")),
    )
    out_specs = (P(("groups", "expert", "tensor"), None), P(("groups", "expert", "tensor")))
    return jax.shard_map(
        per_device, mesh=mesh, in_specs=in_specs, out_specs=out_specs, check_vma=False
    )
```

profile of v0, /device:TPU:0, one launch (start us, length us, event | category | flops | bytes accessed | tf_op | source)
XLA Modules:
  0.0 116.1 jit_solution(17714865205878004157)
XLA Ops:
  8.0 0.8 add_select_fusion
  8.8 0.4 copy-done
  9.2 1.1 fusion
  10.3 7.3 %all-to-all-start = ((bf16[8,8,3584]{2,1,0:T(8,128)(2,1)}), bf16[8,8,3584]{2,1,0:T(8,128)(2,1)S(1)}, u32[]{:S(2)}, u32[]{:S(2)}) async-start(bf16[8,8,3584]{2,1,0:T(8,128)(2,1)} %fusion), calls=%async_computation | async-start | bytes 917504 | tf_op jit(solution)/shard_map/all_to_all | solution.py:72
  17.6 0.5 broadcast.58
  18.1 1.3 %reduce.4 = s32[16]{0:T(128)S(1)} reduce(s32[1,16]{1,0:T(1,128)} %param.18, s32[]{:T(128)} %broadcast.58), dimensions={0}, to_apply=%param.18.reduce_sub_computation.3 | reduce | bytes 132 | tf_op args[8]
  19.5 0.1 copy.31
  19.7 0.1 lt.44
  19.9 10.8 %all-to-all-done = bf16[8,8,3584]{2,1,0:T(8,128)(2,1)S(1)} async-done(((bf16[8,8,3584]{2,1,0:T(8,128)(2,1)}), bf16[8,8,3584]{2,1,0:T(8,128)(2,1)S(1)}, u32[]{:S(2)}, u32[]{:S(2)}) %all-to-all-start) | async-done | bytes 458784 | tf_op jit(solution)/shard_map/all_to_all | solution.py:72
  30.6 2.5 %all_gather.7 = bf16[128,3584]{1,0:T(8,128)(2,1)S(1)} all-gather(bf16[64,3584]{1,0:T(8,128)(2,1)S(1)} %bitcast.36), channel_id=1, replica_groups=mesh['groups'=2,'expert'=8,'tensor'=2] {'tensor'}, dimensions={0}, use_global_device_ids=true | all-gather | bytes 1376256 | tf_op jit(solution)/shard_map/all_gather | solution.py:75
  33.1 2.7 %fusion.4 = f32[128,512]{1,0:T(8,128)S(1)} fusion(bf16[128,3584]{1,0:T(8,128)(2,1)S(1)} %all_gather.7, bf16[1,3584,512]{2,1,0:T(8,128)(2,1)} %param.12), kind=kOutput, calls=%fused_computation.8 | convolution fusion | flops 469762048 | bytes 4849664 | tf_op jit(solution)/shard_map/dot_general | solution.py:76
  35.8 5.4 %convolution_convert_fusion.1 = bf16[128,3584]{1,0:T(8,128)(2,1)} fusion(bf16[1,512,3584]{2,1,0:T(8,128)(2,1)} %param.14, bf16[128,3584]{1,0:T(8,128)(2,1)S(1)} %all_gather.7, bf16[1,3584,512]{2,1,0:T(8,128)(2,1)} %param.13, f32[128,512]{1,0:T(8,128)S(1)} %fusion.4, pred[128]{0:T(512)(128)(4,1)S(1)} %lt.44), kind=kOutput, calls=%fused_computation.2 | convolution fusion | flops 940441600 | bytes 9437312 | tf_op jit(solution)/shard_map/dot_general | solution.py:83
  41.2 0.5 all-gather.2.cloned.1.call-update
  41.8 0.1 fusion.35
  41.9 0.1 copy.29
  42.0 0.1 reshape.67
  42.1 6.7 %reduce-scatter.2.cloned.1.call-done = bf16[64,3584]{1,0:T(8,128)(2,1)} async-done(((bf16[128,3584]{1,0:T(8,128)(2,1)}), bf16[64,3584]{1,0:T(8,128)(2,1)}) %reduce-scatter.2.cloned.1.call-update) | async-done | bytes 458768 | tf_op jit(solution)/shard_map/reduce_scatter | solution.py:85
  48.8 5.7 %all-to-all-start.1 = ((bf16[8,8,3584]{2,1,0:T(8,128)(2,1)}), bf16[8,8,3584]{2,1,0:T(8,128)(2,1)S(1)}, u32[]{:S(2)}, u32[]{:S(2)}) async-start(bf16[8,8,3584]{2,1,0:T(8,128)(2,1)} %bitcast.37), calls=%async_computation.2 | async-start | bytes 917504 | tf_op jit(solution)/shard_map/all_to_all | solution.py:91
  54.5 40.9 %all-gather.2.cloned.1.call-done = bf16[256,3584]{1,0:T(8,128)(2,1)} async-done(((bf16[32,3584]{1,0:T(8,128)(2,1)}), bf16[256,3584]{1,0:T(8,128)(2,1)}) %all-gather.2.cloned.1.call-update) | async-done | bytes 1835024 | tf_op jit(solution)/shard_map/all_gather | solution.py:56
  95.4 2.3 %fusion.40 = (f32[128]{0:T(128)S(1)}, f32[128,256]{1,0:T(8,128)S(1)}, f32[128,256]{1,0:T(8,128)S(1)}) fusion(bf16[128,3584]{1,0:T(8,128)(2,1)S(1)} %copy-done, bf16[256,3584]{1,0:T(8,128)(2,1)} %all-gather.2.cloned.1.call-done), kind=kOutput, calls=%fused_computation.49 | convolution fusion | flops 235011968 | bytes 3015168 | tf_op jit(solution)/shard_map/dot_general | solution.py:54
  97.7 8.6 %gather_fusion = f32[1024]{0:T(1024)S(1)} fusion(f32[128,256]{1,0:T(8,128)S(1)} %get-tuple-element.3, s32[1024]{0:T(1024)S(1)} %reshape.67), kind=kCustom, calls=%fused_computation | custom fusion | bytes 16384 | tf_op jit(solution)/shard_map/jit(take_along_axis)/gather | solution.py:29
  106.5 0.3 fusion.32
  106.8 0.5 convert_multiply_fusion
  107.3 1.3 %convolution_convert_fusion = bf16[128,3584]{1,0:T(8,128)(2,1)} fusion(bf16[128,64]{0,1:T(8,128)(2,1)S(1)} %fusion.25, bf16[8,8,3584]{2,1,0:T(8,128)(2,1)S(1)} %all-to-all-done.1), kind=kOutput, calls=%fused_computation.1 | convolution fusion | flops 59179008 | bytes 1392640 | tf_op jit(solution)/shard_map/dot_general | solution.py:95
  (23 shorter events, 0.6 us)
Async XLA Ops:
  8.0 1.2 %copy-start = (bf16[128,3584]{1,0:T(8,128)(2,1)S(1)}, bf16[128,3584]{1,0:T(8,128)(2,1)}, u32[]{:S(2)}) copy-start(bf16[128,3584]{1,0:T(8,128)(2,1)} %param.10) | copy-start | bytes 2752516
  10.3 20.4 %all-to-all-start = ((bf16[8,8,3584]{2,1,0:T(8,128)(2,1)}), bf16[8,8,3584]{2,1,0:T(8,128)(2,1)S(1)}, u32[]{:S(2)}, u32[]{:S(2)}) async-start(bf16[8,8,3584]{2,1,0:T(8,128)(2,1)} %fusion), calls=%async_computation | async-start | bytes 917504 | tf_op jit(solution)/shard_map/all_to_all | solution.py:72
  17.5 31.2 %reduce-scatter.2.cloned.1.call-start = ((), (), s32[]{:S(2)}) async-start(), calls=%async_computation.4 | async-start | bytes 1376256 | tf_op jit(solution)/shard_map/reduce_scatter | solution.py:85
  35.8 6.0 %copy-start.1 = (f32[128,256]{1,0:T(8,128)S(1)}, f32[128,256]{1,0:T(8,128)}, u32[]{:S(2)}) copy-start(f32[128,256]{1,0:T(8,128)} %param.15) | copy-start | bytes 393220
  35.8 6.1 %copy-start.2 = (s32[128,8]{0,1:T(8,128)S(1)}, s32[128,8]{0,1:T(8,128)}, u32[]{:S(2)}) copy-start(s32[128,8]{0,1:T(8,128)} %param.16) | copy-start | bytes 12292
  41.2 54.2 %all-gather.2.cloned.1.call-start = ((), (), s32[]{:S(2)}) async-start(), calls=%async_computation.3 | async-start | bytes 2064384 | tf_op jit(solution)/shard_map/all_gather | solution.py:56
  48.8 58.6 %all-to-all-start.1 = ((bf16[8,8,3584]{2,1,0:T(8,128)(2,1)}), bf16[8,8,3584]{2,1,0:T(8,128)(2,1)S(1)}, u32[]{:S(2)}, u32[]{:S(2)}) async-start(bf16[8,8,3584]{2,1,0:T(8,128)(2,1)} %bitcast.37), calls=%async_computation.2 | async-start | bytes 917504 | tf_op jit(solution)/shard_map/all_to_all | solution.py:91
  97.7 9.1 %copy-start.3 = (s32[128]{0:T(128)S(1)}, s32[128]{0:T(128)}, u32[]{:S(2)}) copy-start(s32[128]{0:T(128)} %param.19) | copy-start | bytes 1540
Sparse Core Ops, SparseCore 0:
  41.3 7.4 reduce-scatter.1
Sparse Core Ops, SparseCore 1:
  43.8 51.5 all-gather.1
where the time goes:
time: 117 us; the launch traced here: 116 us
  waiting for transfers between devices  58.9 us (50%)
  between operations  15.6 us (13%)
  starting transfers between devices  13.1 us (11%)
  matrix products  12.7 us (11%)
  local copies, waits for them, and re-layouts  10.2 us (9%)
  other arithmetic  3.22 us (3%)
  blocking collectives  2.45 us (2%)
    all_gather x1, waiting for transfers between devices, per_device(): lax.all_gather(router_weight, 'expert', axis=0, tiled=True)  40.9 us
    all_to_all x1, waiting for transfers between devices, per_device(): lax.all_to_all(outgoing, 'expert', split_axis=0, concat_axis=0, tiled=True)  10.8 us
    gather x5, local copies, waits for them, and re-layouts, router_terms(): chosen = jnp.take_along_axis(scores, expert_ids, axis=1)  8.91 us
    all_to_all x1, starting transfers between devices, per_device(): lax.all_to_all(outgoing, 'expert', split_axis=0, concat_axis=0, tiled=True)  7.28 us
    reduce_scatter x1, waiting for transfers between devices, per_device(): lax.psum_scatter(partial_value.astype(jnp.float32).astype(jnp.bfloat16),...  6.68 us
    all_to_all x1, starting transfers between devices, per_device(): lax.all_to_all(summed.reshape(experts, CAP, model_width), 'expert', split...  5.73 us
    dot_general x1, matrix products, per_device(): jnp.dot(rows, w_down, preferred_element_type=jnp.float32)  5.36 us
    dot_general x1, matrix products, per_device(): gate = jnp.dot(rows, w_gate, preferred_element_type=jnp.float32)  2.67 us
  transfers between devices with their start and end apart: 4, of which 3 were waited for; matrix products, arithmetic and copies ran while one was open for 12% of the time, Pallas kernels for 0%

commit v1 on v0

v1 whole, which is shorter than its diff:
```python
import jax
import jax.numpy as jnp
from jax import lax
from jax.sharding import PartitionSpec as P

CAP = 8
SWAP = [(0, 1), (1, 0)]


def swap_cores(value):
    return lax.ppermute(value, "tensor", SWAP)


def across(value, axis, distance):
    size = lax.axis_size(axis)
    return lax.ppermute(value, axis, [(s, s ^ distance) for s in range(size)])


def placed_columns(expert_ids, slots, count):
    valid = (expert_ids < count) & (slots < CAP)
    return jnp.where(valid, expert_ids * CAP + slots, -1)


def select_matrix(place, width):
    columns = jnp.arange(width, dtype=jnp.int32)
    hits = place[:, :, None] == columns[None, None, :]
    return jnp.any(hits, axis=1).astype(jnp.bfloat16)


def weighted_matrix(place, weights, width):
    columns = jnp.arange(width, dtype=jnp.int32)
    hits = place[:, :, None] == columns[None, None, :]
    picked = jnp.where(hits, weights[:, :, None], jnp.zeros((), jnp.bfloat16))
    return jnp.sum(picked, axis=1)


def router_terms(logits, policy_logits, expert_ids, env_mask):
    scores = jax.nn.sigmoid(logits)
    columns = jnp.arange(logits.shape[1], dtype=jnp.int32)
    chosen = jnp.stack(
        [
            jnp.sum(jnp.where(expert_ids[:, k : k + 1] == columns[None, :], scores, 0.0), axis=1)
            for k in range(expert_ids.shape[1])
        ],
        axis=1,
    )
    combine_weights = (2.5 * chosen / jnp.sum(chosen, axis=1, keepdims=True)).astype(jnp.bfloat16)
    log_p = jax.nn.log_sigmoid(logits) - jnp.log(jnp.sum(scores, axis=1, keepdims=True))
    policy = jax.nn.sigmoid(policy_logits)
    log_q = jax.nn.log_sigmoid(policy_logits) - jnp.log(jnp.sum(policy, axis=1, keepdims=True))
    keep = (1 - env_mask).astype(jnp.float32)
    kl_terms = keep * jnp.sum(jnp.exp(log_q) * (log_q - log_p), axis=1)
    return (combine_weights, kl_terms)


def dot_rows(left, right):
    return lax.dot_general(
        left, right, (((1,), (1,)), ((), ())), preferred_element_type=jnp.float32
    )


def z_pieces(piece):
    z = lax.axis_index("expert") // 2
    got = [piece] + [across(piece, "expert", 2 * d) for d in (1, 2, 3)]
    out = jnp.zeros((4,) + piece.shape, piece.dtype)
    for d in range(4):
        out = lax.dynamic_update_index_in_dim(out, got[d], z ^ d, 0)
    return out


def per_device(
    tokens,
    router_weight,
    gate_weight,
    up_weight,
    down_weight,
    policy_logits,
    expert_ids,
    slots,
    occupancy,
    env_mask,
):
    experts = lax.axis_size("expert")
    groups = lax.axis_size("groups")
    pairs = lax.axis_size("tensor")
    core = lax.axis_index("tensor")
    model_width = tokens.shape[1]
    width = experts * CAP
    staged = experts == 8 and groups == 2 and pairs == 2
    half = model_width // 2
    if staged:
        group = lax.axis_index("groups")
        quarter = half // 2
        piece = lax.dynamic_slice_in_dim(router_weight, core * half + group * quarter, quarter, axis=1)
        level_z = z_pieces(piece)
        peer_tokens = swap_cores(lax.dynamic_slice_in_dim(tokens, (1 - core) * half, half, axis=1))
    place = placed_columns(expert_ids, slots, experts)
    matrix = select_matrix(place, width)
    outgoing = lax.dot_general(
        matrix, tokens, (((0,), (0,)), ((), ())), preferred_element_type=jnp.float32
    )
    outgoing = outgoing.astype(jnp.bfloat16).reshape(experts, CAP, model_width)
    arrived = lax.all_to_all(outgoing, "expert", split_axis=0, concat_axis=0, tiled=True)
    arrived = arrived.reshape(-1, model_width)
    if staged:
        level_y = across(level_z, "expert", 1)
        level_x = across(level_z, "groups", 1)
        level_xy = across(level_y, "groups", 1)

    used = occupancy[0].reshape(experts, pairs)
    used = jnp.stack(
        [jnp.take(used, core, axis=1), jnp.take(used, 1 - core, axis=1)], axis=0
    ).reshape(-1)
    alive = (jnp.arange(CAP, dtype=jnp.int32)[None, :] < used[:, None]).reshape(-1)
    rows = jnp.concatenate([arrived, swap_cores(arrived)], axis=0)
    gate = jnp.dot(rows, gate_weight[0], preferred_element_type=jnp.float32)
    up = jnp.dot(rows, up_weight[0], preferred_element_type=jnp.float32)
    hidden = jnp.where(alive[:, None], jax.nn.silu(gate) * up, jnp.zeros((), jnp.float32)).astype(
        jnp.bfloat16
    )
    partial_value = jnp.dot(hidden, down_weight[0], preferred_element_type=jnp.float32).astype(
        jnp.bfloat16
    )
    other = swap_cores(partial_value[width:])
    summed = (partial_value[:width].astype(jnp.float32) + other.astype(jnp.float32)).astype(jnp.bfloat16)
    returned = lax.all_to_all(
        summed.reshape(experts, CAP, model_width), "expert", split_axis=0, concat_axis=0, tiled=True
    )
    if staged:
        y = lax.axis_index("expert") % 2

        def in_order(own, other):
            return jnp.where(
                y == 0, jnp.stack([own, other], axis=1), jnp.stack([other, own], axis=1)
            ).reshape(-1, quarter)

        mine = in_order(level_z, level_y)
        theirs = in_order(level_x, level_xy)
        at_mine = group * quarter
        at_theirs = (1 - group) * quarter
        own_tokens = lax.dynamic_slice_in_dim(tokens, core * half, half, axis=1)

        def half_logits(value):
            first = lax.dynamic_slice_in_dim(value, at_mine, quarter, axis=1)
            second = lax.dynamic_slice_in_dim(value, at_theirs, quarter, axis=1)
            return dot_rows(first, mine) + dot_rows(second, theirs)

        logits = half_logits(own_tokens) + swap_cores(half_logits(peer_tokens))
    else:
        logits = dot_rows(tokens, lax.all_gather(router_weight, "expert", axis=0, tiled=True))
    combine_weights, kl_terms = router_terms(logits, policy_logits, expert_ids, env_mask)
    combine_matrix = weighted_matrix(place, combine_weights, width)
    mixed = jnp.dot(
        combine_matrix, returned.reshape(width, model_width), preferred_element_type=jnp.float32
    ).astype(jnp.bfloat16)
    return (mixed, kl_terms)


def solution(mesh):
    in_specs = (
        P(("groups", "expert", "tensor"), None),
        P("expert", None),
        P("expert", None, "tensor"),
        P("expert", None, "tensor"),
        P("expert", "tensor", None),
        P(("groups", "expert", "tensor"), None),
        P(("groups", "expert", "tensor"), None),
        P(("groups", "expert", "tensor"), None),
        P("expert", "groups"),
        P(("groups", "expert", "tensor")),
    )
    out_specs = (P(("groups", "expert", "tensor"), None), P(("groups", "expert", "tensor")))
    return jax.shard_map(
        per_device, mesh=mesh, in_specs=in_specs, out_specs=out_specs, check_vma=False
    )
```

time: 117 us -> 69.8 us (0.60)
  waiting for transfers between devices: 58.9 us -> 26.9 us
  between operations: 15.6 us -> 0.95 us
  starting transfers between devices: 13.1 us -> 21.9 us
  local copies, waits for them, and re-layouts: 10.2 us -> 1.96 us
  blocking collectives: 2.45 us -> 0 us
  other arithmetic: 3.22 us -> 4.75 us
    all_gather x1 -> x0, waiting for transfers between devices: 40.9 us -> none  [per_device(): lax.all_gather(router_weight, 'expert', axis=0, tiled=True)]
    ppermute x0 -> x10, waiting for transfers between devices: none -> 14.2 us  [the longest x6 13.4 us: across(): return lax.ppermute(value, axis, [(s, s ^ distance) for s in range(size)])]
    all_to_all x1, waiting for transfers between devices: 0.01 us -> 12.7 us  [per_device(): lax.all_to_all(summed.reshape(experts, CAP, model_width), 'expert', split...]
    ppermute x0 -> x10, starting transfers between devices: none -> 11.7 us  [the longest x6 10.8 us: across(): return lax.ppermute(value, axis, [(s, s ^ distance) for s in range(size)])]
    all_to_all x1, waiting for transfers between devices: 10.8 us -> 0.01 us  [per_device(): lax.all_to_all(outgoing, 'expert', split_axis=0, concat_axis=0, tiled=True)]
    gather x5 -> x0, local copies, waits for them, and re-layouts: 8.91 us -> none  [router_terms(): chosen = jnp.take_along_axis(scores, expert_ids, axis=1)]
    reduce_scatter x1 -> x0, waiting for transfers between devices: 6.68 us -> none  [per_device(): lax.psum_scatter(partial_value.astype(jnp.float32).astype(jnp.bfloat16),...]
    all_gather x1 -> x0, blocking collectives: 2.45 us -> none  [per_device(): lax.all_gather(arrived.reshape(-1, model_width), 'tensor', axis=0, tiled=...]
  transfers between devices with their start and end apart: 4 -> 12, of which waited for: 3 -> 4; matrix products, arithmetic and copies ran while one was open for 12% -> 24% of each run, Pallas kernels for 0% -> 0%
where the time goes in v1:
time: 69.8 us; the launch traced here: 69.4 us
  waiting for transfers between devices  26.9 us (39%)
  starting transfers between devices  21.9 us (31%)
  matrix products  13 us (19%)
  other arithmetic  4.75 us (7%)
  local copies, waits for them, and re-layouts  1.96 us (3%)
  between operations  0.95 us (1%)
    ppermute x6, waiting for transfers between devices, across(): return lax.ppermute(value, axis, [(s, s ^ distance) for s in range(size)])  13.4 us
    all_to_all x1, waiting for transfers between devices, per_device(): lax.all_to_all(summed.reshape(experts, CAP, model_width), 'expert', split...  12.7 us
    ppermute x6, starting transfers between devices, across(): return lax.ppermute(value, axis, [(s, s ^ distance) for s in range(size)])  10.8 us
    all_to_all x1, starting transfers between devices, per_device(): lax.all_to_all(outgoing, 'expert', split_axis=0, concat_axis=0, tiled=True)  6.05 us
    dot_general x1, matrix products, per_device(): jnp.dot(hidden, down_weight[0], preferred_element_type=jnp.float32)  4.67 us
    all_to_all x1, starting transfers between devices, per_device(): lax.all_to_all(summed.reshape(experts, CAP, model_width), 'expert', split...  4.16 us
    dot_general x1, matrix products, per_device(): up = jnp.dot(rows, up_weight[0], preferred_element_type=jnp.float32)  3.54 us
    dot_general x4, matrix products, dot_rows(): lax.dot_general(left, right, (((1,), (1,)), ((), ())), preferred_element_...  2.38 us
  transfers between devices with their start and end apart: 12, of which 4 were waited for; matrix products, arithmetic and copies ran while one was open for 24% of the time, Pallas kernels for 0%

profile of v1, /device:TPU:0, one launch (start us, length us, event | category | flops | bytes accessed | tf_op | source)
XLA Modules:
  0.0 69.4 jit_solution(3431257088571218836)
XLA Ops:
  0.7 0.9 %bitcast_dynamic-update-slice_fusion.3 = (bf16[4,32,896]{2,1,0:T(8,128)(2,1)S(1)}, bf16[32,896]{1,0:T(8,128)(2,1)S(1)}) fusion(bf16[4,32,896]{2,1,0:T(8,128)(2,1)S(1)} %broadcast_in_dim.79, s32[]{:T(128)S(6)} %select_n.127, bf16[32,3584]{1,0:T(8,128)(2,1)} %param.13, s32[]{:T(128)S(6)} %select_n.125), kind=kLoop, calls=%fused_computation.64 | loop fusion | bytes 172040 | tf_op jit(solution)/shard_map/jit(dynamic_update_index_in_dim)/dynamic_update_slice | solution.py:67
  1.6 3.1 %collective-permute-start = (bf16[32,896]{1,0:T(8,128)(2,1)S(1)}, bf16[32,896]{1,0:T(8,128)(2,1)S(1)}, u32[]{:S(2)}, u32[]{:S(2)}) collective-permute-start(bf16[32,896]{1,0:T(8,128)(2,1)S(1)} %get-tuple-element.26), channel_id=1, source_target_pairs={{0,4},{2,6},{4,0},{6,2},{8,12},{10,14},{12,8},{14,10},{1,5},{3,7},... | collective-permute-start | bytes 172040 | tf_op jit(solution)/shard_map/ppermute | solution.py:16
  4.7 2.6 %collective-permute-start.1 = (bf16[32,896]{1,0:T(8,128)(2,1)S(1)}, bf16[32,896]{1,0:T(8,128)(2,1)S(1)}, u32[]{:S(2)}, u32[]{:S(2)}) collective-permute-start(bf16[32,896]{1,0:T(8,128)(2,1)S(1)} %get-tuple-element.26), channel_id=1, source_target_pairs={{0,8},{2,10},{4,12},{6,14},{8,0},{10,2},{12,4},{14,6},{1,9},{3,11}... | collective-permute-start | bytes 172040 | tf_op jit(solution)/shard_map/ppermute | solution.py:16
  7.4 0.7 %add_select_fusion = s32[128,8]{0,1:T(8,128)S(1)} fusion(s32[128,8]{0,1:T(8,128)} %param.19, s32[128,8]{0,1:T(8,128)} %param.18), kind=kLoop, calls=%fused_computation.69 | loop fusion | flops 6144 | bytes 12288 | tf_op jit(solution)/shard_map/jit(_where)/select_n | solution.py:21
  8.2 1.1 %fusion = bf16[8,8,3584]{2,1,0:T(8,128)(2,1)} fusion(pred[128,64]{0,1:T(8,128)(4,1)S(1)} %fusion.8, bf16[128,3584]{1,0:T(8,128)(2,1)S(1)} %copy-done), kind=kOutput, calls=%fused_computation.3 | convolution fusion | flops 58949632 | bytes 1384448 | tf_op jit(solution)/shard_map/dot_general | solution.py:99
  9.2 6.1 %all-to-all-start = ((bf16[8,8,3584]{2,1,0:T(8,128)(2,1)}), bf16[8,8,3584]{2,1,0:T(8,128)(2,1)S(1)}, u32[]{:S(2)}, u32[]{:S(2)}) async-start(bf16[8,8,3584]{2,1,0:T(8,128)(2,1)} %fusion), calls=%async_computation | async-start | bytes 917504 | tf_op jit(solution)/shard_map/all_to_all | solution.py:103
  15.3 0.5 broadcast.88
  15.9 0.7 reduce.16
  16.9 2.1 %collective-permute-start.3 = (bf16[4,32,896]{2,1,0:T(8,128)(2,1)S(1)}, bf16[4,32,896]{2,1,0:T(8,128)(2,1)S(1)}, u32[]{:S(2)}, u32[]{:S(2)}) collective-permute-start(bf16[4,32,896]{2,1,0:T(8,128)(2,1)S(1)} %bitcast_dynamic-update-slice_fusion), channel_id=1, source_target_pairs={{0,2},{2,0},{4,6},{6,4},{8,10},{10,8},{12,14},{14,12},{1,3},{3,1},... | collective-permute-start | bytes 688136 | tf_op jit(solution)/shard_map/ppermute | solution.py:16
  19.2 1.5 %collective-permute-start.4 = (bf16[4,32,896]{2,1,0:T(8,128)(2,1)S(1)}, bf16[4,32,896]{2,1,0:T(8,128)(2,1)S(1)}, u32[]{:S(2)}, u32[]{:S(2)}) collective-permute-start(bf16[4,32,896]{2,1,0:T(8,128)(2,1)S(1)} %bitcast_dynamic-update-slice_fusion), channel_id=1, source_target_pairs={{0,16},{16,0},{1,17},{17,1},{2,18},{18,2},{3,19},{19,3},{4,20},{20... | collective-permute-start | bytes 688136 | tf_op jit(solution)/shard_map/ppermute | solution.py:16
  20.7 7.7 %collective-permute-done.3 = bf16[4,32,896]{2,1,0:T(8,128)(2,1)S(1)} collective-permute-done((bf16[4,32,896]{2,1,0:T(8,128)(2,1)S(1)}, bf16[4,32,896]{2,1,0:T(8,128)(2,1)S(1)}, u32[]{:S(2)}, u32[]{:S(2)}) %collective-permute-start.3) | collective-permute-done | bytes 229408 | tf_op jit(solution)/shard_map/ppermute | solution.py:16
  28.4 1.5 %collective-permute-start.5 = (bf16[4,32,896]{2,1,0:T(8,128)(2,1)S(1)}, bf16[4,32,896]{2,1,0:T(8,128)(2,1)}, u32[]{:S(2)}, u32[]{:S(2)}) collective-permute-start(bf16[4,32,896]{2,1,0:T(8,128)(2,1)S(1)} %collective-permute-done.3), channel_id=1, source_target_pairs={{0,16},{16,0},{1,17},{17,1},{2,18},{18,2},{3,19},{19,3},{4,20},{20... | collective-permute-start | bytes 688136 | tf_op jit(solution)/shard_map/ppermute | solution.py:16
  30.2 5.7 %collective-permute-done.5 = bf16[4,32,896]{2,1,0:T(8,128)(2,1)} collective-permute-done((bf16[4,32,896]{2,1,0:T(8,128)(2,1)S(1)}, bf16[4,32,896]{2,1,0:T(8,128)(2,1)}, u32[]{:S(2)}, u32[]{:S(2)}) %collective-permute-start.5) | collective-permute-done | bytes 229408 | tf_op jit(solution)/shard_map/ppermute | solution.py:16
  35.9 1.1 %maximum_select_fusion.1 = bf16[4,2,32,896]{3,2,0,1:T(8,128)(2,1)S(1)} fusion(bf16[4,1,32,896]{3,2,0,1:T(8,128)(2,1)} %bitcast.9, bf16[4,1,32,896]{3,2,0,1:T(8,128)(2,1)S(1)} %bitcast.77, pred[]{:T(512)S(6)} %eq.153), kind=kLoop, calls=%fused_computation.15 | loop fusion | flops 688128 | bytes 917505 | tf_op jit(solution)/shard_map/jit(_where)/select_n | solution.py:133
  37.8 0.5 collective-permute-start.7
  38.4 0.8 %collective-permute-done.8 = bf16[64,3584]{1,0:T(8,128)(2,1)} collective-permute-done((bf16[64,3584]{1,0:T(8,128)(2,1)S(1)}, bf16[64,3584]{1,0:T(8,128)(2,1)}, u32[]{:S(2)}, u32[]{:S(2)}) %collective-permute-start.8) | collective-permute-done | bytes 458784 | tf_op jit(solution)/shard_map/ppermute | solution.py:11
  39.1 3.5 %fusion.2 = f32[128,512]{1,0:T(8,128)} fusion(bf16[1,3584,512]{2,1,0:T(8,128)(2,1)} %param.15, bf16[64,3584]{1,0:T(8,128)(2,1)} %collective-permute-done.8, bf16[64,3584]{1,0:T(8,128)(2,1)S(1)} %bitcast.74), kind=kOutput, calls=%fused_computation.5 | convolution fusion | flops 471597056 | bytes 4849664 | tf_op jit(solution)/shard_map/dot_general | solution.py:117
  42.7 4.7 %convolution_convert_fusion.1 = bf16[128,3584]{1,0:T(8,128)(2,1)S(1)} fusion(bf16[1,512,3584]{2,1,0:T(8,128)(2,1)} %param.16, f32[128,512]{1,0:T(8,128)} %fusion.2, bf16[1,3584,512]{2,1,0:T(8,128)(2,1)} %param.14, bf16[64,3584]{1,0:T(8,128)(2,1)} %collective-permute-done.8, bf16[64,3584]{1,0:T(8,128)(2,1)S(1)} %bitcast.75, pred[128]{0:T(512)(128)(4,1)S(1)} %lt.83), kind=kOutput, calls=%fused_computation.1 | convolution fusion | flops 942276608 | bytes 9437312 | tf_op jit(solution)/shard_map/dot_general | solution.py:121
  47.9 1.5 %fusion.47 = (f32[128]{0:T(128)S(1)}, f32[128]{0:T(128)S(1)}, f32[128]{0:T(128)S(1)}, f32[128]{0:T(128)S(1)}, f32[128]{0:T(128)S(1)}, /*index=5*/f32[128]{0:T(12...) fusion(s32[128]{0:T(128)S(1)} %get-tuple-element.33, s32[128]{0:T(128)S(1)} %get-tuple-element.34, ...), kind=kOutput, calls=%fused_computation.91 | convolution fusion | flops 59702144 | bytes 1090052 | tf_op jit(solution)/shard_map/dot_general | solution.py:57
  49.4 0.9 %fusion.6 = bf16[8,8,3584]{2,1,0:T(8,128)(2,1)} fusion(bf16[64,3584]{1,0:T(8,128)(2,1)S(1)} %collective-permute-done.9, bf16[128,3584]{1,0:T(8,128)(2,1)S(1)} %convolution_convert_fusion.1), kind=kLoop, calls=%fused_computation.13 | loop fusion | flops 917504 | bytes 1376256 | tf_op jit(solution)/shard_map/reshape | solution.py:127
  50.3 4.2 %all-to-all-start.1 = ((bf16[8,8,3584]{2,1,0:T(8,128)(2,1)}), bf16[8,8,3584]{2,1,0:T(8,128)(2,1)S(1)}, u32[]{:S(2)}, u32[]{:S(2)}) async-start(bf16[8,8,3584]{2,1,0:T(8,128)(2,1)} %fusion.6), calls=%async_computation.1 | async-start | bytes 917504 | tf_op jit(solution)/shard_map/all_to_all | solution.py:126
  54.9 0.5 convert_multiply_fusion
  55.4 12.7 %all-to-all-done.1 = bf16[8,8,3584]{2,1,0:T(8,128)(2,1)S(1)} async-done(((bf16[8,8,3584]{2,1,0:T(8,128)(2,1)}), bf16[8,8,3584]{2,1,0:T(8,128)(2,1)S(1)}, u32[]{:S(2)}, u32[]{:S(2)}) %all-to-all-start.1) | async-done | bytes 458784 | tf_op jit(solution)/shard_map/all_to_all | solution.py:126
  68.1 1.3 %convolution_convert_fusion = bf16[128,3584]{1,0:T(8,128)(2,1)} fusion(bf16[128,64]{0,1:T(8,128)(2,1)S(1)} %fusion.22, bf16[8,8,3584]{2,1,0:T(8,128)(2,1)S(1)} %all-to-all-done.1), kind=kOutput, calls=%fused_computation | convolution fusion | flops 59179008 | bytes 1392640 | tf_op jit(solution)/shard_map/dot_general | solution.py:153
  (51 shorter events, 2.6 us)
Async XLA Ops:
  0.6 6.7 %copy-start = (bf16[128,3584]{1,0:T(8,128)(2,1)S(1)}, bf16[128,3584]{1,0:T(8,128)(2,1)}, u32[]{:S(2)}) copy-start(bf16[128,3584]{1,0:T(8,128)(2,1)} %param.12) | copy-start | bytes 2752516
  0.6 14.7 %copy-start.3 = (s32[128,8]{0,1:T(8,128)S(1)}, s32[128,8]{0,1:T(8,128)}, u32[]{:S(2)}) copy-start(s32[128,8]{0,1:T(8,128)} %param.18) | copy-start | bytes 12292
  0.7 15.2 %copy-start.4 = (s32[1,16]{1,0:T(1,128)S(1)}, s32[1,16]{1,0:T(1,128)}, u32[]{:S(2)}) copy-start(s32[1,16]{1,0:T(1,128)} %param.20) | copy-start | bytes 196
  0.7 29.2 %copy-start.1 = (f32[128,256]{1,0:T(8,128)S(1)}, f32[128,256]{1,0:T(8,128)}, u32[]{:S(2)}) copy-start(f32[128,256]{1,0:T(8,128)} %param.17) | copy-start | bytes 393220
  1.6 15.2 %collective-permute-start = (bf16[32,896]{1,0:T(8,128)(2,1)S(1)}, bf16[32,896]{1,0:T(8,128)(2,1)S(1)}, u32[]{:S(2)}, u32[]{:S(2)}) collective-permute-start(bf16[32,896]{1,0:T(8,128)(2,1)S(1)} %get-tuple-element.26), channel_id=1, source_target_pairs={{0,4},{2,6},{4,0},{6,2},{8,12},{10,14},{12,8},{14,10},{1,5},{3,7},... | collective-permute-start | bytes 172040 | tf_op jit(solution)/shard_map/ppermute | solution.py:16
  4.7 12.1 %collective-permute-start.1 = (bf16[32,896]{1,0:T(8,128)(2,1)S(1)}, bf16[32,896]{1,0:T(8,128)(2,1)S(1)}, u32[]{:S(2)}, u32[]{:S(2)}) collective-permute-start(bf16[32,896]{1,0:T(8,128)(2,1)S(1)} %get-tuple-element.26), channel_id=1, source_target_pairs={{0,8},{2,10},{4,12},{6,14},{8,0},{10,2},{12,4},{14,6},{1,9},{3,11}... | collective-permute-start | bytes 172040 | tf_op jit(solution)/shard_map/ppermute | solution.py:16
  7.3 9.6 %collective-permute-start.2 = (bf16[32,896]{1,0:T(8,128)(2,1)S(1)}, bf16[32,896]{1,0:T(8,128)(2,1)S(1)}, u32[]{:S(2)}, u32[]{:S(2)}) collective-permute-start(bf16[32,896]{1,0:T(8,128)(2,1)S(1)} %get-tuple-element.26), channel_id=1, source_target_pairs={{0,12},{2,14},{4,8},{6,10},{8,4},{10,6},{12,0},{14,2},{1,13},{3,15... | collective-permute-start | bytes 172040 | tf_op jit(solution)/shard_map/ppermute | solution.py:16
  7.4 29.8 %collective-permute-start.6 = (bf16[128,1792]{1,0:T(8,128)(2,1)S(1)}, bf16[128,1792]{1,0:T(8,128)(2,1)S(1)}, u32[]{:S(2)}, u32[]{:S(2)}) collective-permute-start(bf16[128,1792]{1,0:T(8,128)(2,1)S(1)} %constant_dynamic-slice_fusion), channel_id=1, source_target_pairs={{0,1},{1,0},{2,3},{3,2},{4,5},{5,4},{6,7},{7,6},{8,9},{9,8},{10,11... | collective-permute-start | bytes 1376264 | tf_op jit(solution)/shard_map/ppermute | solution.py:11
  9.2 27.9 %all-to-all-start = ((bf16[8,8,3584]{2,1,0:T(8,128)(2,1)}), bf16[8,8,3584]{2,1,0:T(8,128)(2,1)S(1)}, u32[]{:S(2)}, u32[]{:S(2)}) async-start(bf16[8,8,3584]{2,1,0:T(8,128)(2,1)} %fusion), calls=%async_computation | async-start | bytes 917504 | tf_op jit(solution)/shard_map/all_to_all | solution.py:103
  16.9 11.5 %collective-permute-start.3 = (bf16[4,32,896]{2,1,0:T(8,128)(2,1)S(1)}, bf16[4,32,896]{2,1,0:T(8,128)(2,1)S(1)}, u32[]{:S(2)}, u32[]{:S(2)}) collective-permute-start(bf16[4,32,896]{2,1,0:T(8,128)(2,1)S(1)} %bitcast_dynamic-update-slice_fusion), channel_id=1, source_target_pairs={{0,2},{2,0},{4,6},{6,4},{8,10},{10,8},{12,14},{14,12},{1,3},{3,1},... | collective-permute-start | bytes 688136 | tf_op jit(solution)/shard_map/ppermute | solution.py:16
  19.2 11.0 %collective-permute-start.4 = (bf16[4,32,896]{2,1,0:T(8,128)(2,1)S(1)}, bf16[4,32,896]{2,1,0:T(8,128)(2,1)S(1)}, u32[]{:S(2)}, u32[]{:S(2)}) collective-permute-start(bf16[4,32,896]{2,1,0:T(8,128)(2,1)S(1)} %bitcast_dynamic-update-slice_fusion), channel_id=1, source_target_pairs={{0,16},{16,0},{1,17},{17,1},{2,18},{18,2},{3,19},{19,3},{4,20},{20... | collective-permute-start | bytes 688136 | tf_op jit(solution)/shard_map/ppermute | solution.py:16
  28.4 7.5 %collective-permute-start.5 = (bf16[4,32,896]{2,1,0:T(8,128)(2,1)S(1)}, bf16[4,32,896]{2,1,0:T(8,128)(2,1)}, u32[]{:S(2)}, u32[]{:S(2)}) collective-permute-start(bf16[4,32,896]{2,1,0:T(8,128)(2,1)S(1)} %collective-permute-done.3), channel_id=1, source_target_pairs={{0,16},{16,0},{1,17},{17,1},{2,18},{18,2},{3,19},{19,3},{4,20},{20... | collective-permute-start | bytes 688136 | tf_op jit(solution)/shard_map/ppermute | solution.py:16
  37.1 2.0 %collective-permute-start.8 = (bf16[64,3584]{1,0:T(8,128)(2,1)S(1)}, bf16[64,3584]{1,0:T(8,128)(2,1)}, u32[]{:S(2)}, u32[]{:S(2)}) collective-permute-start(bf16[64,3584]{1,0:T(8,128)(2,1)S(1)} %bitcast.73), channel_id=1, source_target_pairs={{0,1},{1,0},{2,3},{3,2},{4,5},{5,4},{6,7},{7,6},{8,9},{9,8},{10,11... | collective-permute-start | bytes 1376264 | tf_op jit(solution)/shard_map/ppermute | solution.py:11
  37.8 10.1 %collective-permute-start.7 = (f32[128,256]{1,0:T(8,128)S(1)}, f32[128,256]{1,0:T(8,128)}, u32[]{:S(2)}, u32[]{:S(2)}) collective-permute-start(f32[128,256]{1,0:T(8,128)S(1)} %convolution_add_fusion), channel_id=1, source_target_pairs={{0,1},{1,0},{2,3},{3,2},{4,5},{5,4},{6,7},{7,6},{8,9},{9,8},{10,11... | collective-permute-start | bytes 393224 | tf_op jit(solution)/shard_map/ppermute | solution.py:11
  47.3 7.2 %copy-start.2 = (f32[128,256]{1,0:T(8,128)S(1)}, f32[128,256]{1,0:T(8,128)}, u32[]{:S(2)}) copy-start(f32[128,256]{1,0:T(8,128)} %param.17) | copy-start | bytes 393220
  47.4 7.5 %copy-start.5 = (s32[128]{0:T(128)S(1)}, s32[128]{0:T(128)}, u32[]{:S(2)}) copy-start(s32[128]{0:T(128)} %param.21) | copy-start | bytes 1540
  47.4 2.0 %collective-permute-start.9 = (bf16[64,3584]{1,0:T(8,128)(2,1)S(1)}, bf16[64,3584]{1,0:T(8,128)(2,1)S(1)}, u32[]{:S(2)}, u32[]{:S(2)}) collective-permute-start(bf16[64,3584]{1,0:T(8,128)(2,1)S(1)} %slice.48), channel_id=1, source_target_pairs={{0,1},{1,0},{2,3},{3,2},{4,5},{5,4},{6,7},{7,6},{8,9},{9,8},{10,11... | collective-permute-start | bytes 1376264 | tf_op jit(solution)/shard_map/ppermute | solution.py:11
  50.3 17.8 %all-to-all-start.1 = ((bf16[8,8,3584]{2,1,0:T(8,128)(2,1)}), bf16[8,8,3584]{2,1,0:T(8,128)(2,1)S(1)}, u32[]{:S(2)}, u32[]{:S(2)}) async-start(bf16[8,8,3584]{2,1,0:T(8,128)(2,1)} %fusion.6), calls=%async_computation.1 | async-start | bytes 917504 | tf_op jit(solution)/shard_map/all_to_all | solution.py:126

commit v2 on v0

v2 whole, which is shorter than its diff:
```python
import functools

import jax
import jax.numpy as jnp
from jax import lax
from jax.experimental import pallas as pl
from jax.experimental.pallas import tpu as pltpu
from jax.sharding import PartitionSpec as P

CAP = 8
SWAP = [(0, 1), (1, 0)]
WHOLE = pl.BlockSpec(memory_space=pltpu.VMEM)
LEFT = pl.BlockSpec(memory_space=pltpu.HBM)


def swap_cores(value):
    return lax.ppermute(value, "tensor", SWAP)


def across(value, axis, distance):
    size = lax.axis_size(axis)
    return lax.ppermute(value, axis, [(s, s ^ distance) for s in range(size)])


def dot_rows(left, right):
    return lax.dot_general(
        left, right, (((1,), (1,)), ((), ())), preferred_element_type=jnp.float32
    )


def dot_columns(left, right):
    return lax.dot_general(
        left, right, (((0,), (0,)), ((), ())), preferred_element_type=jnp.float32
    )


def params(mib):
    return pltpu.CompilerParams(vmem_limit_bytes=mib << 20)


def cost(flops, nbytes):
    return pl.CostEstimate(flops=flops, bytes_accessed=nbytes, transcendentals=0)


def buffer_hits(ids, slots, width):
    choices, tokens = ids.shape
    valid = (ids < width // CAP) & (slots < CAP)
    place = jnp.where(valid, ids * CAP + slots, -1)
    rows = lax.broadcasted_iota(jnp.int32, (width, tokens), 0)
    hits = rows == place[0:1, :]
    for k in range(1, choices):
        hits = hits | (rows == place[k : k + 1, :])
    return hits


def masked_hidden(g, u, occupancy, side):
    count = g.shape[0]
    sources = occupancy.shape[1]
    row = lax.broadcasted_iota(jnp.int32, (count, sources), 0)
    column = lax.broadcasted_iota(jnp.int32, (count, sources), 1)
    here = column == row // CAP * 2 + side
    used = jnp.sum(jnp.where(here, occupancy[...], 0), axis=1, keepdims=True)
    live = row[:, 0:1] % CAP < used
    return jnp.where(live, g / (1.0 + jnp.exp(-g)) * u, 0.0).astype(jnp.bfloat16)


def near_kernel(parts, own, occupancy, gate, up, down, w_gate, w_up, w_down, hidden, sems):
    depth = own.shape[1] // parts
    copies = []
    for part in range(parts):
        at = pl.ds(part * depth, depth)
        copies.append(pltpu.make_async_copy(gate.at[:, at, :], w_gate.at[:, at, :], sems.at[0, part]))
        copies.append(pltpu.make_async_copy(up.at[:, at, :], w_up.at[:, at, :], sems.at[1, part]))
    last = pltpu.make_async_copy(down, w_down, sems.at[2, 0])
    for copy in copies + [last]:
        copy.start()
    g = u = 0.0
    for part in range(parts):
        at = slice(part * depth, (part + 1) * depth)
        rows = own[:, at]
        copies[2 * part].wait()
        g = g + jnp.dot(rows, w_gate[0, at, :], preferred_element_type=jnp.float32)
        copies[2 * part + 1].wait()
        u = u + jnp.dot(rows, w_up[0, at, :], preferred_element_type=jnp.float32)
    hidden[...] = masked_hidden(g, u, occupancy, lax.axis_index("tensor"))
    last.wait()


def ffn_near(own, occupancy, gate, up, down):
    count, model_width = own.shape
    hidden_width = gate.shape[2]
    parts = 4 if model_width % 512 == 0 else 1
    weights = [pltpu.with_memory_space_constraint(w, pltpu.HBM) for w in (gate, up, down)]
    return pl.pallas_call(
        functools.partial(near_kernel, parts),
        out_shape=tuple(jax.ShapeDtypeStruct(w.shape, w.dtype) for w in (gate, up, down))
        + (jax.ShapeDtypeStruct((count, hidden_width), own.dtype),),
        in_specs=[WHOLE, WHOLE, LEFT, LEFT, LEFT],
        out_specs=(WHOLE,) * 4,
        scratch_shapes=[pltpu.SemaphoreType.DMA((3, parts))],
        compiler_params=params(16),
        cost_estimate=cost(4 * count * model_width * hidden_width, 2 * count * model_width),
        name="ffn_near",
    )(own, occupancy, *weights)


def far_kernel(parts, peer, occupancy, own_hidden, gate, up, down, out_own, out_peer):
    count = peer.shape[0]
    wide = down.shape[2] // parts
    g = jnp.dot(peer[...], gate[0], preferred_element_type=jnp.float32)
    u = jnp.dot(peer[...], up[0], preferred_element_type=jnp.float32)
    far = masked_hidden(g, u, occupancy, 1 - lax.axis_index("tensor"))
    hidden = jnp.concatenate([own_hidden[...], far], axis=0)
    for part in range(parts):
        at = slice(part * wide, (part + 1) * wide)
        value = jnp.dot(hidden, down[0, :, at], preferred_element_type=jnp.float32)
        value = value.astype(jnp.bfloat16)
        out_own[:, at] = value[:count]
        out_peer[:, at] = value[count:]


def ffn_far(peer, occupancy, own_hidden, gate, up, down):
    half = jax.ShapeDtypeStruct(peer.shape, peer.dtype)
    count, model_width = peer.shape
    hidden_width = gate.shape[2]
    parts = 4 if model_width % 512 == 0 else 1
    return pl.pallas_call(
        functools.partial(far_kernel, parts),
        out_shape=(half, half),
        in_specs=[WHOLE] * 6,
        out_specs=(WHOLE, WHOLE),
        compiler_params=params(16),
        cost_estimate=cost(8 * count * model_width * hidden_width, 2 * count * model_width),
        name="ffn_far",
    )(peer, occupancy, own_hidden, gate, up, down)


def add_kernel(ours, other, out):
    out[...] = (ours[...].astype(jnp.float32) + other[...].astype(jnp.float32)).astype(out.dtype)


def add_halves(ours, other):
    return pl.pallas_call(
        add_kernel,
        out_shape=jax.ShapeDtypeStruct(ours.shape, ours.dtype),
        in_specs=[WHOLE] * 2,
        out_specs=WHOLE,
        compiler_params=params(16),
        cost_estimate=cost(ours.size, 6 * ours.size),
        name="add_halves",
    )(ours, other)


def logits_kernel(place, own_tokens, peer_tokens, level, level_y, level_x, level_xy, out_own, out_peer):
    z, y, near = place[0], place[1], place[2]
    quarter = level.shape[1]
    depth = level.shape[0] // 4
    ends = [pl.multiple_of(near * quarter, 128), pl.multiple_of((1 - near) * quarter, 128)]
    for tokens, out in ((own_tokens, out_own), (peer_tokens, out_peer)):
        first = tokens[:, pl.ds(ends[0], quarter)]
        second = tokens[:, pl.ds(ends[1], quarter)]
        for side, (left, right) in enumerate(((level, level_x), (level_y, level_xy))):
            value = dot_rows(left[...], first) + dot_rows(right[...], second)
            for d in range(4):
                expert = 2 * (z ^ d) + (y ^ side)
                at = pl.ds(pl.multiple_of(expert * depth, depth), depth)
                out[at, :] = value[d * depth : (d + 1) * depth]


def half_logits(place, own_tokens, peer_tokens, *levels):
    rows = 2 * levels[0].shape[0]
    count, half = own_tokens.shape
    out = jax.ShapeDtypeStruct((rows, count), jnp.float32)
    return pl.pallas_call(
        logits_kernel,
        out_shape=(out, out),
        in_specs=[pl.BlockSpec(memory_space=pltpu.SMEM)] + [WHOLE] * 6,
        out_specs=(WHOLE, WHOLE),
        compiler_params=params(16),
        cost_estimate=cost(4 * rows * count * half, 2 * half * (rows + 2 * count)),
        name="half_logits",
    )(place, own_tokens, peer_tokens, *levels)


def log_sigmoid(value):
    return jnp.minimum(value, 0.0) - jnp.log1p(jnp.exp(-jnp.abs(value)))


def terms_kernel(ids, slots, mask, policy, *refs):
    parts, (weights, kl) = refs[:-2], refs[-2:]
    logits = parts[0][...]
    for part in parts[1:]:
        logits = logits + part[...]
    experts, tokens = logits.shape
    width = weights.shape[0]
    window = width // CAP
    scores = 1.0 / (1.0 + jnp.exp(-logits))
    names = lax.broadcasted_iota(jnp.int32, (experts, tokens), 0)
    choices = ids[...]
    chosen = jnp.zeros((experts, tokens), jnp.float32)
    for k in range(choices.shape[0]):
        chosen = chosen + jnp.where(names == choices[k : k + 1, :], scores, 0.0)
    total = jnp.sum(chosen, axis=0, keepdims=True)
    shares = (2.5 * scores[:window] / total).astype(jnp.bfloat16).astype(jnp.float32)
    spread = jnp.broadcast_to(shares[:, None, :], (window, CAP, tokens)).reshape(width, tokens)
    hits = buffer_hits(choices, slots[...], width)
    weights[...] = jnp.where(hits, spread, 0.0).astype(jnp.bfloat16)
    log_p = log_sigmoid(logits) - jnp.log(jnp.sum(scores, axis=0, keepdims=True))
    q = policy[...]
    policy_scores = 1.0 / (1.0 + jnp.exp(-q))
    log_q = log_sigmoid(q) - jnp.log(jnp.sum(policy_scores, axis=0, keepdims=True))
    keep = (1 - mask[...]).astype(jnp.float32)
    kl[...] = keep * jnp.sum(jnp.exp(log_q) * (log_q - log_p), axis=0, keepdims=True)


def router_terms(ids, slots, mask, policy, parts, width):
    experts, tokens = policy.shape
    return pl.pallas_call(
        terms_kernel,
        out_shape=(
            jax.ShapeDtypeStruct((width, tokens), jnp.bfloat16),
            jax.ShapeDtypeStruct((1, tokens), jnp.float32),
        ),
        in_specs=[WHOLE] * (4 + len(parts)),
        out_specs=(WHOLE, WHOLE),
        compiler_params=params(16),
        cost_estimate=cost(30 * experts * tokens, 12 * experts * tokens),
        name="router_terms",
    )(ids, slots, mask, policy, *parts)


def per_device(
    tokens,
    router_weight,
    gate_weight,
    up_weight,
    down_weight,
    policy_logits,
    expert_ids,
    slots,
    occupancy,
    env_mask,
):
    experts = lax.axis_size("expert")
    groups = lax.axis_size("groups")
    core = lax.axis_index("tensor")
    model_width = tokens.shape[1]
    width = experts * CAP
    half = model_width // 2
    staged = experts == 8 and groups == 2
    ids, slots = expert_ids.T, slots.T

    hits = buffer_hits(ids, slots, width)
    outgoing = jnp.dot(hits.astype(jnp.bfloat16), tokens, preferred_element_type=jnp.float32)
    outgoing = outgoing.astype(jnp.bfloat16).reshape(experts, CAP, model_width)
    arrived = lax.all_to_all(outgoing, "expert", split_axis=0, concat_axis=0, tiled=True)
    arrived = arrived.reshape(width, model_width)
    if staged:
        group, at = lax.axis_index("groups"), lax.axis_index("expert")
        quarter = half // 2
        piece = lax.dynamic_slice_in_dim(router_weight, core * half + group * quarter, quarter, axis=1)
        level = jnp.concatenate([piece] + [across(piece, "expert", 2 * d) for d in (1, 2, 3)], axis=0)
        own_tokens = lax.dynamic_slice_in_dim(tokens, core * half, half, axis=1)
        peer_tokens = swap_cores(lax.dynamic_slice_in_dim(tokens, (1 - core) * half, half, axis=1))
        arrived, level, peer_tokens = lax.optimization_barrier((arrived, level, peer_tokens))
        level_y = across(level, "expert", 1)
        level_x = across(level, "groups", 1)
    peer = swap_cores(arrived)
    *held, hidden = ffn_near(arrived, occupancy, gate_weight, up_weight, down_weight)
    ours, theirs = ffn_far(peer, occupancy, hidden, *held)
    if staged:
        ours, theirs, level_y, level_x = lax.optimization_barrier((ours, theirs, level_y, level_x))
    summed = add_halves(ours, swap_cores(theirs))
    returned = lax.all_to_all(
        summed.reshape(experts, CAP, model_width), "expert", split_axis=0, concat_axis=0, tiled=True
    )
    if staged:
        level_xy = across(level_y, "groups", 1)
        place = jnp.stack([at // 2, at % 2, group])
        mine, theirs = half_logits(
            place, own_tokens, peer_tokens, level, level_y, level_x, level_xy
        )
        parts = (mine, swap_cores(theirs))
    else:
        parts = (dot_rows(lax.all_gather(router_weight, "expert", axis=0, tiled=True), tokens),)
    weights, kl_terms = router_terms(
        ids, slots, env_mask[None, :], policy_logits.T, parts, width
    )
    mixed = dot_columns(weights, returned.reshape(width, model_width)).astype(jnp.bfloat16)
    return (mixed, kl_terms[0])


def solution(mesh):
    in_specs = (
        P(("groups", "expert", "tensor"), None),
        P("expert", None),
        P("expert", None, "tensor"),
        P("expert", None, "tensor"),
        P("expert", "tensor", None),
        P(("groups", "expert", "tensor"), None),
        P(("groups", "expert", "tensor"), None),
        P(("groups", "expert", "tensor"), None),
        P("expert", "groups"),
        P(("groups", "expert", "tensor")),
    )
    out_specs = (P(("groups", "expert", "tensor"), None), P(("groups", "expert", "tensor")))
    return jax.shard_map(
        per_device, mesh=mesh, in_specs=in_specs, out_specs=out_specs, check_vma=False
    )
```

time: 117 us -> 59.5 us (0.51)
  waiting for transfers between devices: 58.9 us -> 23.3 us
  between operations: 15.6 us -> 0.84 us
  Pallas kernels: 0 us -> 9.42 us
  matrix products: 12.7 us -> 3.59 us
  local copies, waits for them, and re-layouts: 10.2 us -> 1.36 us
  starting transfers between devices: 13.1 us -> 19.8 us
  blocking collectives: 2.45 us -> 0 us
  other arithmetic: 3.22 us -> 0.84 us
    all_gather x1 -> x0, waiting for transfers between devices: 40.9 us -> none  [per_device(): lax.all_gather(router_weight, 'expert', axis=0, tiled=True)]
    ppermute x0 -> x10, waiting for transfers between devices: none -> 21 us  [the longest x6 18 us: across(): return lax.ppermute(value, axis, [(s, s ^ distance) for s in range(size)])]
    all_to_all x1, waiting for transfers between devices: 10.8 us -> 0.01 us  [per_device(): lax.all_to_all(outgoing, 'expert', split_axis=0, concat_axis=0, tiled=True)]
    pallas_call x0 -> x5, Pallas kernels: none -> 9.42 us  [the longest x1 4.34 us: ffn_near(): pl.pallas_call(functools.partial(near_kernel, parts), out_shape=tuple((ja...]
    dot_general x5 -> x2, matrix products: 12.7 us -> 3.59 us  [the longest x1 2.24 us: per_device(): jnp.dot(hits.astype(jnp.bfloat16), tokens, preferred_element_type=jnp.flo...]
    ppermute x0 -> x10, starting transfers between devices: none -> 9.03 us  [the longest x6 8.74 us: across(): return lax.ppermute(value, axis, [(s, s ^ distance) for s in range(size)])]
    gather x5 -> x0, local copies, waits for them, and re-layouts: 8.91 us -> none  [router_terms(): chosen = jnp.take_along_axis(scores, expert_ids, axis=1)]
    reduce_scatter x1 -> x0, waiting for transfers between devices: 6.68 us -> none  [per_device(): lax.psum_scatter(partial_value.astype(jnp.float32).astype(jnp.bfloat16),...]
  transfers between devices with their start and end apart: 4 -> 12, of which waited for: 3 -> 6; matrix products, arithmetic and copies ran while one was open for 12% -> 2% of each run, Pallas kernels for 0% -> 14%
where the time goes in v2:
time: 59.5 us; the launch traced here: 59.1 us
  waiting for transfers between devices  23.3 us (39%)
  starting transfers between devices  19.8 us (33%)
  Pallas kernels  9.42 us (16%)
  matrix products  3.59 us (6%)
  local copies, waits for them, and re-layouts  1.36 us (2%)
  other arithmetic  0.84 us (1%)
  between operations  0.84 us (1%)
    ppermute x6, waiting for transfers between devices, across(): return lax.ppermute(value, axis, [(s, s ^ distance) for s in range(size)])  18 us
    ppermute x6, starting transfers between devices, across(): return lax.ppermute(value, axis, [(s, s ^ distance) for s in range(size)])  8.74 us
    all_to_all x1, starting transfers between devices, per_device(): lax.all_to_all(outgoing, 'expert', split_axis=0, concat_axis=0, tiled=True)  7.27 us
    pallas_call x1, Pallas kernels, ffn_near(): pl.pallas_call(functools.partial(near_kernel, parts), out_shape=tuple((ja...  4.34 us
    all_to_all x1, starting transfers between devices, per_device(): lax.all_to_all(summed.reshape(experts, CAP, model_width), 'expert', split...  3.47 us
    ppermute x4, waiting for transfers between devices, swap_cores(): return lax.ppermute(value, 'tensor', SWAP)  3.04 us
    all_to_all x1, waiting for transfers between devices, per_device(): lax.all_to_all(summed.reshape(experts, CAP, model_width), 'expert', split...  2.27 us
    dot_general x1, matrix products, per_device(): jnp.dot(hits.astype(jnp.bfloat16), tokens, preferred_element_type=jnp.flo...  2.24 us
  transfers between devices with their start and end apart: 12, of which 6 were waited for; matrix products, arithmetic and copies ran while one was open for 2% of the time, Pallas kernels for 14%

profile of v2, /device:TPU:0, one launch (start us, length us, event | category | flops | bytes accessed | tf_op | source)
XLA Modules:
  0.0 59.1 jit_solution(5988916416663878490)
XLA Ops:
  0.7 0.7 %add_select_fusion = s32[8,128]{1,0:T(8,128)S(1)} fusion(s32[128,8]{0,1:T(8,128)} %param.17, s32[128,8]{0,1:T(8,128)} %param.16), kind=kLoop, calls=%fused_computation.28 | loop fusion | flops 6144 | bytes 12288 | tf_op jit(solution)/shard_map/jit(_where)/select_n | solution.py:48
  1.4 2.2 %fusion = bf16[8,8,3584]{2,1,0:T(8,128)(2,1)} fusion(bf16[128,3584]{1,0:T(8,128)(2,1)} %param.10, s32[128]{0:T(128)S(1)} %get-tuple-element.39, s32[128]{0:T(128)S(1)} %get-tuple-element.40, s32[128]{0:T(128)S(1)} %get-tuple-element.41, s32[128]{0:T(128)S(1)} %get-tuple-element.42, s32[128]{0:T(128)S(1)} %get-tuple-element.43, ...), kind=kOutput, calls=%fused_computation.2 | convolution fusion | flops 59072512 | bytes 1380352 | tf_op jit(solution)/shard_map/dot_general | solution.py:254
  3.7 7.3 %all-to-all-start = ((bf16[8,8,3584]{2,1,0:T(8,128)(2,1)}), bf16[8,8,3584]{2,1,0:T(8,128)(2,1)S(1)}, u32[]{:S(2)}, u32[]{:S(2)}) async-start(bf16[8,8,3584]{2,1,0:T(8,128)(2,1)} %fusion), calls=%async_computation | async-start | bytes 917504 | tf_op jit(solution)/shard_map/all_to_all | solution.py:256
  10.9 1.2 %constant_dynamic-slice_fusion = (bf16[128,1792]{1,0:T(8,128)(2,1)S(1)}, bf16[128,1792]{1,0:T(8,128)(2,1)S(1)}) fusion(bf16[128,3584]{1,0:T(8,128)(2,1)} %param.10, s32[]{:T(128)S(6)} %select_n.29, s32[]{:T(128)S(6)} %select_n.26), kind=kLoop, calls=%fused_computation.29 | loop fusion | bytes 1835016 | tf_op jit(solution)/shard_map/dynamic_slice | solution.py:264
  12.3 2.1 %collective-permute-start = (bf16[32,896]{1,0:T(8,128)(2,1)S(1)}, bf16[32,896]{1,0:T(8,128)(2,1)S(1)}, u32[]{:S(2)}, u32[]{:S(2)}) collective-permute-start(bf16[32,896]{1,0:T(8,128)(2,1)S(1)} %constant_dynamic-slice_fusion.1), channel_id=1, source_target_pairs={{0,4},{2,6},{4,0},{6,2},{8,12},{10,14},{12,8},{14,10},{1,5},{3,7},... | collective-permute-start | bytes 172040 | tf_op jit(solution)/shard_map/ppermute | solution.py:22
  14.3 2.4 %collective-permute-start.1 = (bf16[32,896]{1,0:T(8,128)(2,1)S(1)}, bf16[32,896]{1,0:T(8,128)(2,1)S(1)}, u32[]{:S(2)}, u32[]{:S(2)}) collective-permute-start(bf16[32,896]{1,0:T(8,128)(2,1)S(1)} %constant_dynamic-slice_fusion.1), channel_id=1, source_target_pairs={{0,8},{2,10},{4,12},{6,14},{8,0},{10,2},{12,4},{14,6},{1,9},{3,11}... | collective-permute-start | bytes 172040 | tf_op jit(solution)/shard_map/ppermute | solution.py:22
  16.7 0.1 collective-permute-start.2
  16.8 4.1 %collective-permute-done = bf16[32,896]{1,0:T(8,128)(2,1)S(1)} collective-permute-done((bf16[32,896]{1,0:T(8,128)(2,1)S(1)}, bf16[32,896]{1,0:T(8,128)(2,1)S(1)}, u32[]{:S(2)}, u32[]{:S(2)}) %collective-permute-start) | collective-permute-done | bytes 57376 | tf_op jit(solution)/shard_map/ppermute | solution.py:22
  20.9 7.4 %collective-permute-done.1 = bf16[32,896]{1,0:T(8,128)(2,1)S(1)} collective-permute-done((bf16[32,896]{1,0:T(8,128)(2,1)S(1)}, bf16[32,896]{1,0:T(8,128)(2,1)S(1)}, u32[]{:S(2)}, u32[]{:S(2)}) %collective-permute-start.1) | collective-permute-done | bytes 57376 | tf_op jit(solution)/shard_map/ppermute | solution.py:22
  28.4 1.5 %collective-permute-start.5 = (bf16[128,896]{1,0:T(8,128)(2,1)S(1)}, bf16[128,896]{1,0:T(8,128)(2,1)S(1)}, u32[]{:S(2)}, u32[]{:S(2)}) collective-permute-start(bf16[128,896]{1,0:T(8,128)(2,1)S(1)} %pad_maximum_fusion.level), channel_id=1, source_target_pairs={{0,2},{2,0},{4,6},{6,4},{8,10},{10,8},{12,14},{14,12},{1,3},{3,1},... | collective-permute-start | bytes 688136 | tf_op jit(solution)/shard_map/ppermute | solution.py:22
  30.0 1.5 %collective-permute-start.6 = (bf16[128,896]{1,0:T(8,128)(2,1)S(1)}, bf16[128,896]{1,0:T(8,128)(2,1)S(1)}, u32[]{:S(2)}, u32[]{:S(2)}) collective-permute-start(bf16[128,896]{1,0:T(8,128)(2,1)S(1)} %pad_maximum_fusion.level), channel_id=1, source_target_pairs={{0,16},{16,0},{1,17},{17,1},{2,18},{18,2},{3,19},{19,3},{4,20},{20... | collective-permute-start | bytes 688136 | tf_op jit(solution)/shard_map/ppermute | solution.py:22
  31.5 4.3 %ffn_near.1 = (bf16[1,3584,512]{2,1,0:T(8,128)(2,1)S(1)}, bf16[1,3584,512]{2,1,0:T(8,128)(2,1)S(1)}, bf16[1,512,3584]{2,1,0:T(8,128)(2,1)S(1)}, bf16[64,512]{1,0:T(8,128)(2,1)S(1)}) custom-call(bf16[64,3584]{1,0:T(8,128)(2,1)S(1)} %bitcast.36, s32[1,16]{1,0:T(1,128)S(1)} %copy-done.3, bf16[1,3584,512]{2,1,0:T(8,128)(2,1)} %gate.1, bf16[1,3584,512]{2,1,0:T(8,128)(2,1)} %up.1, ...), custom_call_target="tpu_custom_call" | custom-call | flops 469762048 | bytes 458752 | tf_op jit(solution)/shard_map/ffn_near/pallas_call | solution.py:94
  35.8 2.0 %ffn_far.1 = (bf16[64,3584]{1,0:T(8,128)(2,1)S(1)}, bf16[64,3584]{1,0:T(8,128)(2,1)S(1)}) custom-call(bf16[64,3584]{1,0:T(8,128)(2,1)S(1)} %collective-permute-done.4.peer, s32[1,16]{1,0:T(1,128)S(1)} %copy-done.3, bf16[64,512]{1,0:T(8,128)(2,1)S(1)} %get-tuple-element.22.own_hidden, bf16[1,3584,512]{2,1,0:T(8,128)(2,1)S(1)} %get-tuple-element.23.gate, ...), custom_call_target="tpu_custom_call" | custom-call | flops 939524096 | bytes 458752 | tf_op jit(solution)/shard_map/ffn_far/pallas_call | solution.py:127
  38.0 1.8 %collective-permute-done.9.other = bf16[64,3584]{1,0:T(8,128)(2,1)S(1)} collective-permute-done((bf16[64,3584]{1,0:T(8,128)(2,1)S(1)}, bf16[64,3584]{1,0:T(8,128)(2,1)S(1)}, u32[]{:S(2)}, u32[]{:S(2)}) %collective-permute-start.9) | collective-permute-done | bytes 458784 | tf_op jit(solution)/shard_map/ppermute | solution.py:17
  39.8 0.9 %add_halves.1 = bf16[64,3584]{1,0:T(8,128)(2,1)} custom-call(bf16[64,3584]{1,0:T(8,128)(2,1)S(1)} %get-tuple-element.33.ours, bf16[64,3584]{1,0:T(8,128)(2,1)S(1)} %collective-permute-done.9.other), custom_call_target="tpu_custom_call" | custom-call | flops 229376 | bytes 1376256 | tf_op jit(solution)/shard_map/add_halves/pallas_call | solution.py:143
  40.7 3.5 %all-to-all-start.1 = ((bf16[8,8,3584]{2,1,0:T(8,128)(2,1)}), bf16[8,8,3584]{2,1,0:T(8,128)(2,1)S(1)}, u32[]{:S(2)}, u32[]{:S(2)}) async-start(bf16[8,8,3584]{2,1,0:T(8,128)(2,1)} %bitcast.17), calls=%async_computation.1 | async-start | bytes 917504 | tf_op jit(solution)/shard_map/all_to_all | solution.py:274
  44.2 1.2 %collective-permute-start.7 = (bf16[128,896]{1,0:T(8,128)(2,1)S(1)}, bf16[128,896]{1,0:T(8,128)(2,1)S(1)}, u32[]{:S(2)}, u32[]{:S(2)}) collective-permute-start(bf16[128,896]{1,0:T(8,128)(2,1)S(1)} %collective-permute-done.5.level_y), channel_id=1, source_target_pairs={{0,16},{16,0},{1,17},{17,1},{2,18},{18,2},{3,19},{19,3},{4,20},{20... | collective-permute-start | bytes 688136 | tf_op jit(solution)/shard_map/ppermute | solution.py:22
  45.4 6.4 %collective-permute-done.7.level_xy = bf16[128,896]{1,0:T(8,128)(2,1)S(1)} collective-permute-done((bf16[128,896]{1,0:T(8,128)(2,1)S(1)}, bf16[128,896]{1,0:T(8,128)(2,1)S(1)}, u32[]{:S(2)}, u32[]{:S(2)}) %collective-permute-start.7) | collective-permute-done | bytes 229408 | tf_op jit(solution)/shard_map/ppermute | solution.py:22
  51.9 1.3 %half_logits.1 = (f32[256,128]{1,0:T(8,128)S(1)}, f32[256,128]{1,0:T(8,128)S(1)}) custom-call(s32[3]{0:T(128)S(1)} %pad_add_fusion.place, bf16[128,1792]{1,0:T(8,128)(2,1)S(1)} %get-tuple-element.37.own_tokens, bf16[128,1792]{1,0:T(8,128)(2,1)S(1)} %collective-permute-done.3.peer_tokens, bf16[128,896]{1,0:T(8,128)(2,1)S(1)} %pad_maximum_fusion.level, ...), custom_call_target="tpu_custom_call" | custom-call | flops 234881024 | bytes 1835008 | tf_op jit(solution)/shard_map/half_logits/pallas_call | solution.py:174
  53.3 0.1 copy.12
  53.4 1.2 %collective-permute-done.8.refs_1_ = f32[256,128]{1,0:T(8,128)S(1)} collective-permute-done((f32[256,128]{1,0:T(8,128)S(1)}, f32[256,128]{1,0:T(8,128)S(1)}, u32[]{:S(2)}, u32[]{:S(2)}) %collective-permute-start.8) | collective-permute-done | bytes 131104 | tf_op jit(solution)/shard_map/ppermute | solution.py:17
  54.6 0.9 %router_terms.1 = (bf16[64,128]{1,0:T(8,128)(2,1)S(1)}, f32[1,128]{1,0:T(1,128)}) custom-call(s32[8,128]{1,0:T(8,128)S(1)} %bitcast.38, s32[8,128]{1,0:T(8,128)S(1)} %bitcast.39, s32[1,128]{1,0:T(1,128)S(1)} %bitcast.40, f32[256,128]{1,0:T(8,128)S(1)} %bitcast.37, f32[256,128]{1,0:T(8,128)S(1)} %get-tuple-element.30.refs_0_, ...), custom_call_target="tpu_custom_call" | custom-call | flops 983040 | bytes 393216 | tf_op jit(solution)/shard_map/router_terms/pallas_call | solution.py:218
  55.5 2.3 %all-to-all-done.1 = bf16[8,8,3584]{2,1,0:T(8,128)(2,1)S(1)} async-done(((bf16[8,8,3584]{2,1,0:T(8,128)(2,1)}), bf16[8,8,3584]{2,1,0:T(8,128)(2,1)S(1)}, u32[]{:S(2)}, u32[]{:S(2)}) %all-to-all-start.1) | async-done | bytes 458784 | tf_op jit(solution)/shard_map/all_to_all | solution.py:274
  57.8 1.4 %convolution_convert_fusion = bf16[128,3584]{1,0:T(8,128)(2,1)} fusion(bf16[64,128]{1,0:T(8,128)(2,1)S(1)} %get-tuple-element.32, bf16[8,8,3584]{2,1,0:T(8,128)(2,1)S(1)} %all-to-all-done.1), kind=kOutput, calls=%fused_computation | convolution fusion | flops 59179008 | bytes 1392640 | tf_op jit(solution)/shard_map/dot_general | solution.py:32
  (26 shorter events, 0.5 us)
Async XLA Ops:
  0.6 11.6 %copy-start = (bf16[32,3584]{1,0:T(8,128)(2,1)S(1)}, bf16[32,3584]{1,0:T(8,128)(2,1)}, u32[]{:S(2)}) copy-start(bf16[32,3584]{1,0:T(8,128)(2,1)} %param.11) | copy-start | bytes 688132
  0.6 30.8 %copy-start.3 = (s32[1,16]{1,0:T(1,128)S(1)}, s32[1,16]{1,0:T(1,128)}, u32[]{:S(2)}) copy-start(s32[1,16]{1,0:T(1,128)} %occupancy.3) | copy-start | bytes 196
  3.7 24.7 %all-to-all-start = ((bf16[8,8,3584]{2,1,0:T(8,128)(2,1)}), bf16[8,8,3584]{2,1,0:T(8,128)(2,1)S(1)}, u32[]{:S(2)}, u32[]{:S(2)}) async-start(bf16[8,8,3584]{2,1,0:T(8,128)(2,1)} %fusion), calls=%async_computation | async-start | bytes 917504 | tf_op jit(solution)/shard_map/all_to_all | solution.py:256
  12.1 16.2 %collective-permute-start.3 = (bf16[128,1792]{1,0:T(8,128)(2,1)S(1)}, bf16[128,1792]{1,0:T(8,128)(2,1)S(1)}, u32[]{:S(2)}, u32[]{:S(2)}) collective-permute-start(bf16[128,1792]{1,0:T(8,128)(2,1)S(1)} %get-tuple-element.36), channel_id=1, source_target_pairs={{0,1},{1,0},{2,3},{3,2},{4,5},{5,4},{6,7},{7,6},{8,9},{9,8},{10,11... | collective-permute-start | bytes 1376264 | tf_op jit(solution)/shard_map/ppermute | solution.py:17
  12.3 8.7 %collective-permute-start = (bf16[32,896]{1,0:T(8,128)(2,1)S(1)}, bf16[32,896]{1,0:T(8,128)(2,1)S(1)}, u32[]{:S(2)}, u32[]{:S(2)}) collective-permute-start(bf16[32,896]{1,0:T(8,128)(2,1)S(1)} %constant_dynamic-slice_fusion.1), channel_id=1, source_target_pairs={{0,4},{2,6},{4,0},{6,2},{8,12},{10,14},{12,8},{14,10},{1,5},{3,7},... | collective-permute-start | bytes 172040 | tf_op jit(solution)/shard_map/ppermute | solution.py:22
  14.3 14.0 %collective-permute-start.1 = (bf16[32,896]{1,0:T(8,128)(2,1)S(1)}, bf16[32,896]{1,0:T(8,128)(2,1)S(1)}, u32[]{:S(2)}, u32[]{:S(2)}) collective-permute-start(bf16[32,896]{1,0:T(8,128)(2,1)S(1)} %constant_dynamic-slice_fusion.1), channel_id=1, source_target_pairs={{0,8},{2,10},{4,12},{6,14},{8,0},{10,2},{12,4},{14,6},{1,9},{3,11}... | collective-permute-start | bytes 172040 | tf_op jit(solution)/shard_map/ppermute | solution.py:22
  16.7 11.6 %collective-permute-start.2 = (bf16[32,896]{1,0:T(8,128)(2,1)S(1)}, bf16[32,896]{1,0:T(8,128)(2,1)S(1)}, u32[]{:S(2)}, u32[]{:S(2)}) collective-permute-start(bf16[32,896]{1,0:T(8,128)(2,1)S(1)} %constant_dynamic-slice_fusion.1), channel_id=1, source_target_pairs={{0,12},{2,14},{4,8},{6,10},{8,4},{10,6},{12,0},{14,2},{1,13},{3,15... | collective-permute-start | bytes 172040 | tf_op jit(solution)/shard_map/ppermute | solution.py:22
  28.4 7.5 %collective-permute-start.4 = (bf16[64,3584]{1,0:T(8,128)(2,1)S(1)}, bf16[64,3584]{1,0:T(8,128)(2,1)S(1)}, u32[]{:S(2)}, u32[]{:S(2)}) collective-permute-start(bf16[64,3584]{1,0:T(8,128)(2,1)S(1)} %bitcast.35), channel_id=1, source_target_pairs={{0,1},{1,0},{2,3},{3,2},{4,5},{5,4},{6,7},{7,6},{8,9},{9,8},{10,11... | collective-permute-start | bytes 1376264 | tf_op jit(solution)/shard_map/ppermute | solution.py:17
  28.4 9.5 %collective-permute-start.5 = (bf16[128,896]{1,0:T(8,128)(2,1)S(1)}, bf16[128,896]{1,0:T(8,128)(2,1)S(1)}, u32[]{:S(2)}, u32[]{:S(2)}) collective-permute-start(bf16[128,896]{1,0:T(8,128)(2,1)S(1)} %pad_maximum_fusion.level), channel_id=1, source_target_pairs={{0,2},{2,0},{4,6},{6,4},{8,10},{10,8},{12,14},{14,12},{1,3},{3,1},... | collective-permute-start | bytes 688136 | tf_op jit(solution)/shard_map/ppermute | solution.py:22
  30.0 8.0 %collective-permute-start.6 = (bf16[128,896]{1,0:T(8,128)(2,1)S(1)}, bf16[128,896]{1,0:T(8,128)(2,1)S(1)}, u32[]{:S(2)}, u32[]{:S(2)}) collective-permute-start(bf16[128,896]{1,0:T(8,128)(2,1)S(1)} %pad_maximum_fusion.level), channel_id=1, source_target_pairs={{0,16},{16,0},{1,17},{17,1},{2,18},{18,2},{3,19},{19,3},{4,20},{20... | collective-permute-start | bytes 688136 | tf_op jit(solution)/shard_map/ppermute | solution.py:22
  37.9 15.4 %copy-start.5 = (f32[128,256]{1,0:T(8,128)S(1)}, f32[128,256]{1,0:T(8,128)}, u32[]{:S(2)}) copy-start(f32[128,256]{1,0:T(8,128)} %param.15) | copy-start | bytes 393220
  37.9 16.7 %copy-start.1 = (s32[128,8]{0,1:T(8,128)S(1)}, s32[128,8]{0,1:T(8,128)}, u32[]{:S(2)}) copy-start(s32[128,8]{0,1:T(8,128)} %param.16) | copy-start | bytes 12292
  37.9 16.7 %copy-start.2 = (s32[128,8]{0,1:T(8,128)S(1)}, s32[128,8]{0,1:T(8,128)}, u32[]{:S(2)}) copy-start(s32[128,8]{0,1:T(8,128)} %param.17) | copy-start | bytes 12292
  37.9 16.7 %copy-start.4 = (s32[128]{0:T(128)S(1)}, s32[128]{0:T(128)}, u32[]{:S(2)}) copy-start(s32[128]{0:T(128)} %param.19) | copy-start | bytes 1540
  37.9 1.9 %collective-permute-start.9 = (bf16[64,3584]{1,0:T(8,128)(2,1)S(1)}, bf16[64,3584]{1,0:T(8,128)(2,1)S(1)}, u32[]{:S(2)}, u32[]{:S(2)}) collective-permute-start(bf16[64,3584]{1,0:T(8,128)(2,1)S(1)} %get-tuple-element.34), channel_id=1, source_target_pairs={{0,1},{1,0},{2,3},{3,2},{4,5},{5,4},{6,7},{7,6},{8,9},{9,8},{10,11... | collective-permute-start | bytes 1376264 | tf_op jit(solution)/shard_map/ppermute | solution.py:17
  40.7 17.1 %all-to-all-start.1 = ((bf16[8,8,3584]{2,1,0:T(8,128)(2,1)}), bf16[8,8,3584]{2,1,0:T(8,128)(2,1)S(1)}, u32[]{:S(2)}, u32[]{:S(2)}) async-start(bf16[8,8,3584]{2,1,0:T(8,128)(2,1)} %bitcast.17), calls=%async_computation.1 | async-start | bytes 917504 | tf_op jit(solution)/shard_map/all_to_all | solution.py:274
  44.2 7.7 %collective-permute-start.7 = (bf16[128,896]{1,0:T(8,128)(2,1)S(1)}, bf16[128,896]{1,0:T(8,128)(2,1)S(1)}, u32[]{:S(2)}, u32[]{:S(2)}) collective-permute-start(bf16[128,896]{1,0:T(8,128)(2,1)S(1)} %collective-permute-done.5.level_y), channel_id=1, source_target_pairs={{0,16},{16,0},{1,17},{17,1},{2,18},{18,2},{3,19},{19,3},{4,20},{20... | collective-permute-start | bytes 688136 | tf_op jit(solution)/shard_map/ppermute | solution.py:22
  53.2 1.4 %collective-permute-start.8 = (f32[256,128]{1,0:T(8,128)S(1)}, f32[256,128]{1,0:T(8,128)S(1)}, u32[]{:S(2)}, u32[]{:S(2)}) collective-permute-start(f32[256,128]{1,0:T(8,128)S(1)} %get-tuple-element.31), channel_id=1, source_target_pairs={{0,1},{1,0},{2,3},{3,2},{4,5},{5,4},{6,7},{7,6},{8,9},{9,8},{10,11... | collective-permute-start | bytes 393224 | tf_op jit(solution)/shard_map/ppermute | solution.py:17

commit v3 on v2

v3 whole, which is shorter than its diff:
```python
import functools

import jax
import jax.numpy as jnp
from jax import lax
from jax.experimental import pallas as pl
from jax.experimental.pallas import tpu as pltpu
from jax.sharding import PartitionSpec as P

CAP = 8
SWAP = [(0, 1), (1, 0)]
WHOLE = pl.BlockSpec(memory_space=pltpu.VMEM)
LEFT = pl.BlockSpec(memory_space=pltpu.HBM)


def swap_cores(value):
    return lax.ppermute(value, "tensor", SWAP)


def across(value, axis, distance):
    size = lax.axis_size(axis)
    return lax.ppermute(value, axis, [(s, s ^ distance) for s in range(size)])


def dot_rows(left, right):
    return lax.dot_general(
        left, right, (((1,), (1,)), ((), ())), preferred_element_type=jnp.float32
    )


def dot_columns(left, right):
    return lax.dot_general(
        left, right, (((0,), (0,)), ((), ())), preferred_element_type=jnp.float32
    )


def params(mib):
    return pltpu.CompilerParams(vmem_limit_bytes=mib << 20)


def cost(flops, nbytes):
    return pl.CostEstimate(flops=flops, bytes_accessed=nbytes, transcendentals=0)


def buffer_hits(ids, slots, width):
    choices, tokens = ids.shape
    valid = (ids < width // CAP) & (slots < CAP)
    place = jnp.where(valid, ids * CAP + slots, -1)
    rows = lax.broadcasted_iota(jnp.int32, (width, tokens), 0)
    hits = rows == place[0:1, :]
    for k in range(1, choices):
        hits = hits | (rows == place[k : k + 1, :])
    return hits


def load_kernel(*refs):
    sems = refs[-1]
    count = (len(refs) - 1) // 2
    copies = [
        pltpu.make_async_copy(refs[n], refs[count + n], sems.at[n]) for n in range(count)
    ]
    for copy in copies:
        copy.start()
    for copy in copies:
        copy.wait()


def load(*weights):
    there = [pltpu.with_memory_space_constraint(w, pltpu.HBM) for w in weights]
    return pl.pallas_call(
        load_kernel,
        out_shape=tuple(jax.ShapeDtypeStruct(w.shape, w.dtype) for w in weights),
        in_specs=[LEFT] * len(weights),
        out_specs=(WHOLE,) * len(weights),
        scratch_shapes=[pltpu.SemaphoreType.DMA((len(weights),))],
        compiler_params=params(16),
        cost_estimate=cost(0, sum(2 * w.size for w in weights)),
        name="load",
    )(*there)


def masked_hidden(g, u, occupancy, order, side):
    count = g.shape[0]
    sources = occupancy.shape[1]
    row = lax.broadcasted_iota(jnp.int32, (count, sources), 0)
    column = lax.broadcasted_iota(jnp.int32, (count, sources), 1)
    here = column == 2 * ((row // CAP) ^ order) + side
    used = jnp.sum(jnp.where(here, occupancy[...], 0), axis=1, keepdims=True)
    live = row[:, 0:1] % CAP < used
    return jnp.where(live, g / (1.0 + jnp.exp(-g)) * u, 0.0).astype(jnp.bfloat16)


def ffn_kernel(parts, relative, own, peer, occupancy, gate, up, down, out_own, out_peer):
    count = own.shape[0]
    wide = down.shape[2] // parts
    order = lax.axis_index("expert") if relative else 0
    core = lax.axis_index("tensor")
    rows = jnp.concatenate([own[...], peer[...]], axis=0)
    g = jnp.dot(rows, gate[0], preferred_element_type=jnp.float32)
    u = jnp.dot(rows, up[0], preferred_element_type=jnp.float32)
    hidden = jnp.concatenate(
        [
            masked_hidden(g[:count], u[:count], occupancy, order, core),
            masked_hidden(g[count:], u[count:], occupancy, order, 1 - core),
        ],
        axis=0,
    )
    for part in range(parts):
        at = slice(part * wide, (part + 1) * wide)
        value = jnp.dot(hidden, down[0, :, at], preferred_element_type=jnp.float32)
        value = value.astype(jnp.bfloat16)
        out_own[:, at] = value[:count]
        out_peer[:, at] = value[count:]


def ffn(relative, own, peer, occupancy, gate, up, down):
    half = jax.ShapeDtypeStruct(own.shape, own.dtype)
    count, model_width = own.shape
    hidden_width = gate.shape[2]
    parts = 4 if model_width % 512 == 0 else 1
    return pl.pallas_call(
        functools.partial(ffn_kernel, parts, relative),
        out_shape=(half, half),
        in_specs=[WHOLE] * 6,
        out_specs=(WHOLE, WHOLE),
        compiler_params=params(16),
        cost_estimate=cost(12 * count * model_width * hidden_width, 6 * model_width * hidden_width),
        name="ffn",
    )(own, peer, occupancy, gate, up, down)


def add_kernel(relative, ours, other, out):
    value = ours[...].astype(jnp.float32) + other[...].astype(jnp.float32)
    order = lax.axis_index("expert") if relative else 0
    for block in range(out.shape[0]):
        out[block ^ order] = value[block * CAP : (block + 1) * CAP].astype(out.dtype)


def add_halves(relative, ours, other):
    rows, model_width = ours.shape
    return pl.pallas_call(
        functools.partial(add_kernel, relative),
        out_shape=jax.ShapeDtypeStruct((rows // CAP, CAP, model_width), ours.dtype),
        in_specs=[WHOLE] * 2,
        out_specs=WHOLE,
        compiler_params=params(16),
        cost_estimate=cost(ours.size, 6 * ours.size),
        name="add_halves",
    )(ours, other)


def logits_kernel(own_tokens, peer_tokens, *refs):
    levels, (out_own, out_peer) = refs[:-2], refs[-2:]
    expert, group = lax.axis_index("expert"), lax.axis_index("groups")
    rows = jnp.concatenate([level[...] for level in levels], axis=0)
    for tokens, out in ((own_tokens, out_own), (peer_tokens, out_peer)):
        value = dot_rows(rows, tokens[...])
        for near in range(2):
            for d in range(8):
                block = near * 8 + d
                at = 2 * (expert ^ d) + (group ^ near)
                at = pl.ds(pl.multiple_of(at * 8, 8), 8)
                out[at, :] = value[block * 8 : (block + 1) * 8]


def half_logits(own_tokens, peer_tokens, *levels):
    rows = sum(level.shape[0] for level in levels)
    count, model_width = own_tokens.shape
    out = jax.ShapeDtypeStruct((rows, count), jnp.float32)
    return pl.pallas_call(
        logits_kernel,
        out_shape=(out, out),
        in_specs=[WHOLE] * 6,
        out_specs=(WHOLE, WHOLE),
        compiler_params=params(16),
        cost_estimate=cost(4 * rows * count * model_width, 2 * model_width * (rows + 2 * count)),
        name="half_logits",
    )(own_tokens, peer_tokens, *levels)


def log_sigmoid(value):
    return jnp.minimum(value, 0.0) - jnp.log1p(jnp.exp(-jnp.abs(value)))


def terms_kernel(count, ids, slots, mask, policy, *refs):
    weights, kl = refs[count : count + 2]
    parts = refs[:count] + refs[count + 2 :]
    if len(parts) == 1:
        logits = parts[0][...]
    else:
        mine, theirs, whole = parts
        core = lax.axis_index("tensor")
        for block in range(mine.shape[0] // 16):
            for part, side in ((mine, core), (theirs, 1 - core)):
                at = pl.multiple_of(block * 32 + side * 16, 16)
                whole[pl.ds(at, 16), :] = part[block * 16 : (block + 1) * 16]
        logits = whole[...]
    experts, tokens = logits.shape
    width = weights.shape[0]
    window = width // CAP
    scores = 1.0 / (1.0 + jnp.exp(-logits))
    names = lax.broadcasted_iota(jnp.int32, (experts, tokens), 0)
    choices = ids[...]
    chosen = jnp.zeros((experts, tokens), jnp.float32)
    for k in range(choices.shape[0]):
        chosen = chosen + jnp.where(names == choices[k : k + 1, :], scores, 0.0)
    total = jnp.sum(chosen, axis=0, keepdims=True)
    shares = (2.5 * scores[:window] / total).astype(jnp.bfloat16).astype(jnp.float32)
    spread = jnp.broadcast_to(shares[:, None, :], (window, CAP, tokens)).reshape(width, tokens)
    hits = buffer_hits(choices, slots[...], width)
    weights[...] = jnp.where(hits, spread, 0.0).astype(jnp.bfloat16)
    log_p = log_sigmoid(logits) - jnp.log(jnp.sum(scores, axis=0, keepdims=True))
    q = policy[...]
    policy_scores = 1.0 / (1.0 + jnp.exp(-q))
    log_q = log_sigmoid(q) - jnp.log(jnp.sum(policy_scores, axis=0, keepdims=True))
    keep = (1 - mask[...]).astype(jnp.float32)
    kl[...] = keep * jnp.sum(jnp.exp(log_q) * (log_q - log_p), axis=0, keepdims=True)


def router_terms(ids, slots, mask, policy, parts, width):
    experts, tokens = policy.shape
    whole = [pltpu.VMEM(policy.shape, jnp.float32)] if len(parts) > 1 else []
    return pl.pallas_call(
        functools.partial(terms_kernel, len(parts)),
        out_shape=(
            jax.ShapeDtypeStruct((width, tokens), jnp.bfloat16),
            jax.ShapeDtypeStruct((1, tokens), jnp.float32),
        ),
        in_specs=[WHOLE] * (4 + len(parts)),
        out_specs=(WHOLE, WHOLE),
        scratch_shapes=whole,
        compiler_params=params(16),
        cost_estimate=cost(30 * experts * tokens, 12 * experts * tokens),
        name="router_terms",
    )(ids, slots, mask, policy, *parts)


def per_device(
    tokens,
    router_weight,
    gate_weight,
    up_weight,
    down_weight,
    policy_logits,
    expert_ids,
    slots,
    occupancy,
    env_mask,
):
    experts = lax.axis_size("expert")
    groups = lax.axis_size("groups")
    core = lax.axis_index("tensor")
    model_width = tokens.shape[1]
    width = experts * CAP
    staged = experts == 8 and groups == 2 and router_weight.shape[0] == 32
    ids, slots = expert_ids.T, slots.T

    hits = buffer_hits(ids, slots, width)
    outgoing = jnp.dot(hits.astype(jnp.bfloat16), tokens, preferred_element_type=jnp.float32)
    outgoing = outgoing.astype(jnp.bfloat16).reshape(experts, CAP, model_width)
    if staged:
        at, group = lax.axis_index("expert"), lax.axis_index("groups")
        piece = lax.dynamic_slice_in_dim(router_weight, (2 * core + group) * 8, 8, axis=0)
        blocks, pieces = [lax.dynamic_index_in_dim(outgoing, at, 0, keepdims=False)], [piece]
        for d in range(1, 8):
            block = lax.dynamic_index_in_dim(outgoing, at ^ d, 0, keepdims=False)
            if d < 6:
                pair = across(jnp.concatenate([block, piece], axis=0), "expert", d)
                block = pair[:CAP]
                pieces.append(pair[CAP:])
            else:
                block = across(block, "expert", d)
            blocks.append(block)
        level_a = jnp.concatenate(pieces[:4], axis=0)
        level_b = jnp.concatenate(pieces[4:], axis=0)
        level_b = jnp.concatenate([level_b, across(level_b, "expert", 2)], axis=0)
        next_a = across(level_a, "groups", 1)
        weights = (gate_weight, up_weight, down_weight)
        blocks[4], *weights = lax.optimization_barrier((blocks[4], *weights))
        held = load(*weights)
        arrived = jnp.concatenate(blocks, axis=0)
        arrived, level_b, next_a, *held = lax.optimization_barrier((arrived, level_b, next_a, *held))
    else:
        arrived = lax.all_to_all(outgoing, "expert", split_axis=0, concat_axis=0, tiled=True)
        arrived = arrived.reshape(width, model_width)
        held = (gate_weight, up_weight, down_weight)
    ours, theirs = ffn(staged, arrived, swap_cores(arrived), occupancy, *held)
    summed = add_halves(staged, ours, swap_cores(theirs))
    returned = lax.all_to_all(summed, "expert", split_axis=0, concat_axis=0, tiled=True)
    if staged:
        next_b = across(level_b, "groups", 1)
        peer_tokens = swap_cores(tokens)
        mine, theirs = half_logits(tokens, peer_tokens, level_a, level_b, next_a, next_b)
        parts = (mine, swap_cores(theirs))
    else:
        parts = (dot_rows(lax.all_gather(router_weight, "expert", axis=0, tiled=True), tokens),)
    weights, kl_terms = router_terms(
        ids, slots, env_mask[None, :], policy_logits.T, parts, width
    )
    mixed = dot_columns(weights, returned.reshape(width, model_width)).astype(jnp.bfloat16)
    return (mixed, kl_terms[0])


def solution(mesh):
    in_specs = (
        P(("groups", "expert", "tensor"), None),
        P("expert", None),
        P("expert", None, "tensor"),
        P("expert", None, "tensor"),
        P("expert", "tensor", None),
        P(("groups", "expert", "tensor"), None),
        P(("groups", "expert", "tensor"), None),
        P(("groups", "expert", "tensor"), None),
        P("expert", "groups"),
        P(("groups", "expert", "tensor")),
    )
    out_specs = (P(("groups", "expert", "tensor"), None), P(("groups", "expert", "tensor")))
    return jax.shard_map(
        per_device, mesh=mesh, in_specs=in_specs, out_specs=out_specs, check_vma=False
    )
```

time: 59.5 us -> 55.1 us (0.926)
  waiting for transfers between devices: 23.3 us -> 19 us
  starting transfers between devices: 19.8 us -> 22.5 us
  local copies, waits for them, and re-layouts: 1.36 us -> 0.32 us
  Pallas kernels: 9.42 us -> 8.51 us
  matrix products: 3.59 us -> 2.81 us
    ppermute x6 -> x10, starting transfers between devices: 8.74 us -> 16.9 us  [across(): return lax.ppermute(value, axis, [(s, s ^ distance) for s in range(size)])]
    ppermute x6 -> x10, waiting for transfers between devices: 18 us -> 11.7 us  [across(): return lax.ppermute(value, axis, [(s, s ^ distance) for s in range(size)])]
    all_to_all x2 -> x1, starting transfers between devices: 10.7 us -> 4.9 us  [per_device(): lax.all_to_all(summed, 'expert', split_axis=0, concat_axis=0, tiled=True)]
    dynamic_slice x2 -> x1, local copies, waits for them, and re-layouts: 1.23 us -> 0.01 us  [per_device(): lax.dynamic_slice_in_dim(router_weight, (2 * core + group) * 8, 8, axis=0)]
    ppermute x4, waiting for transfers between devices: 3.04 us -> 4.25 us  [swap_cores(): return lax.ppermute(value, 'tensor', SWAP)]
    pallas_call x5, Pallas kernels: 9.42 us -> 8.51 us  [the longest x1 4.23 us: load(): pl.pallas_call(load_kernel, out_shape=tuple((jax.ShapeDtypeStruct(w.shape...]
    all_to_all x2 -> x1, waiting for transfers between devices: 2.28 us -> 3.07 us  [per_device(): lax.all_to_all(summed, 'expert', split_axis=0, concat_axis=0, tiled=True)]
    dot_general x1, matrix products: 2.24 us -> 1.46 us  [per_device(): jnp.dot(hits.astype(jnp.bfloat16), tokens, preferred_element_type=jnp.flo...]
  transfers between devices with their start and end apart: 12 -> 15, of which waited for: 6 -> 9; matrix products, arithmetic and copies ran while one was open for 2% -> 0% of each run, Pallas kernels for 14% -> 12%
where the time goes in v3:
time: 55.1 us; the launch traced here: 54.9 us
  starting transfers between devices  22.5 us (41%)
  waiting for transfers between devices  19 us (34%)
  Pallas kernels  8.51 us (15%)
  matrix products  2.81 us (5%)
  between operations  0.95 us (2%)
  other arithmetic  0.86 us (2%)
    ppermute x10, starting transfers between devices, across(): return lax.ppermute(value, axis, [(s, s ^ distance) for s in range(size)])  16.9 us
    ppermute x10, waiting for transfers between devices, across(): return lax.ppermute(value, axis, [(s, s ^ distance) for s in range(size)])  11.7 us
    all_to_all x1, starting transfers between devices, per_device(): lax.all_to_all(summed, 'expert', split_axis=0, concat_axis=0, tiled=True)  4.9 us
    ppermute x4, waiting for transfers between devices, swap_cores(): return lax.ppermute(value, 'tensor', SWAP)  4.25 us
    pallas_call x1, Pallas kernels, load(): pl.pallas_call(load_kernel, out_shape=tuple((jax.ShapeDtypeStruct(w.shape...  4.23 us
    all_to_all x1, waiting for transfers between devices, per_device(): lax.all_to_all(summed, 'expert', split_axis=0, concat_axis=0, tiled=True)  3.07 us
    pallas_call x1, Pallas kernels, ffn(): pl.pallas_call(functools.partial(ffn_kernel, parts, relative), out_shape=...  1.8 us
    dot_general x1, matrix products, per_device(): jnp.dot(hits.astype(jnp.bfloat16), tokens, preferred_element_type=jnp.flo...  1.46 us
  transfers between devices with their start and end apart: 15, of which 9 were waited for; matrix products, arithmetic and copies ran while one was open for 0% of the time, Pallas kernels for 12%

profile of v3, /device:TPU:0, one launch (start us, length us, event | category | flops | bytes accessed | tf_op | source)
XLA Modules:
  0.0 54.9 jit_solution(6989046629155932839)
XLA Ops:
  0.7 0.8 %add_select_fusion = s32[8,128]{1,0:T(8,128)S(1)} fusion(s32[128,8]{0,1:T(8,128)} %param.17, s32[128,8]{0,1:T(8,128)} %param.16), kind=kLoop, calls=%fused_computation.50 | loop fusion | flops 6144 | bytes 12288 | tf_op jit(solution)/shard_map/jit(_where)/select_n | solution.py:48
  1.6 1.5 %fusion = bf16[8,8,3584]{2,1,0:T(8,128)(2,1)S(1)} fusion(bf16[128,3584]{1,0:T(8,128)(2,1)} %own_tokens.1, s32[128]{0:T(128)S(1)} %get-tuple-element.63, s32[128]{0:T(128)S(1)} %get-tuple-element.64, s32[128]{0:T(128)S(1)} %get-tuple-element.65, s32[128]{0:T(128)S(1)} %get-tuple-element.66, s32[128]{0:T(128)S(1)} %get-tuple-element.67, ...), kind=kOutput, calls=%fused_computation.2 | convolution fusion | flops 59072512 | bytes 1380352 | tf_op jit(solution)/shard_map/dot_general | solution.py:259
  3.1 4.1 %collective-permute-start.4 = (bf16[16,3584]{1,0:T(8,128)(2,1)S(1)}, bf16[16,3584]{1,0:T(8,128)(2,1)S(1)}, u32[]{:S(2)}, u32[]{:S(2)}) collective-permute-start(bf16[16,3584]{1,0:T(8,128)(2,1)S(1)} %get-tuple-element.60), channel_id=1, source_target_pairs={{0,8},{2,10},{4,12},{6,14},{8,0},{10,2},{12,4},{14,6},{1,9},{3,11}... | collective-permute-start | bytes 344072 | tf_op jit(solution)/shard_map/ppermute | solution.py:22
  7.3 1.5 %collective-permute-start.1 = (bf16[16,3584]{1,0:T(8,128)(2,1)S(1)}, bf16[16,3584]{1,0:T(8,128)(2,1)S(1)}, u32[]{:S(2)}, u32[]{:S(2)}) collective-permute-start(bf16[16,3584]{1,0:T(8,128)(2,1)S(1)} %get-tuple-element.61), channel_id=1, source_target_pairs={{0,2},{2,0},{4,6},{6,4},{8,10},{10,8},{12,14},{14,12},{1,3},{3,1},... | collective-permute-start | bytes 344072 | tf_op jit(solution)/shard_map/ppermute | solution.py:22
  8.8 1.6 %collective-permute-start.2 = (bf16[16,3584]{1,0:T(8,128)(2,1)S(1)}, bf16[16,3584]{1,0:T(8,128)(2,1)S(1)}, u32[]{:S(2)}, u32[]{:S(2)}) collective-permute-start(bf16[16,3584]{1,0:T(8,128)(2,1)S(1)} %get-tuple-element.58), channel_id=1, source_target_pairs={{0,4},{2,6},{4,0},{6,2},{8,12},{10,14},{12,8},{14,10},{1,5},{3,7},... | collective-permute-start | bytes 344072 | tf_op jit(solution)/shard_map/ppermute | solution.py:22
  10.7 1.3 %collective-permute-start.5 = (bf16[16,3584]{1,0:T(8,128)(2,1)S(1)}, bf16[16,3584]{1,0:T(8,128)(2,1)S(1)}, u32[]{:S(2)}, u32[]{:S(2)}) collective-permute-start(bf16[16,3584]{1,0:T(8,128)(2,1)S(1)} %get-tuple-element.57), channel_id=1, source_target_pairs={{0,10},{2,8},{4,14},{6,12},{8,2},{10,0},{12,6},{14,4},{1,11},{3,9}... | collective-permute-start | bytes 344072 | tf_op jit(solution)/shard_map/ppermute | solution.py:22
  12.0 0.9 %collective-permute-done.4 = bf16[16,3584]{1,0:T(8,128)(2,1)S(1)} collective-permute-done((bf16[16,3584]{1,0:T(8,128)(2,1)S(1)}, bf16[16,3584]{1,0:T(8,128)(2,1)S(1)}, u32[]{:S(2)}, u32[]{:S(2)}) %collective-permute-start.4) | collective-permute-done | bytes 114720 | tf_op jit(solution)/shard_map/ppermute | solution.py:22
  12.9 3.6 %collective-permute-start.6 = (bf16[8,3584]{1,0:T(8,128)(2,1)S(1)}, bf16[8,3584]{1,0:T(8,128)(2,1)S(1)}, u32[]{:S(2)}, u32[]{:S(2)}) collective-permute-start(bf16[8,3584]{1,0:T(8,128)(2,1)S(1)} %get-tuple-element.41), channel_id=1, source_target_pairs={{0,12},{2,14},{4,8},{6,10},{8,4},{10,6},{12,0},{14,2},{1,13},{3,15... | collective-permute-start | bytes 172040 | tf_op jit(solution)/shard_map/ppermute | solution.py:22
  16.6 1.3 %collective-permute-start.7 = (bf16[8,3584]{1,0:T(8,128)(2,1)S(1)}, bf16[8,3584]{1,0:T(8,128)(2,1)S(1)}, u32[]{:S(2)}, u32[]{:S(2)}) collective-permute-start(bf16[8,3584]{1,0:T(8,128)(2,1)S(1)} %get-tuple-element.40), channel_id=1, source_target_pairs={{0,14},{2,12},{4,10},{6,8},{8,6},{10,4},{12,2},{14,0},{1,15},{3,13... | collective-permute-start | bytes 172040 | tf_op jit(solution)/shard_map/ppermute | solution.py:22
  17.9 1.2 %collective-permute-done.3 = bf16[16,3584]{1,0:T(8,128)(2,1)S(1)} collective-permute-done((bf16[16,3584]{1,0:T(8,128)(2,1)S(1)}, bf16[16,3584]{1,0:T(8,128)(2,1)S(1)}, u32[]{:S(2)}, u32[]{:S(2)}) %collective-permute-start.3) | collective-permute-done | bytes 114720 | tf_op jit(solution)/shard_map/ppermute | solution.py:22
  19.1 3.5 %collective-permute-done.5 = bf16[16,3584]{1,0:T(8,128)(2,1)S(1)} collective-permute-done((bf16[16,3584]{1,0:T(8,128)(2,1)S(1)}, bf16[16,3584]{1,0:T(8,128)(2,1)S(1)}, u32[]{:S(2)}, u32[]{:S(2)}) %collective-permute-start.5) | collective-permute-done | bytes 114720 | tf_op jit(solution)/shard_map/ppermute | solution.py:22
  22.7 1.6 %collective-permute-start.9 = (bf16[32,3584]{1,0:T(8,128)(2,1)S(1)}, bf16[32,3584]{1,0:T(8,128)(2,1)S(1)}, u32[]{:S(2)}, u32[]{:S(2)}) collective-permute-start(bf16[32,3584]{1,0:T(8,128)(2,1)S(1)} %pad_maximum_fusion.refs_0_), channel_id=1, source_target_pairs={{0,16},{16,0},{1,17},{17,1},{2,18},{18,2},{3,19},{19,3},{4,20},{20... | collective-permute-start | bytes 688136 | tf_op jit(solution)/shard_map/ppermute | solution.py:22
  24.3 4.2 %load.1 = (bf16[1,3584,512]{2,1,0:T(8,128)(2,1)S(1)}, bf16[1,3584,512]{2,1,0:T(8,128)(2,1)S(1)}, bf16[1,512,3584]{2,1,0:T(8,128)(2,1)S(1)}) custom-call(bf16[1,3584,512]{2,1,0:T(8,128)(2,1)} %refs_0_, bf16[1,3584,512]{2,1,0:T(8,128)(2,1)} %refs_1_, bf16[1,512,3584]{2,1,0:T(8,128)(2,1)} %refs_2_), custom_call_target="tpu_custom_call" | custom-call | bytes 11010048 | tf_op jit(solution)/shard_map/load/pallas_call | solution.py:70
  28.8 1.8 %collective-permute-done.12.peer = bf16[64,3584]{1,0:T(8,128)(2,1)S(1)} collective-permute-done((bf16[64,3584]{1,0:T(8,128)(2,1)S(1)}, bf16[64,3584]{1,0:T(8,128)(2,1)S(1)}, u32[]{:S(2)}, u32[]{:S(2)}) %collective-permute-start.12) | collective-permute-done | bytes 458784 | tf_op jit(solution)/shard_map/ppermute | solution.py:17
  30.6 1.8 %ffn.1 = (bf16[64,3584]{1,0:T(8,128)(2,1)S(1)}, bf16[64,3584]{1,0:T(8,128)(2,1)S(1)}) custom-call(bf16[64,3584]{1,0:T(8,128)(2,1)S(1)} %constant_dynamic-update-slice_fusion.own, bf16[64,3584]{1,0:T(8,128)(2,1)S(1)} %collective-permute-done.12.peer, s32[1,16]{1,0:T(1,128)S(1)} %copy-done.4, bf16[1,3584,512]{2,1,0:T(8,128)(2,1)S(1)} %get-tuple-element.34.gate, ...), custom_call_target="tpu_custom_call" | custom-call | flops 1409286144 | bytes 11010048 | tf_op jit(solution)/shard_map/ffn/pallas_call | solution.py:121
  33.1 1.3 %collective-permute-done.13.other = bf16[64,3584]{1,0:T(8,128)(2,1)S(1)} collective-permute-done((bf16[64,3584]{1,0:T(8,128)(2,1)S(1)}, bf16[64,3584]{1,0:T(8,128)(2,1)S(1)}, u32[]{:S(2)}, u32[]{:S(2)}) %collective-permute-start.13) | collective-permute-done | bytes 458784 | tf_op jit(solution)/shard_map/ppermute | solution.py:17
  34.4 0.9 %add_halves.1 = bf16[8,8,3584]{2,1,0:T(8,128)(2,1)} custom-call(bf16[64,3584]{1,0:T(8,128)(2,1)S(1)} %get-tuple-element.37.ours, bf16[64,3584]{1,0:T(8,128)(2,1)S(1)} %collective-permute-done.13.other), custom_call_target="tpu_custom_call" | custom-call | flops 229376 | bytes 1376256 | tf_op jit(solution)/shard_map/add_halves/pallas_call | solution.py:141
  35.2 4.9 %all-to-all-start = ((bf16[8,8,3584]{2,1,0:T(8,128)(2,1)}), bf16[8,8,3584]{2,1,0:T(8,128)(2,1)S(1)}, u32[]{:S(2)}, u32[]{:S(2)}) async-start(bf16[8,8,3584]{2,1,0:T(8,128)(2,1)} %add_halves.1), calls=%async_computation | async-start | bytes 917504 | tf_op jit(solution)/shard_map/all_to_all | solution.py:289
  40.1 1.5 %collective-permute-start.10 = (bf16[32,3584]{1,0:T(8,128)(2,1)S(1)}, bf16[32,3584]{1,0:T(8,128)(2,1)S(1)}, u32[]{:S(2)}, u32[]{:S(2)}) collective-permute-start(bf16[32,3584]{1,0:T(8,128)(2,1)S(1)} %pad_maximum_fusion.1.refs_1_), channel_id=1, source_target_pairs={{0,16},{16,0},{1,17},{17,1},{2,18},{18,2},{3,19},{19,3},{4,20},{20... | collective-permute-start | bytes 688136 | tf_op jit(solution)/shard_map/ppermute | solution.py:22
  41.6 5.9 %collective-permute-done.10.refs_3_ = bf16[32,3584]{1,0:T(8,128)(2,1)S(1)} collective-permute-done((bf16[32,3584]{1,0:T(8,128)(2,1)S(1)}, bf16[32,3584]{1,0:T(8,128)(2,1)S(1)}, u32[]{:S(2)}, u32[]{:S(2)}) %collective-permute-start.10) | collective-permute-done | bytes 229408 | tf_op jit(solution)/shard_map/ppermute | solution.py:22
  48.3 1.1 %collective-permute-done.11.refs_1_ = f32[128,128]{1,0:T(8,128)S(1)} collective-permute-done((f32[128,128]{1,0:T(8,128)S(1)}, f32[128,128]{1,0:T(8,128)S(1)}, u32[]{:S(2)}, u32[]{:S(2)}) %collective-permute-start.11) | collective-permute-done | bytes 65568 | tf_op jit(solution)/shard_map/ppermute | solution.py:17
  49.5 1.0 %router_terms.1 = (bf16[64,128]{1,0:T(8,128)(2,1)S(1)}, f32[1,128]{1,0:T(1,128)}) custom-call(s32[8,128]{1,0:T(8,128)S(1)} %bitcast.47, s32[8,128]{1,0:T(8,128)S(1)} %bitcast.48, s32[1,128]{1,0:T(1,128)S(1)} %bitcast.49, f32[256,128]{1,0:T(8,128)S(1)} %bitcast.46, f32[128,128]{1,0:T(8,128)S(1)} %get-tuple-element.30.refs_0_, ...), custom_call_target="tpu_custom_call" | custom-call | flops 983040 | bytes 393216 | tf_op jit(solution)/shard_map/router_terms/pallas_call | solution.py:223
  50.5 3.1 %all-to-all-done = bf16[8,8,3584]{2,1,0:T(8,128)(2,1)S(1)} async-done(((bf16[8,8,3584]{2,1,0:T(8,128)(2,1)}), bf16[8,8,3584]{2,1,0:T(8,128)(2,1)S(1)}, u32[]{:S(2)}, u32[]{:S(2)}) %all-to-all-start) | async-done | bytes 458784 | tf_op jit(solution)/shard_map/all_to_all | solution.py:289
  53.5 1.4 %convolution_convert_fusion = bf16[128,3584]{1,0:T(8,128)(2,1)} fusion(bf16[64,128]{1,0:T(8,128)(2,1)S(1)} %get-tuple-element.32, bf16[8,8,3584]{2,1,0:T(8,128)(2,1)S(1)} %all-to-all-done), kind=kOutput, calls=%fused_computation | convolution fusion | flops 59179008 | bytes 1392640 | tf_op jit(solution)/shard_map/dot_general | solution.py:32
  (45 shorter events, 2.4 us)
Async XLA Ops:
  0.6 0.9 %copy-start = (bf16[32,3584]{1,0:T(8,128)(2,1)S(1)}, bf16[32,3584]{1,0:T(8,128)(2,1)}, u32[]{:S(2)}) copy-start(bf16[32,3584]{1,0:T(8,128)(2,1)} %param.11) | copy-start | bytes 688132
  3.1 9.8 %collective-permute-start.4 = (bf16[16,3584]{1,0:T(8,128)(2,1)S(1)}, bf16[16,3584]{1,0:T(8,128)(2,1)S(1)}, u32[]{:S(2)}, u32[]{:S(2)}) collective-permute-start(bf16[16,3584]{1,0:T(8,128)(2,1)S(1)} %get-tuple-element.60), channel_id=1, source_target_pairs={{0,8},{2,10},{4,12},{6,14},{8,0},{10,2},{12,4},{14,6},{1,9},{3,11}... | collective-permute-start | bytes 344072 | tf_op jit(solution)/shard_map/ppermute | solution.py:22
  7.3 9.3 %collective-permute-start.1 = (bf16[16,3584]{1,0:T(8,128)(2,1)S(1)}, bf16[16,3584]{1,0:T(8,128)(2,1)S(1)}, u32[]{:S(2)}, u32[]{:S(2)}) collective-permute-start(bf16[16,3584]{1,0:T(8,128)(2,1)S(1)} %get-tuple-element.61), channel_id=1, source_target_pairs={{0,2},{2,0},{4,6},{6,4},{8,10},{10,8},{12,14},{14,12},{1,3},{3,1},... | collective-permute-start | bytes 344072 | tf_op jit(solution)/shard_map/ppermute | solution.py:22
  8.8 9.1 %collective-permute-start.2 = (bf16[16,3584]{1,0:T(8,128)(2,1)S(1)}, bf16[16,3584]{1,0:T(8,128)(2,1)S(1)}, u32[]{:S(2)}, u32[]{:S(2)}) collective-permute-start(bf16[16,3584]{1,0:T(8,128)(2,1)S(1)} %get-tuple-element.58), channel_id=1, source_target_pairs={{0,4},{2,6},{4,0},{6,2},{8,12},{10,14},{12,8},{14,10},{1,5},{3,7},... | collective-permute-start | bytes 344072 | tf_op jit(solution)/shard_map/ppermute | solution.py:22
  10.3 8.7 %collective-permute-start.3 = (bf16[16,3584]{1,0:T(8,128)(2,1)S(1)}, bf16[16,3584]{1,0:T(8,128)(2,1)S(1)}, u32[]{:S(2)}, u32[]{:S(2)}) collective-permute-start(bf16[16,3584]{1,0:T(8,128)(2,1)S(1)} %get-tuple-element.59), channel_id=1, source_target_pairs={{0,6},{2,4},{4,2},{6,0},{8,14},{10,12},{12,10},{14,8},{1,7},{3,5},... | collective-permute-start | bytes 344072 | tf_op jit(solution)/shard_map/ppermute | solution.py:22
  10.7 11.8 %collective-permute-start.5 = (bf16[16,3584]{1,0:T(8,128)(2,1)S(1)}, bf16[16,3584]{1,0:T(8,128)(2,1)S(1)}, u32[]{:S(2)}, u32[]{:S(2)}) collective-permute-start(bf16[16,3584]{1,0:T(8,128)(2,1)S(1)} %get-tuple-element.57), channel_id=1, source_target_pairs={{0,10},{2,8},{4,14},{6,12},{8,2},{10,0},{12,6},{14,4},{1,11},{3,9}... | collective-permute-start | bytes 344072 | tf_op jit(solution)/shard_map/ppermute | solution.py:22
  12.9 11.3 %collective-permute-start.6 = (bf16[8,3584]{1,0:T(8,128)(2,1)S(1)}, bf16[8,3584]{1,0:T(8,128)(2,1)S(1)}, u32[]{:S(2)}, u32[]{:S(2)}) collective-permute-start(bf16[8,3584]{1,0:T(8,128)(2,1)S(1)} %get-tuple-element.41), channel_id=1, source_target_pairs={{0,12},{2,14},{4,8},{6,10},{8,4},{10,6},{12,0},{14,2},{1,13},{3,15... | collective-permute-start | bytes 172040 | tf_op jit(solution)/shard_map/ppermute | solution.py:22
  16.6 7.7 %collective-permute-start.7 = (bf16[8,3584]{1,0:T(8,128)(2,1)S(1)}, bf16[8,3584]{1,0:T(8,128)(2,1)S(1)}, u32[]{:S(2)}, u32[]{:S(2)}) collective-permute-start(bf16[8,3584]{1,0:T(8,128)(2,1)S(1)} %get-tuple-element.40), channel_id=1, source_target_pairs={{0,14},{2,12},{4,10},{6,8},{8,6},{10,4},{12,2},{14,0},{1,15},{3,13... | collective-permute-start | bytes 172040 | tf_op jit(solution)/shard_map/ppermute | solution.py:22
  22.6 6.0 %collective-permute-start.8 = (bf16[16,3584]{1,0:T(8,128)(2,1)S(1)}, bf16[16,3584]{1,0:T(8,128)(2,1)S(1)}, u32[]{:S(2)}, u32[]{:S(2)}) collective-permute-start(bf16[16,3584]{1,0:T(8,128)(2,1)S(1)} %pad_maximum_fusion.7), channel_id=1, source_target_pairs={{0,4},{2,6},{4,0},{6,2},{8,12},{10,14},{12,8},{14,10},{1,5},{3,7},... | collective-permute-start | bytes 344072 | tf_op jit(solution)/shard_map/ppermute | solution.py:22
  22.7 6.1 %collective-permute-start.9 = (bf16[32,3584]{1,0:T(8,128)(2,1)S(1)}, bf16[32,3584]{1,0:T(8,128)(2,1)S(1)}, u32[]{:S(2)}, u32[]{:S(2)}) collective-permute-start(bf16[32,3584]{1,0:T(8,128)(2,1)S(1)} %pad_maximum_fusion.refs_0_), channel_id=1, source_target_pairs={{0,16},{16,0},{1,17},{17,1},{2,18},{18,2},{3,19},{19,3},{4,20},{20... | collective-permute-start | bytes 688136 | tf_op jit(solution)/shard_map/ppermute | solution.py:22
  24.3 6.3 %copy-start.4 = (s32[1,16]{1,0:T(1,128)S(1)}, s32[1,16]{1,0:T(1,128)}, u32[]{:S(2)}) copy-start(s32[1,16]{1,0:T(1,128)} %occupancy.1) | copy-start | bytes 196
  28.8 3.9 %copy-start.1 = (bf16[128,3584]{1,0:T(8,128)(2,1)S(1)}, bf16[128,3584]{1,0:T(8,128)(2,1)}, u32[]{:S(2)}) copy-start(bf16[128,3584]{1,0:T(8,128)(2,1)} %own_tokens.1) | copy-start | bytes 2752516
  28.8 1.8 %collective-permute-start.12 = (bf16[64,3584]{1,0:T(8,128)(2,1)S(1)}, bf16[64,3584]{1,0:T(8,128)(2,1)S(1)}, u32[]{:S(2)}, u32[]{:S(2)}) collective-permute-start(bf16[64,3584]{1,0:T(8,128)(2,1)S(1)} %constant_dynamic-update-slice_fusion.own), channel_id=1, source_target_pairs={{0,1},{1,0},{2,3},{3,2},{4,5},{5,4},{6,7},{7,6},{8,9},{9,8},{10,11... | collective-permute-start | bytes 1376264 | tf_op jit(solution)/shard_map/ppermute | solution.py:17
  32.4 15.8 %copy-start.6 = (f32[128,256]{1,0:T(8,128)S(1)}, f32[128,256]{1,0:T(8,128)}, u32[]{:S(2)}) copy-start(f32[128,256]{1,0:T(8,128)} %param.15) | copy-start | bytes 393220
  32.4 17.0 %copy-start.2 = (s32[128,8]{0,1:T(8,128)S(1)}, s32[128,8]{0,1:T(8,128)}, u32[]{:S(2)}) copy-start(s32[128,8]{0,1:T(8,128)} %param.16) | copy-start | bytes 12292
  32.5 17.0 %copy-start.3 = (s32[128,8]{0,1:T(8,128)S(1)}, s32[128,8]{0,1:T(8,128)}, u32[]{:S(2)}) copy-start(s32[128,8]{0,1:T(8,128)} %param.17) | copy-start | bytes 12292
  32.5 17.0 %copy-start.5 = (s32[128]{0:T(128)S(1)}, s32[128]{0:T(128)}, u32[]{:S(2)}) copy-start(s32[128]{0:T(128)} %param.19) | copy-start | bytes 1540
  32.5 1.9 %collective-permute-start.13 = (bf16[64,3584]{1,0:T(8,128)(2,1)S(1)}, bf16[64,3584]{1,0:T(8,128)(2,1)S(1)}, u32[]{:S(2)}, u32[]{:S(2)}) collective-permute-start(bf16[64,3584]{1,0:T(8,128)(2,1)S(1)} %get-tuple-element.38), channel_id=1, source_target_pairs={{0,1},{1,0},{2,3},{3,2},{4,5},{5,4},{6,7},{7,6},{8,9},{9,8},{10,11... | collective-permute-start | bytes 1376264 | tf_op jit(solution)/shard_map/ppermute | solution.py:17
  32.7 14.8 %collective-permute-start = (bf16[128,3584]{1,0:T(8,128)(2,1)S(1)}, bf16[128,3584]{1,0:T(8,128)(2,1)S(1)}, u32[]{:S(2)}, u32[]{:S(2)}) collective-permute-start(bf16[128,3584]{1,0:T(8,128)(2,1)S(1)} %copy-done.1), channel_id=1, source_target_pairs={{0,1},{1,0},{2,3},{3,2},{4,5},{5,4},{6,7},{7,6},{8,9},{9,8},{10,11... | collective-permute-start | bytes 2752520 | tf_op jit(solution)/shard_map/ppermute | solution.py:17
  35.2 18.3 %all-to-all-start = ((bf16[8,8,3584]{2,1,0:T(8,128)(2,1)}), bf16[8,8,3584]{2,1,0:T(8,128)(2,1)S(1)}, u32[]{:S(2)}, u32[]{:S(2)}) async-start(bf16[8,8,3584]{2,1,0:T(8,128)(2,1)} %add_halves.1), calls=%async_computation | async-start | bytes 917504 | tf_op jit(solution)/shard_map/all_to_all | solution.py:289
  40.1 7.4 %collective-permute-start.10 = (bf16[32,3584]{1,0:T(8,128)(2,1)S(1)}, bf16[32,3584]{1,0:T(8,128)(2,1)S(1)}, u32[]{:S(2)}, u32[]{:S(2)}) collective-permute-start(bf16[32,3584]{1,0:T(8,128)(2,1)S(1)} %pad_maximum_fusion.1.refs_1_), channel_id=1, source_target_pairs={{0,16},{16,0},{1,17},{17,1},{2,18},{18,2},{3,19},{19,3},{4,20},{20... | collective-permute-start | bytes 688136 | tf_op jit(solution)/shard_map/ppermute | solution.py:22
  48.2 1.3 %collective-permute-start.11 = (f32[128,128]{1,0:T(8,128)S(1)}, f32[128,128]{1,0:T(8,128)S(1)}, u32[]{:S(2)}, u32[]{:S(2)}) collective-permute-start(f32[128,128]{1,0:T(8,128)S(1)} %get-tuple-element.31), channel_id=1, source_target_pairs={{0,1},{1,0},{2,3},{3,2},{4,5},{5,4},{6,7},{7,6},{8,9},{9,8},{10,11... | collective-permute-start | bytes 196616 | tf_op jit(solution)/shard_map/ppermute | solution.py:17

commit v4 on v3

--- a/solution.py
+++ b/solution.py
@@ -153,14 +153,17 @@
     levels, (out_own, out_peer) = refs[:-2], refs[-2:]
     expert, group = lax.axis_index("expert"), lax.axis_index("groups")
     rows = jnp.concatenate([level[...] for level in levels], axis=0)
+    places = [(expert ^ d) * 16 for d in range(4)]
+    for side in range(2):
+        places += [(expert ^ d) * 16 + (group ^ side) * 8 for d in range(4, 8)]
     for tokens, out in ((own_tokens, out_own), (peer_tokens, out_peer)):
         value = dot_rows(rows, tokens[...])
-        for near in range(2):
-            for d in range(8):
-                block = near * 8 + d
-                at = 2 * (expert ^ d) + (group ^ near)
-                at = pl.ds(pl.multiple_of(at * 8, 8), 8)
-                out[at, :] = value[block * 8 : (block + 1) * 8]
+        first = 0
+        for n, place in enumerate(places):
+            count = 16 if n < 4 else 8
+            at = pl.ds(pl.multiple_of(place, 8), count)
+            out[at, :] = value[first : first + count]
+            first += count
 
 
 def half_logits(own_tokens, peer_tokens, *levels):
@@ -170,7 +173,7 @@
     return pl.pallas_call(
         logits_kernel,
         out_shape=(out, out),
-        in_specs=[WHOLE] * 6,
+        in_specs=[WHOLE] * (2 + len(levels)),
         out_specs=(WHOLE, WHOLE),
         compiler_params=params(16),
         cost_estimate=cost(4 * rows * count * model_width, 2 * model_width * (rows + 2 * count)),
@@ -260,37 +263,42 @@
     outgoing = outgoing.astype(jnp.bfloat16).reshape(experts, CAP, model_width)
     if staged:
         at, group = lax.axis_index("expert"), lax.axis_index("groups")
-        piece = lax.dynamic_slice_in_dim(router_weight, (2 * core + group) * 8, 8, axis=0)
-        blocks, pieces = [lax.dynamic_index_in_dim(outgoing, at, 0, keepdims=False)], [piece]
+        mine = lax.dynamic_slice_in_dim(router_weight, core * 16, 16, axis=0)
+        piece = lax.dynamic_slice_in_dim(router_weight, core * 16 + group * 8, 8, axis=0)
+        blocks, near = [lax.dynamic_index_in_dim(outgoing, at, 0, keepdims=False)], [mine]
+        far = []
         for d in range(1, 8):
             block = lax.dynamic_index_in_dim(outgoing, at ^ d, 0, keepdims=False)
             if d < 6:
-                pair = across(jnp.concatenate([block, piece], axis=0), "expert", d)
+                along = mine if d < 4 else piece
+                pair = across(jnp.concatenate([block, along], axis=0), "expert", d)
                 block = pair[:CAP]
-                pieces.append(pair[CAP:])
+                (near if d < 4 else far).append(pair[CAP:])
             else:
                 block = across(block, "expert", d)
             blocks.append(block)
-        level_a = jnp.concatenate(pieces[:4], axis=0)
-        level_b = jnp.concatenate(pieces[4:], axis=0)
-        level_b = jnp.concatenate([level_b, across(level_b, "expert", 2)], axis=0)
-        next_a = across(level_a, "groups", 1)
+        level_a = jnp.concatenate(near, axis=0)
+        level_b = jnp.concatenate(far, axis=0)
         weights = (gate_weight, up_weight, down_weight)
         blocks[4], *weights = lax.optimization_barrier((blocks[4], *weights))
         held = load(*weights)
+        level_b, *held = lax.optimization_barrier((level_b, *held))
+        level_b = jnp.concatenate([level_b, across(level_b, "expert", 2)], axis=0)
         arrived = jnp.concatenate(blocks, axis=0)
-        arrived, level_b, next_a, *held = lax.optimization_barrier((arrived, level_b, next_a, *held))
+        arrived, *held = lax.optimization_barrier((arrived, *held))
     else:
         arrived = lax.all_to_all(outgoing, "expert", split_axis=0, concat_axis=0, tiled=True)
         arrived = arrived.reshape(width, model_width)
         held = (gate_weight, up_weight, down_weight)
     ours, theirs = ffn(staged, arrived, swap_cores(arrived), occupancy, *held)
+    if staged:
+        ours, theirs, level_b = lax.optimization_barrier((ours, theirs, level_b))
     summed = add_halves(staged, ours, swap_cores(theirs))
     returned = lax.all_to_all(summed, "expert", split_axis=0, concat_axis=0, tiled=True)
     if staged:
         next_b = across(level_b, "groups", 1)
         peer_tokens = swap_cores(tokens)
-        mine, theirs = half_logits(tokens, peer_tokens, level_a, level_b, next_a, next_b)
+        mine, theirs = half_logits(tokens, peer_tokens, level_a, level_b, next_b)
         parts = (mine, swap_cores(theirs))
     else:
         parts = (dot_rows(lax.all_gather(router_weight, "expert", axis=0, tiled=True), tokens),)

time: 55.1 us -> 53.4 us (0.969)
  starting transfers between devices: 22.5 us -> 20.7 us
    all_to_all x1, starting transfers between devices: 4.9 us -> 3.47 us  [per_device(): lax.all_to_all(summed, 'expert', split_axis=0, concat_axis=0, tiled=True)]
    ppermute x10 -> x9, starting transfers between devices: 16.9 us -> 16.6 us  [across(): return lax.ppermute(value, axis, [(s, s ^ distance) for s in range(size)])]
    ppermute x10 -> x9, waiting for transfers between devices: 11.7 us -> 11.9 us  [across(): return lax.ppermute(value, axis, [(s, s ^ distance) for s in range(size)])]
  transfers between devices with their start and end apart: 15 -> 14, of which waited for: 9 -> 8; matrix products, arithmetic and copies ran while one was open for 0% -> 1% of each run, Pallas kernels for 12% -> 13%
where the time goes in v4:
time: 53.4 us; the launch traced here: 53.2 us
  starting transfers between devices  20.7 us (39%)
  waiting for transfers between devices  19 us (36%)
  Pallas kernels  8.51 us (16%)
  matrix products  2.8 us (5%)
  between operations  0.97 us (2%)
  other arithmetic  0.89 us (2%)
    ppermute x9, starting transfers between devices, across(): return lax.ppermute(value, axis, [(s, s ^ distance) for s in range(size)])  16.6 us
    ppermute x9, waiting for transfers between devices, across(): return lax.ppermute(value, axis, [(s, s ^ distance) for s in range(size)])  11.9 us
    pallas_call x1, Pallas kernels, load(): pl.pallas_call(load_kernel, out_shape=tuple((jax.ShapeDtypeStruct(w.shape...  4.23 us
    ppermute x4, waiting for transfers between devices, swap_cores(): return lax.ppermute(value, 'tensor', SWAP)  4.2 us
    all_to_all x1, starting transfers between devices, per_device(): lax.all_to_all(summed, 'expert', split_axis=0, concat_axis=0, tiled=True)  3.47 us
    all_to_all x1, waiting for transfers between devices, per_device(): lax.all_to_all(summed, 'expert', split_axis=0, concat_axis=0, tiled=True)  2.87 us
    pallas_call x1, Pallas kernels, ffn(): pl.pallas_call(functools.partial(ffn_kernel, parts, relative), out_shape=...  1.79 us
    dot_general x1, matrix products, per_device(): jnp.dot(hits.astype(jnp.bfloat16), tokens, preferred_element_type=jnp.flo...  1.46 us
  transfers between devices with their start and end apart: 14, of which 8 were waited for; matrix products, arithmetic and copies ran while one was open for 1% of the time, Pallas kernels for 13%

profile of v4, /device:TPU:0, one launch (start us, length us, event | category | flops | bytes accessed | tf_op | source)
XLA Modules:
  0.0 53.2 jit_solution(1571462004134313466)
XLA Ops:
  0.7 0.8 %add_select_fusion = s32[8,128]{1,0:T(8,128)S(1)} fusion(s32[128,8]{0,1:T(8,128)} %param.17, s32[128,8]{0,1:T(8,128)} %param.16), kind=kLoop, calls=%fused_computation.50 | loop fusion | flops 6144 | bytes 12288 | tf_op jit(solution)/shard_map/jit(_where)/select_n | solution.py:48
  1.6 1.5 %fusion = bf16[8,8,3584]{2,1,0:T(8,128)(2,1)S(1)} fusion(bf16[128,3584]{1,0:T(8,128)(2,1)} %own_tokens.1, s32[128]{0:T(128)S(1)} %get-tuple-element.67, s32[128]{0:T(128)S(1)} %get-tuple-element.68, s32[128]{0:T(128)S(1)} %get-tuple-element.69, s32[128]{0:T(128)S(1)} %get-tuple-element.70, s32[128]{0:T(128)S(1)} %get-tuple-element.71, ...), kind=kOutput, calls=%fused_computation.2 | convolution fusion | flops 59072512 | bytes 1380352 | tf_op jit(solution)/shard_map/dot_general | solution.py:262
  3.1 4.1 %collective-permute-start.4 = (bf16[16,3584]{1,0:T(8,128)(2,1)S(1)}, bf16[16,3584]{1,0:T(8,128)(2,1)S(1)}, u32[]{:S(2)}, u32[]{:S(2)}) collective-permute-start(bf16[16,3584]{1,0:T(8,128)(2,1)S(1)} %get-tuple-element.65), channel_id=1, source_target_pairs={{0,8},{2,10},{4,12},{6,14},{8,0},{10,2},{12,4},{14,6},{1,9},{3,11}... | collective-permute-start | bytes 344072 | tf_op jit(solution)/shard_map/ppermute | solution.py:22
  7.3 1.6 %collective-permute-start.1 = (bf16[24,3584]{1,0:T(8,128)(2,1)S(1)}, bf16[24,3584]{1,0:T(8,128)(2,1)S(1)}, u32[]{:S(2)}, u32[]{:S(2)}) collective-permute-start(bf16[24,3584]{1,0:T(8,128)(2,1)S(1)} %get-tuple-element.61), channel_id=1, source_target_pairs={{0,2},{2,0},{4,6},{6,4},{8,10},{10,8},{12,14},{14,12},{1,3},{3,1},... | collective-permute-start | bytes 516104 | tf_op jit(solution)/shard_map/ppermute | solution.py:22
  8.9 1.6 %collective-permute-start.2 = (bf16[24,3584]{1,0:T(8,128)(2,1)S(1)}, bf16[24,3584]{1,0:T(8,128)(2,1)S(1)}, u32[]{:S(2)}, u32[]{:S(2)}) collective-permute-start(bf16[24,3584]{1,0:T(8,128)(2,1)S(1)} %get-tuple-element.62), channel_id=1, source_target_pairs={{0,4},{2,6},{4,0},{6,2},{8,12},{10,14},{12,8},{14,10},{1,5},{3,7},... | collective-permute-start | bytes 516104 | tf_op jit(solution)/shard_map/ppermute | solution.py:22
  10.8 1.3 %collective-permute-start.5 = (bf16[16,3584]{1,0:T(8,128)(2,1)S(1)}, bf16[16,3584]{1,0:T(8,128)(2,1)S(1)}, u32[]{:S(2)}, u32[]{:S(2)}) collective-permute-start(bf16[16,3584]{1,0:T(8,128)(2,1)S(1)} %get-tuple-element.64), channel_id=1, source_target_pairs={{0,10},{2,8},{4,14},{6,12},{8,2},{10,0},{12,6},{14,4},{1,11},{3,9}... | collective-permute-start | bytes 344072 | tf_op jit(solution)/shard_map/ppermute | solution.py:22
  12.1 0.8 %collective-permute-done.4 = bf16[16,3584]{1,0:T(8,128)(2,1)S(1)} collective-permute-done((bf16[16,3584]{1,0:T(8,128)(2,1)S(1)}, bf16[16,3584]{1,0:T(8,128)(2,1)S(1)}, u32[]{:S(2)}, u32[]{:S(2)}) %collective-permute-start.4) | collective-permute-done | bytes 114720 | tf_op jit(solution)/shard_map/ppermute | solution.py:22
  12.9 3.6 %collective-permute-start.6 = (bf16[8,3584]{1,0:T(8,128)(2,1)S(1)}, bf16[8,3584]{1,0:T(8,128)(2,1)S(1)}, u32[]{:S(2)}, u32[]{:S(2)}) collective-permute-start(bf16[8,3584]{1,0:T(8,128)(2,1)S(1)} %get-tuple-element.51), channel_id=1, source_target_pairs={{0,12},{2,14},{4,8},{6,10},{8,4},{10,6},{12,0},{14,2},{1,13},{3,15... | collective-permute-start | bytes 172040 | tf_op jit(solution)/shard_map/ppermute | solution.py:22
  16.6 4.2 %load.1 = (bf16[1,3584,512]{2,1,0:T(8,128)(2,1)S(1)}, bf16[1,3584,512]{2,1,0:T(8,128)(2,1)S(1)}, bf16[1,512,3584]{2,1,0:T(8,128)(2,1)S(1)}) custom-call(bf16[1,3584,512]{2,1,0:T(8,128)(2,1)} %refs_0_, bf16[1,3584,512]{2,1,0:T(8,128)(2,1)} %refs_1_, bf16[1,512,3584]{2,1,0:T(8,128)(2,1)} %refs_2_), custom_call_target="tpu_custom_call" | custom-call | bytes 11010048 | tf_op jit(solution)/shard_map/load/pallas_call | solution.py:70
  20.8 1.3 %collective-permute-start.7 = (bf16[8,3584]{1,0:T(8,128)(2,1)S(1)}, bf16[8,3584]{1,0:T(8,128)(2,1)S(1)}, u32[]{:S(2)}, u32[]{:S(2)}) collective-permute-start(bf16[8,3584]{1,0:T(8,128)(2,1)S(1)} %get-tuple-element.50), channel_id=1, source_target_pairs={{0,14},{2,12},{4,10},{6,8},{8,6},{10,4},{12,2},{14,0},{1,15},{3,13... | collective-permute-start | bytes 172040 | tf_op jit(solution)/shard_map/ppermute | solution.py:22
  22.5 1.2 %collective-permute-start.9 = (bf16[16,3584]{1,0:T(8,128)(2,1)S(1)}, bf16[16,3584]{1,0:T(8,128)(2,1)S(1)}, u32[]{:S(2)}, u32[]{:S(2)}) collective-permute-start(bf16[16,3584]{1,0:T(8,128)(2,1)S(1)} %pad_maximum_fusion.7), channel_id=1, source_target_pairs={{0,4},{2,6},{4,0},{6,2},{8,12},{10,14},{12,8},{14,10},{1,5},{3,7},... | collective-permute-start | bytes 344072 | tf_op jit(solution)/shard_map/ppermute | solution.py:22
  23.7 4.7 %collective-permute-done.7 = bf16[8,3584]{1,0:T(8,128)(2,1)S(1)} collective-permute-done((bf16[8,3584]{1,0:T(8,128)(2,1)S(1)}, bf16[8,3584]{1,0:T(8,128)(2,1)S(1)}, u32[]{:S(2)}, u32[]{:S(2)}) %collective-permute-start.7) | collective-permute-done | bytes 57376 | tf_op jit(solution)/shard_map/ppermute | solution.py:22
  28.4 1.8 %collective-permute-done.8.peer = bf16[64,3584]{1,0:T(8,128)(2,1)S(1)} collective-permute-done((bf16[64,3584]{1,0:T(8,128)(2,1)S(1)}, bf16[64,3584]{1,0:T(8,128)(2,1)S(1)}, u32[]{:S(2)}, u32[]{:S(2)}) %collective-permute-start.8) | collective-permute-done | bytes 458784 | tf_op jit(solution)/shard_map/ppermute | solution.py:17
  30.2 1.8 %ffn.1 = (bf16[64,3584]{1,0:T(8,128)(2,1)S(1)}, bf16[64,3584]{1,0:T(8,128)(2,1)S(1)}) custom-call(bf16[64,3584]{1,0:T(8,128)(2,1)S(1)} %constant_dynamic-update-slice_fusion.own, bf16[64,3584]{1,0:T(8,128)(2,1)S(1)} %collective-permute-done.8.peer, s32[1,16]{1,0:T(1,128)S(1)} %copy-done.4, bf16[1,3584,512]{2,1,0:T(8,128)(2,1)S(1)} %get-tuple-element.37.gate, ...), custom_call_target="tpu_custom_call" | custom-call | flops 1409286144 | bytes 11010048 | tf_op jit(solution)/shard_map/ffn/pallas_call | solution.py:121
  32.6 1.3 %collective-permute-done.12.other = bf16[64,3584]{1,0:T(8,128)(2,1)S(1)} collective-permute-done((bf16[64,3584]{1,0:T(8,128)(2,1)S(1)}, bf16[64,3584]{1,0:T(8,128)(2,1)S(1)}, u32[]{:S(2)}, u32[]{:S(2)}) %collective-permute-start.12) | collective-permute-done | bytes 458784 | tf_op jit(solution)/shard_map/ppermute | solution.py:17
  33.9 0.9 %add_halves.1 = bf16[8,8,3584]{2,1,0:T(8,128)(2,1)} custom-call(bf16[64,3584]{1,0:T(8,128)(2,1)S(1)} %get-tuple-element.47.ours, bf16[64,3584]{1,0:T(8,128)(2,1)S(1)} %collective-permute-done.12.other), custom_call_target="tpu_custom_call" | custom-call | flops 229376 | bytes 1376256 | tf_op jit(solution)/shard_map/add_halves/pallas_call | solution.py:141
  34.8 3.5 %all-to-all-start = ((bf16[8,8,3584]{2,1,0:T(8,128)(2,1)}), bf16[8,8,3584]{2,1,0:T(8,128)(2,1)S(1)}, u32[]{:S(2)}, u32[]{:S(2)}) async-start(bf16[8,8,3584]{2,1,0:T(8,128)(2,1)} %add_halves.1), calls=%async_computation | async-start | bytes 917504 | tf_op jit(solution)/shard_map/all_to_all | solution.py:297
  38.3 1.6 %collective-permute-start.10 = (bf16[32,3584]{1,0:T(8,128)(2,1)S(1)}, bf16[32,3584]{1,0:T(8,128)(2,1)S(1)}, u32[]{:S(2)}, u32[]{:S(2)}) collective-permute-start(bf16[32,3584]{1,0:T(8,128)(2,1)S(1)} %pad_maximum_fusion.1.refs_1_), channel_id=1, source_target_pairs={{0,16},{16,0},{1,17},{17,1},{2,18},{18,2},{3,19},{19,3},{4,20},{20... | collective-permute-start | bytes 688136 | tf_op jit(solution)/shard_map/ppermute | solution.py:22
  39.9 6.1 %collective-permute-done.10.refs_2_ = bf16[32,3584]{1,0:T(8,128)(2,1)S(1)} collective-permute-done((bf16[32,3584]{1,0:T(8,128)(2,1)S(1)}, bf16[32,3584]{1,0:T(8,128)(2,1)S(1)}, u32[]{:S(2)}, u32[]{:S(2)}) %collective-permute-start.10) | collective-permute-done | bytes 229408 | tf_op jit(solution)/shard_map/ppermute | solution.py:22
  46.0 0.6 %half_logits.1 = (f32[128,128]{1,0:T(8,128)S(1)}, f32[128,128]{1,0:T(8,128)S(1)}) custom-call(bf16[128,3584]{1,0:T(8,128)(2,1)S(1)} %copy-done.1, bf16[128,3584]{1,0:T(8,128)(2,1)S(1)} %collective-permute-done.peer_tokens, bf16[64,3584]{1,0:T(8,128)(2,1)S(1)} %pad_maximum_fusion.refs_0_, bf16[32,3584]{1,0:T(8,128)(2,1)S(1)} %pad_maximum_fusion.1.refs_1_, ...), custom_call_target="tpu_custom_call" | custom-call | flops 234881024 | bytes 2752512 | tf_op jit(solution)/shard_map/half_logits/pallas_call | solution.py:173
  46.8 1.1 %collective-permute-done.11.refs_1_ = f32[128,128]{1,0:T(8,128)S(1)} collective-permute-done((f32[128,128]{1,0:T(8,128)S(1)}, f32[128,128]{1,0:T(8,128)S(1)}, u32[]{:S(2)}, u32[]{:S(2)}) %collective-permute-start.11) | collective-permute-done | bytes 65568 | tf_op jit(solution)/shard_map/ppermute | solution.py:17
  48.0 1.0 %router_terms.1 = (bf16[64,128]{1,0:T(8,128)(2,1)S(1)}, f32[1,128]{1,0:T(1,128)}) custom-call(s32[8,128]{1,0:T(8,128)S(1)} %bitcast.47, s32[8,128]{1,0:T(8,128)S(1)} %bitcast.48, s32[1,128]{1,0:T(1,128)S(1)} %bitcast.49, f32[256,128]{1,0:T(8,128)S(1)} %bitcast.46, f32[128,128]{1,0:T(8,128)S(1)} %get-tuple-element.44.refs_0_, ...), custom_call_target="tpu_custom_call" | custom-call | flops 983040 | bytes 393216 | tf_op jit(solution)/shard_map/router_terms/pallas_call | solution.py:226
  49.0 2.9 %all-to-all-done = bf16[8,8,3584]{2,1,0:T(8,128)(2,1)S(1)} async-done(((bf16[8,8,3584]{2,1,0:T(8,128)(2,1)}), bf16[8,8,3584]{2,1,0:T(8,128)(2,1)S(1)}, u32[]{:S(2)}, u32[]{:S(2)}) %all-to-all-start) | async-done | bytes 458784 | tf_op jit(solution)/shard_map/all_to_all | solution.py:297
  51.8 1.3 %convolution_convert_fusion = bf16[128,3584]{1,0:T(8,128)(2,1)} fusion(bf16[64,128]{1,0:T(8,128)(2,1)S(1)} %get-tuple-element.46, bf16[8,8,3584]{2,1,0:T(8,128)(2,1)S(1)} %all-to-all-done), kind=kOutput, calls=%fused_computation | convolution fusion | flops 59179008 | bytes 1392640 | tf_op jit(solution)/shard_map/dot_general | solution.py:32
  (48 shorter events, 1.8 us)
Async XLA Ops:
  0.6 0.9 %copy-start = (bf16[32,3584]{1,0:T(8,128)(2,1)S(1)}, bf16[32,3584]{1,0:T(8,128)(2,1)}, u32[]{:S(2)}) copy-start(bf16[32,3584]{1,0:T(8,128)(2,1)} %param.11) | copy-start | bytes 688132
  3.1 9.8 %collective-permute-start.4 = (bf16[16,3584]{1,0:T(8,128)(2,1)S(1)}, bf16[16,3584]{1,0:T(8,128)(2,1)S(1)}, u32[]{:S(2)}, u32[]{:S(2)}) collective-permute-start(bf16[16,3584]{1,0:T(8,128)(2,1)S(1)} %get-tuple-element.65), channel_id=1, source_target_pairs={{0,8},{2,10},{4,12},{6,14},{8,0},{10,2},{12,4},{14,6},{1,9},{3,11}... | collective-permute-start | bytes 344072 | tf_op jit(solution)/shard_map/ppermute | solution.py:22
  7.3 13.5 %collective-permute-start.1 = (bf16[24,3584]{1,0:T(8,128)(2,1)S(1)}, bf16[24,3584]{1,0:T(8,128)(2,1)S(1)}, u32[]{:S(2)}, u32[]{:S(2)}) collective-permute-start(bf16[24,3584]{1,0:T(8,128)(2,1)S(1)} %get-tuple-element.61), channel_id=1, source_target_pairs={{0,2},{2,0},{4,6},{6,4},{8,10},{10,8},{12,14},{14,12},{1,3},{3,1},... | collective-permute-start | bytes 516104 | tf_op jit(solution)/shard_map/ppermute | solution.py:22
  8.9 13.2 %collective-permute-start.2 = (bf16[24,3584]{1,0:T(8,128)(2,1)S(1)}, bf16[24,3584]{1,0:T(8,128)(2,1)S(1)}, u32[]{:S(2)}, u32[]{:S(2)}) collective-permute-start(bf16[24,3584]{1,0:T(8,128)(2,1)S(1)} %get-tuple-element.62), channel_id=1, source_target_pairs={{0,4},{2,6},{4,0},{6,2},{8,12},{10,14},{12,8},{14,10},{1,5},{3,7},... | collective-permute-start | bytes 516104 | tf_op jit(solution)/shard_map/ppermute | solution.py:22
  10.4 12.0 %collective-permute-start.3 = (bf16[24,3584]{1,0:T(8,128)(2,1)S(1)}, bf16[24,3584]{1,0:T(8,128)(2,1)S(1)}, u32[]{:S(2)}, u32[]{:S(2)}) collective-permute-start(bf16[24,3584]{1,0:T(8,128)(2,1)S(1)} %get-tuple-element.63), channel_id=1, source_target_pairs={{0,6},{2,4},{4,2},{6,0},{8,14},{10,12},{12,10},{14,8},{1,7},{3,5},... | collective-permute-start | bytes 516104 | tf_op jit(solution)/shard_map/ppermute | solution.py:22
  10.8 11.6 %collective-permute-start.5 = (bf16[16,3584]{1,0:T(8,128)(2,1)S(1)}, bf16[16,3584]{1,0:T(8,128)(2,1)S(1)}, u32[]{:S(2)}, u32[]{:S(2)}) collective-permute-start(bf16[16,3584]{1,0:T(8,128)(2,1)S(1)} %get-tuple-element.64), channel_id=1, source_target_pairs={{0,10},{2,8},{4,14},{6,12},{8,2},{10,0},{12,6},{14,4},{1,11},{3,9}... | collective-permute-start | bytes 344072 | tf_op jit(solution)/shard_map/ppermute | solution.py:22
  12.9 10.7 %collective-permute-start.6 = (bf16[8,3584]{1,0:T(8,128)(2,1)S(1)}, bf16[8,3584]{1,0:T(8,128)(2,1)S(1)}, u32[]{:S(2)}, u32[]{:S(2)}) collective-permute-start(bf16[8,3584]{1,0:T(8,128)(2,1)S(1)} %get-tuple-element.51), channel_id=1, source_target_pairs={{0,12},{2,14},{4,8},{6,10},{8,4},{10,6},{12,0},{14,2},{1,13},{3,15... | collective-permute-start | bytes 172040 | tf_op jit(solution)/shard_map/ppermute | solution.py:22
  16.6 13.6 %copy-start.4 = (s32[1,16]{1,0:T(1,128)S(1)}, s32[1,16]{1,0:T(1,128)}, u32[]{:S(2)}) copy-start(s32[1,16]{1,0:T(1,128)} %occupancy.1) | copy-start | bytes 196
  20.8 7.5 %collective-permute-start.7 = (bf16[8,3584]{1,0:T(8,128)(2,1)S(1)}, bf16[8,3584]{1,0:T(8,128)(2,1)S(1)}, u32[]{:S(2)}, u32[]{:S(2)}) collective-permute-start(bf16[8,3584]{1,0:T(8,128)(2,1)S(1)} %get-tuple-element.50), channel_id=1, source_target_pairs={{0,14},{2,12},{4,10},{6,8},{8,6},{10,4},{12,2},{14,0},{1,15},{3,13... | collective-permute-start | bytes 172040 | tf_op jit(solution)/shard_map/ppermute | solution.py:22
  22.5 5.9 %collective-permute-start.9 = (bf16[16,3584]{1,0:T(8,128)(2,1)S(1)}, bf16[16,3584]{1,0:T(8,128)(2,1)S(1)}, u32[]{:S(2)}, u32[]{:S(2)}) collective-permute-start(bf16[16,3584]{1,0:T(8,128)(2,1)S(1)} %pad_maximum_fusion.7), channel_id=1, source_target_pairs={{0,4},{2,6},{4,0},{6,2},{8,12},{10,14},{12,8},{14,10},{1,5},{3,7},... | collective-permute-start | bytes 344072 | tf_op jit(solution)/shard_map/ppermute | solution.py:22
  28.3 1.8 %collective-permute-start.8 = (bf16[64,3584]{1,0:T(8,128)(2,1)S(1)}, bf16[64,3584]{1,0:T(8,128)(2,1)S(1)}, u32[]{:S(2)}, u32[]{:S(2)}) collective-permute-start(bf16[64,3584]{1,0:T(8,128)(2,1)S(1)} %constant_dynamic-update-slice_fusion.own), channel_id=1, source_target_pairs={{0,1},{1,0},{2,3},{3,2},{4,5},{5,4},{6,7},{7,6},{8,9},{9,8},{10,11... | collective-permute-start | bytes 1376264 | tf_op jit(solution)/shard_map/ppermute | solution.py:17
  28.4 3.8 %copy-start.1 = (bf16[128,3584]{1,0:T(8,128)(2,1)S(1)}, bf16[128,3584]{1,0:T(8,128)(2,1)}, u32[]{:S(2)}) copy-start(bf16[128,3584]{1,0:T(8,128)(2,1)} %own_tokens.1) | copy-start | bytes 2752516
  32.0 14.8 %copy-start.6 = (f32[128,256]{1,0:T(8,128)S(1)}, f32[128,256]{1,0:T(8,128)}, u32[]{:S(2)}) copy-start(f32[128,256]{1,0:T(8,128)} %param.15) | copy-start | bytes 393220
  32.0 16.0 %copy-start.2 = (s32[128,8]{0,1:T(8,128)S(1)}, s32[128,8]{0,1:T(8,128)}, u32[]{:S(2)}) copy-start(s32[128,8]{0,1:T(8,128)} %param.16) | copy-start | bytes 12292
  32.0 16.0 %copy-start.3 = (s32[128,8]{0,1:T(8,128)S(1)}, s32[128,8]{0,1:T(8,128)}, u32[]{:S(2)}) copy-start(s32[128,8]{0,1:T(8,128)} %param.17) | copy-start | bytes 12292
  32.0 16.0 %copy-start.5 = (s32[128]{0:T(128)S(1)}, s32[128]{0:T(128)}, u32[]{:S(2)}) copy-start(s32[128]{0:T(128)} %param.19) | copy-start | bytes 1540
  32.0 1.9 %collective-permute-start.12 = (bf16[64,3584]{1,0:T(8,128)(2,1)S(1)}, bf16[64,3584]{1,0:T(8,128)(2,1)S(1)}, u32[]{:S(2)}, u32[]{:S(2)}) collective-permute-start(bf16[64,3584]{1,0:T(8,128)(2,1)S(1)} %get-tuple-element.48), channel_id=1, source_target_pairs={{0,1},{1,0},{2,3},{3,2},{4,5},{5,4},{6,7},{7,6},{8,9},{9,8},{10,11... | collective-permute-start | bytes 1376264 | tf_op jit(solution)/shard_map/ppermute | solution.py:17
  32.2 13.8 %collective-permute-start = (bf16[128,3584]{1,0:T(8,128)(2,1)S(1)}, bf16[128,3584]{1,0:T(8,128)(2,1)S(1)}, u32[]{:S(2)}, u32[]{:S(2)}) collective-permute-start(bf16[128,3584]{1,0:T(8,128)(2,1)S(1)} %copy-done.1), channel_id=1, source_target_pairs={{0,1},{1,0},{2,3},{3,2},{4,5},{5,4},{6,7},{7,6},{8,9},{9,8},{10,11... | collective-permute-start | bytes 2752520 | tf_op jit(solution)/shard_map/ppermute | solution.py:17
  34.8 17.1 %all-to-all-start = ((bf16[8,8,3584]{2,1,0:T(8,128)(2,1)}), bf16[8,8,3584]{2,1,0:T(8,128)(2,1)S(1)}, u32[]{:S(2)}, u32[]{:S(2)}) async-start(bf16[8,8,3584]{2,1,0:T(8,128)(2,1)} %add_halves.1), calls=%async_computation | async-start | bytes 917504 | tf_op jit(solution)/shard_map/all_to_all | solution.py:297
  38.3 7.7 %collective-permute-start.10 = (bf16[32,3584]{1,0:T(8,128)(2,1)S(1)}, bf16[32,3584]{1,0:T(8,128)(2,1)S(1)}, u32[]{:S(2)}, u32[]{:S(2)}) collective-permute-start(bf16[32,3584]{1,0:T(8,128)(2,1)S(1)} %pad_maximum_fusion.1.refs_1_), channel_id=1, source_target_pairs={{0,16},{16,0},{1,17},{17,1},{2,18},{18,2},{3,19},{19,3},{4,20},{20... | collective-permute-start | bytes 688136 | tf_op jit(solution)/shard_map/ppermute | solution.py:22
  46.6 1.3 %collective-permute-start.11 = (f32[128,128]{1,0:T(8,128)S(1)}, f32[128,128]{1,0:T(8,128)S(1)}, u32[]{:S(2)}, u32[]{:S(2)}) collective-permute-start(f32[128,128]{1,0:T(8,128)S(1)} %get-tuple-element.45), channel_id=1, source_target_pairs={{0,1},{1,0},{2,3},{3,2},{4,5},{5,4},{6,7},{7,6},{8,9},{9,8},{10,11... | collective-permute-start | bytes 196616 | tf_op jit(solution)/shard_map/ppermute | solution.py:17

commit v5 on v4

--- a/solution.py
+++ b/solution.py
@@ -265,35 +265,34 @@
         at, group = lax.axis_index("expert"), lax.axis_index("groups")
         mine = lax.dynamic_slice_in_dim(router_weight, core * 16, 16, axis=0)
         piece = lax.dynamic_slice_in_dim(router_weight, core * 16 + group * 8, 8, axis=0)
-        blocks, near = [lax.dynamic_index_in_dim(outgoing, at, 0, keepdims=False)], [mine]
-        far = []
+        blocks = {0: lax.dynamic_index_in_dim(outgoing, at, 0, keepdims=False)}
+        send = {}
         for d in range(1, 8):
             block = lax.dynamic_index_in_dim(outgoing, at ^ d, 0, keepdims=False)
-            if d < 6:
-                along = mine if d < 4 else piece
-                pair = across(jnp.concatenate([block, along], axis=0), "expert", d)
-                block = pair[:CAP]
-                (near if d < 4 else far).append(pair[CAP:])
-            else:
-                block = across(block, "expert", d)
-            blocks.append(block)
-        level_a = jnp.concatenate(near, axis=0)
-        level_b = jnp.concatenate(far, axis=0)
+            along = [mine] if d < 4 else [piece] if d < 6 else []
+            send[d] = jnp.concatenate([block] + along, axis=0)
+        for d, before in ((4, 0), (2, 0), (3, 0), (5, 0), (6, 0), (7, 4), (1, 2)):
+            if before:
+                blocks[before], send[d] = lax.optimization_barrier((blocks[before], send[d]))
+            blocks[d] = across(send[d], "expert", d)
+        level_a = jnp.concatenate([mine] + [blocks[d][CAP:] for d in (1, 2, 3)], axis=0)
         weights = (gate_weight, up_weight, down_weight)
         blocks[4], *weights = lax.optimization_barrier((blocks[4], *weights))
         held = load(*weights)
+        level_b = jnp.concatenate([blocks[d][CAP:] for d in (4, 5)], axis=0)
         level_b, *held = lax.optimization_barrier((level_b, *held))
         level_b = jnp.concatenate([level_b, across(level_b, "expert", 2)], axis=0)
-        arrived = jnp.concatenate(blocks, axis=0)
+        arrived = jnp.concatenate([blocks[d][:CAP] for d in range(8)], axis=0)
         arrived, *held = lax.optimization_barrier((arrived, *held))
     else:
         arrived = lax.all_to_all(outgoing, "expert", split_axis=0, concat_axis=0, tiled=True)
         arrived = arrived.reshape(width, model_width)
         held = (gate_weight, up_weight, down_weight)
     ours, theirs = ffn(staged, arrived, swap_cores(arrived), occupancy, *held)
+    other = swap_cores(theirs)
     if staged:
-        ours, theirs, level_b = lax.optimization_barrier((ours, theirs, level_b))
-    summed = add_halves(staged, ours, swap_cores(theirs))
+        other, level_b = lax.optimization_barrier((other, level_b))
+    summed = add_halves(staged, ours, other)
     returned = lax.all_to_all(summed, "expert", split_axis=0, concat_axis=0, tiled=True)
     if staged:
         next_b = across(level_b, "groups", 1)

time: 53.4 us -> 51.5 us (0.964)
  waiting for transfers between devices: 19 us -> 12.7 us
  starting transfers between devices: 20.7 us -> 24.1 us
  local copies, waits for them, and re-layouts: 0.35 us -> 1.25 us
    ppermute x9, waiting for transfers between devices: 11.9 us -> 7.79 us  [across(): return lax.ppermute(value, axis, [(s, s ^ distance) for s in range(size)])]
    ppermute x9, starting transfers between devices: 16.6 us -> 19.6 us  [across(): return lax.ppermute(value, axis, [(s, s ^ distance) for s in range(size)])]
    ppermute x4, waiting for transfers between devices: 4.2 us -> 1.97 us  [swap_cores(): return lax.ppermute(value, 'tensor', SWAP)]
    unnamed x21 -> x18, local copies, waits for them, and re-layouts: 0.23 us -> 1.13 us
  transfers between devices with their start and end apart: 14 -> 14, of which waited for: 8 -> 6; matrix products, arithmetic and copies ran while one was open for 1% -> 2% of each run, Pallas kernels for 13% -> 17%
where the time goes in v5:
time: 51.5 us; the launch traced here: 51.2 us
  starting transfers between devices  24.1 us (47%)
  waiting for transfers between devices  12.7 us (25%)
  Pallas kernels  8.5 us (17%)
  matrix products  2.8 us (5%)
  local copies, waits for them, and re-layouts  1.25 us (2%)
  between operations  1 us (2%)
  other arithmetic  0.89 us (2%)
    ppermute x9, starting transfers between devices, across(): return lax.ppermute(value, axis, [(s, s ^ distance) for s in range(size)])  19.6 us
    ppermute x9, waiting for transfers between devices, across(): return lax.ppermute(value, axis, [(s, s ^ distance) for s in range(size)])  7.79 us
    pallas_call x1, Pallas kernels, load(): pl.pallas_call(load_kernel, out_shape=tuple((jax.ShapeDtypeStruct(w.shape...  4.23 us
    all_to_all x1, starting transfers between devices, per_device(): lax.all_to_all(summed, 'expert', split_axis=0, concat_axis=0, tiled=True)  3.8 us
    all_to_all x1, waiting for transfers between devices, per_device(): lax.all_to_all(summed, 'expert', split_axis=0, concat_axis=0, tiled=True)  2.96 us
    ppermute x4, waiting for transfers between devices, swap_cores(): return lax.ppermute(value, 'tensor', SWAP)  1.97 us
    pallas_call x1, Pallas kernels, ffn(): pl.pallas_call(functools.partial(ffn_kernel, parts, relative), out_shape=...  1.8 us
    dot_general x1, matrix products, per_device(): jnp.dot(hits.astype(jnp.bfloat16), tokens, preferred_element_type=jnp.flo...  1.45 us
  transfers between devices with their start and end apart: 14, of which 6 were waited for; matrix products, arithmetic and copies ran while one was open for 2% of the time, Pallas kernels for 17%

profile of v5, /device:TPU:0, one launch (start us, length us, event | category | flops | bytes accessed | tf_op | source)
XLA Modules:
  0.0 51.2 jit_solution(4881804792331904854)
XLA Ops:
  0.7 0.8 %add_select_fusion = s32[8,128]{1,0:T(8,128)S(1)} fusion(s32[128,8]{0,1:T(8,128)} %param.17, s32[128,8]{0,1:T(8,128)} %param.16), kind=kLoop, calls=%fused_computation.50 | loop fusion | flops 6144 | bytes 12288 | tf_op jit(solution)/shard_map/jit(_where)/select_n | solution.py:48
  1.6 1.5 %fusion = bf16[8,8,3584]{2,1,0:T(8,128)(2,1)S(1)} fusion(bf16[128,3584]{1,0:T(8,128)(2,1)} %own_tokens.1, s32[128]{0:T(128)S(1)} %get-tuple-element.73, s32[128]{0:T(128)S(1)} %get-tuple-element.74, s32[128]{0:T(128)S(1)} %get-tuple-element.75, s32[128]{0:T(128)S(1)} %get-tuple-element.76, s32[128]{0:T(128)S(1)} %get-tuple-element.77, ...), kind=kOutput, calls=%fused_computation.2 | convolution fusion | flops 59072512 | bytes 1380352 | tf_op jit(solution)/shard_map/dot_general | solution.py:262
  3.1 3.1 %collective-permute-start.1 = (bf16[24,3584]{1,0:T(8,128)(2,1)S(1)}, bf16[24,3584]{1,0:T(8,128)(2,1)S(1)}, u32[]{:S(2)}, u32[]{:S(2)}) collective-permute-start(bf16[24,3584]{1,0:T(8,128)(2,1)S(1)} %get-tuple-element.69), channel_id=1, source_target_pairs={{0,4},{2,6},{4,0},{6,2},{8,12},{10,14},{12,8},{14,10},{1,5},{3,7},... | collective-permute-start | bytes 516104 | tf_op jit(solution)/shard_map/ppermute | solution.py:22
  6.3 2.7 %collective-permute-start.4 = (bf16[16,3584]{1,0:T(8,128)(2,1)S(1)}, bf16[16,3584]{1,0:T(8,128)(2,1)S(1)}, u32[]{:S(2)}, u32[]{:S(2)}) collective-permute-start(bf16[16,3584]{1,0:T(8,128)(2,1)S(1)} %get-tuple-element.71), channel_id=1, source_target_pairs={{0,8},{2,10},{4,12},{6,14},{8,0},{10,2},{12,4},{14,6},{1,9},{3,11}... | collective-permute-start | bytes 344072 | tf_op jit(solution)/shard_map/ppermute | solution.py:22
  8.9 1.4 %collective-permute-start.3 = (bf16[24,3584]{1,0:T(8,128)(2,1)S(1)}, bf16[24,3584]{1,0:T(8,128)(2,1)S(1)}, u32[]{:S(2)}, u32[]{:S(2)}) collective-permute-start(bf16[24,3584]{1,0:T(8,128)(2,1)S(1)} %get-tuple-element.68), channel_id=1, source_target_pairs={{0,6},{2,4},{4,2},{6,0},{8,14},{10,12},{12,10},{14,8},{1,7},{3,5},... | collective-permute-start | bytes 516104 | tf_op jit(solution)/shard_map/ppermute | solution.py:22
  10.3 3.9 %collective-permute-start.6 = (bf16[8,3584]{1,0:T(8,128)(2,1)S(1)}, bf16[8,3584]{1,0:T(8,128)(2,1)S(1)}, u32[]{:S(2)}, u32[]{:S(2)}) collective-permute-start(bf16[8,3584]{1,0:T(8,128)(2,1)S(1)} %get-tuple-element.56), channel_id=1, source_target_pairs={{0,12},{2,14},{4,8},{6,10},{8,4},{10,6},{12,0},{14,2},{1,13},{3,15... | collective-permute-start | bytes 172040 | tf_op jit(solution)/shard_map/ppermute | solution.py:22
  14.2 0.7 %collective-permute-done.1 = bf16[24,3584]{1,0:T(8,128)(2,1)S(1)} collective-permute-done((bf16[24,3584]{1,0:T(8,128)(2,1)S(1)}, bf16[24,3584]{1,0:T(8,128)(2,1)S(1)}, u32[]{:S(2)}, u32[]{:S(2)}) %collective-permute-start.1) | collective-permute-done | bytes 172064 | tf_op jit(solution)/shard_map/ppermute | solution.py:22
  14.9 2.5 %collective-permute-start.2 = (bf16[24,3584]{1,0:T(8,128)(2,1)S(1)}, bf16[24,3584]{1,0:T(8,128)(2,1)S(1)}, u32[]{:S(2)}, u32[]{:S(2)}) collective-permute-start(bf16[24,3584]{1,0:T(8,128)(2,1)S(1)} %get-tuple-element.29), channel_id=1, source_target_pairs={{0,2},{2,0},{4,6},{6,4},{8,10},{10,8},{12,14},{14,12},{1,3},{3,1},... | collective-permute-start | bytes 516104 | tf_op jit(solution)/shard_map/ppermute | solution.py:22
  17.4 4.4 %collective-permute-start.7 = (bf16[8,3584]{1,0:T(8,128)(2,1)S(1)}, bf16[8,3584]{1,0:T(8,128)(2,1)S(1)}, u32[]{:S(2)}, u32[]{:S(2)}) collective-permute-start(bf16[8,3584]{1,0:T(8,128)(2,1)S(1)} %get-tuple-element.33), channel_id=1, source_target_pairs={{0,14},{2,12},{4,10},{6,8},{8,6},{10,4},{12,2},{14,0},{1,15},{3,13... | collective-permute-start | bytes 172040 | tf_op jit(solution)/shard_map/ppermute | solution.py:22
  21.8 4.2 %load.1 = (bf16[1,3584,512]{2,1,0:T(8,128)(2,1)S(1)}, bf16[1,3584,512]{2,1,0:T(8,128)(2,1)S(1)}, bf16[1,512,3584]{2,1,0:T(8,128)(2,1)S(1)}) custom-call(bf16[1,3584,512]{2,1,0:T(8,128)(2,1)} %refs_0_, bf16[1,3584,512]{2,1,0:T(8,128)(2,1)} %refs_1_, bf16[1,512,3584]{2,1,0:T(8,128)(2,1)} %refs_2_), custom_call_target="tpu_custom_call" | custom-call | bytes 11010048 | tf_op jit(solution)/shard_map/load/pallas_call | solution.py:70
  26.4 1.7 %collective-permute-done.8.peer = bf16[64,3584]{1,0:T(8,128)(2,1)S(1)} collective-permute-done((bf16[64,3584]{1,0:T(8,128)(2,1)S(1)}, bf16[64,3584]{1,0:T(8,128)(2,1)S(1)}, u32[]{:S(2)}, u32[]{:S(2)}) %collective-permute-start.8) | collective-permute-done | bytes 458784 | tf_op jit(solution)/shard_map/ppermute | solution.py:17
  28.1 1.8 %ffn.1 = (bf16[64,3584]{1,0:T(8,128)(2,1)S(1)}, bf16[64,3584]{1,0:T(8,128)(2,1)S(1)}) custom-call(bf16[64,3584]{1,0:T(8,128)(2,1)S(1)} %constant_dynamic-update-slice_fusion.own, bf16[64,3584]{1,0:T(8,128)(2,1)S(1)} %collective-permute-done.8.peer, s32[1,16]{1,0:T(1,128)S(1)} %copy-done.4, bf16[1,3584,512]{2,1,0:T(8,128)(2,1)S(1)} %get-tuple-element.44.gate, ...), custom_call_target="tpu_custom_call" | custom-call | flops 1409286144 | bytes 11010048 | tf_op jit(solution)/shard_map/ffn/pallas_call | solution.py:121
  30.2 0.4 collective-permute-start
  30.5 1.3 %collective-permute-done.10 = bf16[16,3584]{1,0:T(8,128)(2,1)S(1)} collective-permute-done((bf16[16,3584]{1,0:T(8,128)(2,1)S(1)}, bf16[16,3584]{1,0:T(8,128)(2,1)S(1)}, u32[]{:S(2)}, u32[]{:S(2)}) %collective-permute-start.10) | collective-permute-done | bytes 114720 | tf_op jit(solution)/shard_map/ppermute | solution.py:22
  31.9 0.9 %add_halves.1 = bf16[8,8,3584]{2,1,0:T(8,128)(2,1)} custom-call(bf16[64,3584]{1,0:T(8,128)(2,1)S(1)} %get-tuple-element.53.ours, bf16[64,3584]{1,0:T(8,128)(2,1)S(1)} %collective-permute-done.9.other), custom_call_target="tpu_custom_call" | custom-call | flops 229376 | bytes 1376256 | tf_op jit(solution)/shard_map/add_halves/pallas_call | solution.py:141
  32.8 3.8 %all-to-all-start = ((bf16[8,8,3584]{2,1,0:T(8,128)(2,1)}), bf16[8,8,3584]{2,1,0:T(8,128)(2,1)S(1)}, u32[]{:S(2)}, u32[]{:S(2)}) async-start(bf16[8,8,3584]{2,1,0:T(8,128)(2,1)} %add_halves.1), calls=%async_computation | async-start | bytes 917504 | tf_op jit(solution)/shard_map/all_to_all | solution.py:296
  36.6 1.5 %collective-permute-start.11 = (bf16[32,3584]{1,0:T(8,128)(2,1)S(1)}, bf16[32,3584]{1,0:T(8,128)(2,1)S(1)}, u32[]{:S(2)}, u32[]{:S(2)}) collective-permute-start(bf16[32,3584]{1,0:T(8,128)(2,1)S(1)} %pad_maximum_fusion.1.refs_1_), channel_id=1, source_target_pairs={{0,16},{16,0},{1,17},{17,1},{2,18},{18,2},{3,19},{19,3},{4,20},{20... | collective-permute-start | bytes 688136 | tf_op jit(solution)/shard_map/ppermute | solution.py:22
  38.2 5.8 %collective-permute-done.11.refs_2_ = bf16[32,3584]{1,0:T(8,128)(2,1)S(1)} collective-permute-done((bf16[32,3584]{1,0:T(8,128)(2,1)S(1)}, bf16[32,3584]{1,0:T(8,128)(2,1)S(1)}, u32[]{:S(2)}, u32[]{:S(2)}) %collective-permute-start.11) | collective-permute-done | bytes 229408 | tf_op jit(solution)/shard_map/ppermute | solution.py:22
  44.0 0.6 %half_logits.1 = (f32[128,128]{1,0:T(8,128)S(1)}, f32[128,128]{1,0:T(8,128)S(1)}) custom-call(bf16[128,3584]{1,0:T(8,128)(2,1)S(1)} %copy-done.1, bf16[128,3584]{1,0:T(8,128)(2,1)S(1)} %collective-permute-done.peer_tokens, bf16[64,3584]{1,0:T(8,128)(2,1)S(1)} %pad_maximum_fusion.refs_0_, bf16[32,3584]{1,0:T(8,128)(2,1)S(1)} %pad_maximum_fusion.1.refs_1_, ...), custom_call_target="tpu_custom_call" | custom-call | flops 234881024 | bytes 2752512 | tf_op jit(solution)/shard_map/half_logits/pallas_call | solution.py:173
  44.7 1.0 %copy.12 = f32[128,256]{0,1:T(8,128)S(1)} copy(f32[128,256]{1,0:T(8,128)} %param.15) | data formatting | bytes 262144 | tf_op args[5]
  45.7 0.2 collective-permute-done.12.refs_1_
  46.0 1.0 %router_terms.1 = (bf16[64,128]{1,0:T(8,128)(2,1)S(1)}, f32[1,128]{1,0:T(1,128)}) custom-call(s32[8,128]{1,0:T(8,128)S(1)} %bitcast.47, s32[8,128]{1,0:T(8,128)S(1)} %bitcast.48, s32[1,128]{1,0:T(1,128)S(1)} %bitcast.49, f32[256,128]{1,0:T(8,128)S(1)} %bitcast.46, f32[128,128]{1,0:T(8,128)S(1)} %get-tuple-element.50.refs_0_, ...), custom_call_target="tpu_custom_call" | custom-call | flops 983040 | bytes 393216 | tf_op jit(solution)/shard_map/router_terms/pallas_call | solution.py:226
  46.9 3.0 %all-to-all-done = bf16[8,8,3584]{2,1,0:T(8,128)(2,1)S(1)} async-done(((bf16[8,8,3584]{2,1,0:T(8,128)(2,1)}), bf16[8,8,3584]{2,1,0:T(8,128)(2,1)S(1)}, u32[]{:S(2)}, u32[]{:S(2)}) %all-to-all-start) | async-done | bytes 458784 | tf_op jit(solution)/shard_map/all_to_all | solution.py:296
  49.9 1.3 %convolution_convert_fusion = bf16[128,3584]{1,0:T(8,128)(2,1)} fusion(bf16[64,128]{1,0:T(8,128)(2,1)S(1)} %get-tuple-element.52, bf16[8,8,3584]{2,1,0:T(8,128)(2,1)S(1)} %all-to-all-done), kind=kOutput, calls=%fused_computation | convolution fusion | flops 59179008 | bytes 1392640 | tf_op jit(solution)/shard_map/dot_general | solution.py:32
  (45 shorter events, 0.8 us)
Async XLA Ops:
  0.6 0.9 %copy-start = (bf16[32,3584]{1,0:T(8,128)(2,1)S(1)}, bf16[32,3584]{1,0:T(8,128)(2,1)}, u32[]{:S(2)}) copy-start(bf16[32,3584]{1,0:T(8,128)(2,1)} %param.11) | copy-start | bytes 688132
  3.1 11.7 %collective-permute-start.1 = (bf16[24,3584]{1,0:T(8,128)(2,1)S(1)}, bf16[24,3584]{1,0:T(8,128)(2,1)S(1)}, u32[]{:S(2)}, u32[]{:S(2)}) collective-permute-start(bf16[24,3584]{1,0:T(8,128)(2,1)S(1)} %get-tuple-element.69), channel_id=1, source_target_pairs={{0,4},{2,6},{4,0},{6,2},{8,12},{10,14},{12,8},{14,10},{1,5},{3,7},... | collective-permute-start | bytes 516104 | tf_op jit(solution)/shard_map/ppermute | solution.py:22
  6.3 11.1 %collective-permute-start.4 = (bf16[16,3584]{1,0:T(8,128)(2,1)S(1)}, bf16[16,3584]{1,0:T(8,128)(2,1)S(1)}, u32[]{:S(2)}, u32[]{:S(2)}) collective-permute-start(bf16[16,3584]{1,0:T(8,128)(2,1)S(1)} %get-tuple-element.71), channel_id=1, source_target_pairs={{0,8},{2,10},{4,12},{6,14},{8,0},{10,2},{12,4},{14,6},{1,9},{3,11}... | collective-permute-start | bytes 344072 | tf_op jit(solution)/shard_map/ppermute | solution.py:22
  8.9 17.2 %collective-permute-start.3 = (bf16[24,3584]{1,0:T(8,128)(2,1)S(1)}, bf16[24,3584]{1,0:T(8,128)(2,1)S(1)}, u32[]{:S(2)}, u32[]{:S(2)}) collective-permute-start(bf16[24,3584]{1,0:T(8,128)(2,1)S(1)} %get-tuple-element.68), channel_id=1, source_target_pairs={{0,6},{2,4},{4,2},{6,0},{8,14},{10,12},{12,10},{14,8},{1,7},{3,5},... | collective-permute-start | bytes 516104 | tf_op jit(solution)/shard_map/ppermute | solution.py:22
  10.3 15.8 %collective-permute-start.5 = (bf16[16,3584]{1,0:T(8,128)(2,1)S(1)}, bf16[16,3584]{1,0:T(8,128)(2,1)S(1)}, u32[]{:S(2)}, u32[]{:S(2)}) collective-permute-start(bf16[16,3584]{1,0:T(8,128)(2,1)S(1)} %get-tuple-element.70), channel_id=1, source_target_pairs={{0,10},{2,8},{4,14},{6,12},{8,2},{10,0},{12,6},{14,4},{1,11},{3,9}... | collective-permute-start | bytes 344072 | tf_op jit(solution)/shard_map/ppermute | solution.py:22
  10.3 15.8 %collective-permute-start.6 = (bf16[8,3584]{1,0:T(8,128)(2,1)S(1)}, bf16[8,3584]{1,0:T(8,128)(2,1)S(1)}, u32[]{:S(2)}, u32[]{:S(2)}) collective-permute-start(bf16[8,3584]{1,0:T(8,128)(2,1)S(1)} %get-tuple-element.56), channel_id=1, source_target_pairs={{0,12},{2,14},{4,8},{6,10},{8,4},{10,6},{12,0},{14,2},{1,13},{3,15... | collective-permute-start | bytes 172040 | tf_op jit(solution)/shard_map/ppermute | solution.py:22
  14.9 11.2 %collective-permute-start.2 = (bf16[24,3584]{1,0:T(8,128)(2,1)S(1)}, bf16[24,3584]{1,0:T(8,128)(2,1)S(1)}, u32[]{:S(2)}, u32[]{:S(2)}) collective-permute-start(bf16[24,3584]{1,0:T(8,128)(2,1)S(1)} %get-tuple-element.29), channel_id=1, source_target_pairs={{0,2},{2,0},{4,6},{6,4},{8,10},{10,8},{12,14},{14,12},{1,3},{3,1},... | collective-permute-start | bytes 516104 | tf_op jit(solution)/shard_map/ppermute | solution.py:22
  17.4 10.8 %copy-start.4 = (s32[1,16]{1,0:T(1,128)S(1)}, s32[1,16]{1,0:T(1,128)}, u32[]{:S(2)}) copy-start(s32[1,16]{1,0:T(1,128)} %occupancy.1) | copy-start | bytes 196
  17.4 8.8 %collective-permute-start.7 = (bf16[8,3584]{1,0:T(8,128)(2,1)S(1)}, bf16[8,3584]{1,0:T(8,128)(2,1)S(1)}, u32[]{:S(2)}, u32[]{:S(2)}) collective-permute-start(bf16[8,3584]{1,0:T(8,128)(2,1)S(1)} %get-tuple-element.33), channel_id=1, source_target_pairs={{0,14},{2,12},{4,10},{6,8},{8,6},{10,4},{12,2},{14,0},{1,15},{3,13... | collective-permute-start | bytes 172040 | tf_op jit(solution)/shard_map/ppermute | solution.py:22
  26.2 3.9 %copy-start.1 = (bf16[128,3584]{1,0:T(8,128)(2,1)S(1)}, bf16[128,3584]{1,0:T(8,128)(2,1)}, u32[]{:S(2)}) copy-start(bf16[128,3584]{1,0:T(8,128)(2,1)} %own_tokens.1) | copy-start | bytes 2752516
  26.2 1.9 %collective-permute-start.8 = (bf16[64,3584]{1,0:T(8,128)(2,1)S(1)}, bf16[64,3584]{1,0:T(8,128)(2,1)S(1)}, u32[]{:S(2)}, u32[]{:S(2)}) collective-permute-start(bf16[64,3584]{1,0:T(8,128)(2,1)S(1)} %constant_dynamic-update-slice_fusion.own), channel_id=1, source_target_pairs={{0,1},{1,0},{2,3},{3,2},{4,5},{5,4},{6,7},{7,6},{8,9},{9,8},{10,11... | collective-permute-start | bytes 1376264 | tf_op jit(solution)/shard_map/ppermute | solution.py:17
  26.3 5.6 %collective-permute-start.10 = (bf16[16,3584]{1,0:T(8,128)(2,1)S(1)}, bf16[16,3584]{1,0:T(8,128)(2,1)S(1)}, u32[]{:S(2)}, u32[]{:S(2)}) collective-permute-start(bf16[16,3584]{1,0:T(8,128)(2,1)S(1)} %pad_maximum_fusion.7), channel_id=1, source_target_pairs={{0,4},{2,6},{4,0},{6,2},{8,12},{10,14},{12,8},{14,10},{1,5},{3,7},... | collective-permute-start | bytes 344072 | tf_op jit(solution)/shard_map/ppermute | solution.py:22
  29.9 16.0 %copy-start.2 = (s32[128,8]{0,1:T(8,128)S(1)}, s32[128,8]{0,1:T(8,128)}, u32[]{:S(2)}) copy-start(s32[128,8]{0,1:T(8,128)} %param.16) | copy-start | bytes 12292
  29.9 16.0 %copy-start.3 = (s32[128,8]{0,1:T(8,128)S(1)}, s32[128,8]{0,1:T(8,128)}, u32[]{:S(2)}) copy-start(s32[128,8]{0,1:T(8,128)} %param.17) | copy-start | bytes 12292
  29.9 16.0 %copy-start.5 = (s32[128]{0:T(128)S(1)}, s32[128]{0:T(128)}, u32[]{:S(2)}) copy-start(s32[128]{0:T(128)} %param.19) | copy-start | bytes 1540
  30.0 1.9 %collective-permute-start.9 = (bf16[64,3584]{1,0:T(8,128)(2,1)S(1)}, bf16[64,3584]{1,0:T(8,128)(2,1)S(1)}, u32[]{:S(2)}, u32[]{:S(2)}) collective-permute-start(bf16[64,3584]{1,0:T(8,128)(2,1)S(1)} %get-tuple-element.47), channel_id=1, source_target_pairs={{0,1},{1,0},{2,3},{3,2},{4,5},{5,4},{6,7},{7,6},{8,9},{9,8},{10,11... | collective-permute-start | bytes 1376264 | tf_op jit(solution)/shard_map/ppermute | solution.py:17
  30.2 8.0 %collective-permute-start = (bf16[128,3584]{1,0:T(8,128)(2,1)S(1)}, bf16[128,3584]{1,0:T(8,128)(2,1)S(1)}, u32[]{:S(2)}, u32[]{:S(2)}) collective-permute-start(bf16[128,3584]{1,0:T(8,128)(2,1)S(1)} %copy-done.1), channel_id=1, source_target_pairs={{0,1},{1,0},{2,3},{3,2},{4,5},{5,4},{6,7},{7,6},{8,9},{9,8},{10,11... | collective-permute-start | bytes 2752520 | tf_op jit(solution)/shard_map/ppermute | solution.py:17
  32.8 17.1 %all-to-all-start = ((bf16[8,8,3584]{2,1,0:T(8,128)(2,1)}), bf16[8,8,3584]{2,1,0:T(8,128)(2,1)S(1)}, u32[]{:S(2)}, u32[]{:S(2)}) async-start(bf16[8,8,3584]{2,1,0:T(8,128)(2,1)} %add_halves.1), calls=%async_computation | async-start | bytes 917504 | tf_op jit(solution)/shard_map/all_to_all | solution.py:296
  36.6 7.4 %collective-permute-start.11 = (bf16[32,3584]{1,0:T(8,128)(2,1)S(1)}, bf16[32,3584]{1,0:T(8,128)(2,1)S(1)}, u32[]{:S(2)}, u32[]{:S(2)}) collective-permute-start(bf16[32,3584]{1,0:T(8,128)(2,1)S(1)} %pad_maximum_fusion.1.refs_1_), channel_id=1, source_target_pairs={{0,16},{16,0},{1,17},{17,1},{2,18},{18,2},{3,19},{19,3},{4,20},{20... | collective-permute-start | bytes 688136 | tf_op jit(solution)/shard_map/ppermute | solution.py:22
  44.6 1.3 %collective-permute-start.12 = (f32[128,128]{1,0:T(8,128)S(1)}, f32[128,128]{1,0:T(8,128)S(1)}, u32[]{:S(2)}, u32[]{:S(2)}) collective-permute-start(f32[128,128]{1,0:T(8,128)S(1)} %get-tuple-element.51), channel_id=1, source_target_pairs={{0,1},{1,0},{2,3},{3,2},{4,5},{5,4},{6,7},{7,6},{8,9},{9,8},{10,11... | collective-permute-start | bytes 196616 | tf_op jit(solution)/shard_map/ppermute | solution.py:17

commit v6 on v5

--- a/solution.py
+++ b/solution.py
@@ -25,12 +25,6 @@
 def dot_rows(left, right):
     return lax.dot_general(
         left, right, (((1,), (1,)), ((), ())), preferred_element_type=jnp.float32
-    )
-
-
-def dot_columns(left, right):
-    return lax.dot_general(
-        left, right, (((0,), (0,)), ((), ())), preferred_element_type=jnp.float32
     )
 
 
@@ -129,20 +123,32 @@
     )(own, peer, occupancy, gate, up, down)
 
 
-def add_kernel(relative, ours, other, out):
+def add_kernel(relative, ours, other, out, here, sems):
     value = ours[...].astype(jnp.float32) + other[...].astype(jnp.float32)
     order = lax.axis_index("expert") if relative else 0
+    copies = []
     for block in range(out.shape[0]):
-        out[block ^ order] = value[block * CAP : (block + 1) * CAP].astype(out.dtype)
+        here[block] = value[block * CAP : (block + 1) * CAP].astype(here.dtype)
+        copies.append(
+            pltpu.make_async_copy(here.at[block], out.at[block ^ order], sems.at[block])
+        )
+        copies[block].start()
+    for copy in copies:
+        copy.wait()
 
 
 def add_halves(relative, ours, other):
     rows, model_width = ours.shape
+    shape = (rows // CAP, CAP, model_width)
     return pl.pallas_call(
         functools.partial(add_kernel, relative),
-        out_shape=jax.ShapeDtypeStruct((rows // CAP, CAP, model_width), ours.dtype),
+        out_shape=jax.ShapeDtypeStruct(shape, ours.dtype),
         in_specs=[WHOLE] * 2,
-        out_specs=WHOLE,
+        out_specs=LEFT,
+        scratch_shapes=[
+            pltpu.VMEM(shape, ours.dtype),
+            pltpu.SemaphoreType.DMA((rows // CAP,)),
+        ],
         compiler_params=params(16),
         cost_estimate=cost(ours.size, 6 * ours.size),
         name="add_halves",
@@ -153,14 +159,14 @@
     levels, (out_own, out_peer) = refs[:-2], refs[-2:]
     expert, group = lax.axis_index("expert"), lax.axis_index("groups")
     rows = jnp.concatenate([level[...] for level in levels], axis=0)
-    places = [(expert ^ d) * 16 for d in range(4)]
+    places = [(expert ^ d) * 16 for d in (0, 2, 3)]
     for side in range(2):
-        places += [(expert ^ d) * 16 + (group ^ side) * 8 for d in range(4, 8)]
+        places += [(expert ^ d) * 16 + (group ^ side) * 8 for d in (1, 4, 5, 6, 7)]
     for tokens, out in ((own_tokens, out_own), (peer_tokens, out_peer)):
         value = dot_rows(rows, tokens[...])
         first = 0
         for n, place in enumerate(places):
-            count = 16 if n < 4 else 8
+            count = 16 if n < 3 else 8
             at = pl.ds(pl.multiple_of(place, 8), count)
             out[at, :] = value[first : first + count]
             first += count
@@ -199,7 +205,7 @@
                 whole[pl.ds(at, 16), :] = part[block * 16 : (block + 1) * 16]
         logits = whole[...]
     experts, tokens = logits.shape
-    width = weights.shape[0]
+    width = weights.shape[1]
     window = width // CAP
     scores = 1.0 / (1.0 + jnp.exp(-logits))
     names = lax.broadcasted_iota(jnp.int32, (experts, tokens), 0)
@@ -211,7 +217,7 @@
     shares = (2.5 * scores[:window] / total).astype(jnp.bfloat16).astype(jnp.float32)
     spread = jnp.broadcast_to(shares[:, None, :], (window, CAP, tokens)).reshape(width, tokens)
     hits = buffer_hits(choices, slots[...], width)
-    weights[...] = jnp.where(hits, spread, 0.0).astype(jnp.bfloat16)
+    weights[...] = jnp.where(hits, spread, 0.0).T.astype(jnp.bfloat16)
     log_p = log_sigmoid(logits) - jnp.log(jnp.sum(scores, axis=0, keepdims=True))
     q = policy[...]
     policy_scores = 1.0 / (1.0 + jnp.exp(-q))
@@ -226,7 +232,7 @@
     return pl.pallas_call(
         functools.partial(terms_kernel, len(parts)),
         out_shape=(
-            jax.ShapeDtypeStruct((width, tokens), jnp.bfloat16),
+            jax.ShapeDtypeStruct((tokens, width), jnp.bfloat16),
             jax.ShapeDtypeStruct((1, tokens), jnp.float32),
         ),
         in_specs=[WHOLE] * (4 + len(parts)),
@@ -236,6 +242,38 @@
         cost_estimate=cost(30 * experts * tokens, 12 * experts * tokens),
         name="router_terms",
     )(ids, slots, mask, policy, *parts)
+
+
+def combine_kernel(parts, weights, returned, out, here, sems):
+    wide = returned.shape[1] // parts
+    copies = []
+    for part in range(parts):
+        at = pl.ds(part * wide, wide)
+        value = jnp.dot(weights[...], returned[:, at], preferred_element_type=jnp.float32)
+        here[:, at] = value.astype(here.dtype)
+        copies.append(pltpu.make_async_copy(here.at[:, at], out.at[:, at], sems.at[part]))
+        copies[part].start()
+    for copy in copies:
+        copy.wait()
+
+
+def combine(weights, returned):
+    tokens, width = weights.shape
+    model_width = returned.shape[1]
+    parts = 4 if model_width % 512 == 0 else 1
+    return pl.pallas_call(
+        functools.partial(combine_kernel, parts),
+        out_shape=jax.ShapeDtypeStruct((tokens, model_width), returned.dtype),
+        in_specs=[WHOLE] * 2,
+        out_specs=LEFT,
+        scratch_shapes=[
+            pltpu.VMEM((tokens, model_width), returned.dtype),
+            pltpu.SemaphoreType.DMA((parts,)),
+        ],
+        compiler_params=params(16),
+        cost_estimate=cost(2 * tokens * width * model_width, 2 * tokens * model_width),
+        name="combine",
+    )(weights, returned)
 
 
 def per_device(
@@ -269,19 +307,23 @@
         send = {}
         for d in range(1, 8):
             block = lax.dynamic_index_in_dim(outgoing, at ^ d, 0, keepdims=False)
-            along = [mine] if d < 4 else [piece] if d < 6 else []
+            along = [mine] if d in (2, 3) else [piece] if d < 5 else []
             send[d] = jnp.concatenate([block] + along, axis=0)
-        for d, before in ((4, 0), (2, 0), (3, 0), (5, 0), (6, 0), (7, 4), (1, 2)):
+        for d, before in ((4, 0), (2, 0), (3, 0), (6, 0), (7, 0), (5, 4), (1, 2)):
             if before:
                 blocks[before], send[d] = lax.optimization_barrier((blocks[before], send[d]))
+            if d == 1:
+                send[d] = jnp.concatenate([send[d], blocks[4][CAP:]], axis=0)
             blocks[d] = across(send[d], "expert", d)
-        level_a = jnp.concatenate([mine] + [blocks[d][CAP:] for d in (1, 2, 3)], axis=0)
+        level_a = jnp.concatenate([mine] + [blocks[d][CAP : CAP + 16] for d in (2, 3)], axis=0)
         weights = (gate_weight, up_weight, down_weight)
         blocks[4], *weights = lax.optimization_barrier((blocks[4], *weights))
         held = load(*weights)
-        level_b = jnp.concatenate([blocks[d][CAP:] for d in (4, 5)], axis=0)
+        level_b = jnp.concatenate([blocks[4][CAP:], blocks[1][2 * CAP :]], axis=0)
         level_b, *held = lax.optimization_barrier((level_b, *held))
-        level_b = jnp.concatenate([level_b, across(level_b, "expert", 2)], axis=0)
+        level_b = jnp.concatenate(
+            [blocks[1][CAP : 2 * CAP], level_b, across(level_b, "expert", 2)], axis=0
+        )
         arrived = jnp.concatenate([blocks[d][:CAP] for d in range(8)], axis=0)
         arrived, *held = lax.optimization_barrier((arrived, *held))
     else:
@@ -304,8 +346,7 @@
     weights, kl_terms = router_terms(
         ids, slots, env_mask[None, :], policy_logits.T, parts, width
     )
-    mixed = dot_columns(weights, returned.reshape(width, model_width)).astype(jnp.bfloat16)
-    return (mixed, kl_terms[0])
+    return (combine(weights, returned.reshape(width, model_width)), kl_terms[0])
 
 
 def solution(mesh):

time: 51.5 us -> 50.1 us (0.973)
  matrix products: 2.8 us -> 1.45 us
  Pallas kernels: 8.5 us -> 9.64 us
  starting transfers between devices: 24.1 us -> 23.1 us
  local copies, waits for them, and re-layouts: 1.25 us -> 0.34 us
  waiting for transfers between devices: 12.7 us -> 13.5 us
    ppermute x9, waiting for transfers between devices: 7.79 us -> 9.84 us  [across(): return lax.ppermute(value, axis, [(s, s ^ distance) for s in range(size)])]
    ppermute x9, starting transfers between devices: 19.6 us -> 17.8 us  [across(): return lax.ppermute(value, axis, [(s, s ^ distance) for s in range(size)])]
    dot_general x1 -> x0, matrix products: 1.35 us -> none  [dot_columns(): lax.dot_general(left, right, (((0,), (0,)), ((), ())), preferred_element_...]
    all_to_all x1, waiting for transfers between devices: 2.96 us -> 1.73 us  [per_device(): lax.all_to_all(summed, 'expert', split_axis=0, concat_axis=0, tiled=True)]
    pallas_call x0 -> x1, Pallas kernels: none -> 1.15 us  [combine(): pl.pallas_call(functools.partial(combine_kernel, parts), out_shape=jax.Sh...]
    unnamed x18 -> x20, local copies, waits for them, and re-layouts: 1.13 us -> 0.23 us
    all_to_all x1, starting transfers between devices: 3.8 us -> 4.58 us  [per_device(): lax.all_to_all(summed, 'expert', split_axis=0, concat_axis=0, tiled=True)]
  transfers between devices with their start and end apart: 14 -> 14, of which waited for: 6 -> 7; matrix products, arithmetic and copies ran while one was open for 2% -> 0% of each run, Pallas kernels for 17% -> 17%
where the time goes in v6:
time: 50.1 us; the launch traced here: 49.9 us
  starting transfers between devices  23.1 us (46%)
  waiting for transfers between devices  13.5 us (27%)
  Pallas kernels  9.64 us (19%)
  matrix products  1.45 us (3%)
  between operations  0.99 us (2%)
  other arithmetic  0.89 us (2%)
    ppermute x9, starting transfers between devices, across(): return lax.ppermute(value, axis, [(s, s ^ distance) for s in range(size)])  17.8 us
    ppermute x9, waiting for transfers between devices, across(): return lax.ppermute(value, axis, [(s, s ^ distance) for s in range(size)])  9.84 us
    all_to_all x1, starting transfers between devices, per_device(): lax.all_to_all(summed, 'expert', split_axis=0, concat_axis=0, tiled=True)  4.58 us
    pallas_call x1, Pallas kernels, load(): pl.pallas_call(load_kernel, out_shape=tuple((jax.ShapeDtypeStruct(w.shape...  4.23 us
    ppermute x4, waiting for transfers between devices, swap_cores(): return lax.ppermute(value, 'tensor', SWAP)  1.91 us
    pallas_call x1, Pallas kernels, ffn(): pl.pallas_call(functools.partial(ffn_kernel, parts, relative), out_shape=...  1.8 us
    all_to_all x1, waiting for transfers between devices, per_device(): lax.all_to_all(summed, 'expert', split_axis=0, concat_axis=0, tiled=True)  1.73 us
    dot_general x1, matrix products, per_device(): jnp.dot(hits.astype(jnp.bfloat16), tokens, preferred_element_type=jnp.flo...  1.45 us
  transfers between devices with their start and end apart: 14, of which 7 were waited for; matrix products, arithmetic and copies ran while one was open for 0% of the time, Pallas kernels for 17%

profile of v6, /device:TPU:0, one launch (start us, length us, event | category | flops | bytes accessed | tf_op | source)
XLA Modules:
  0.0 49.9 jit_solution(9841315068832761255)
XLA Ops:
  0.7 0.8 %add_select_fusion = s32[8,128]{1,0:T(8,128)S(1)} fusion(s32[128,8]{0,1:T(8,128)} %param.17, s32[128,8]{0,1:T(8,128)} %param.16), kind=kLoop, calls=%fused_computation.48 | loop fusion | flops 6144 | bytes 12288 | tf_op jit(solution)/shard_map/jit(_where)/select_n | solution.py:42
  1.6 1.5 %fusion = bf16[8,8,3584]{2,1,0:T(8,128)(2,1)S(1)} fusion(bf16[128,3584]{1,0:T(8,128)(2,1)} %own_tokens.1, s32[128]{0:T(128)S(1)} %get-tuple-element.73, s32[128]{0:T(128)S(1)} %get-tuple-element.74, s32[128]{0:T(128)S(1)} %get-tuple-element.75, s32[128]{0:T(128)S(1)} %get-tuple-element.76, s32[128]{0:T(128)S(1)} %get-tuple-element.77, ...), kind=kOutput, calls=%fused_computation.1 | convolution fusion | flops 59072512 | bytes 1380352 | tf_op jit(solution)/shard_map/dot_general | solution.py:300
  3.1 3.1 %collective-permute-start.1 = (bf16[24,3584]{1,0:T(8,128)(2,1)S(1)}, bf16[24,3584]{1,0:T(8,128)(2,1)S(1)}, u32[]{:S(2)}, u32[]{:S(2)}) collective-permute-start(bf16[24,3584]{1,0:T(8,128)(2,1)S(1)} %get-tuple-element.68), channel_id=1, source_target_pairs={{0,4},{2,6},{4,0},{6,2},{8,12},{10,14},{12,8},{14,10},{1,5},{3,7},... | collective-permute-start | bytes 516104 | tf_op jit(solution)/shard_map/ppermute | solution.py:22
  6.2 2.7 %collective-permute-start.3 = (bf16[16,3584]{1,0:T(8,128)(2,1)S(1)}, bf16[16,3584]{1,0:T(8,128)(2,1)S(1)}, u32[]{:S(2)}, u32[]{:S(2)}) collective-permute-start(bf16[16,3584]{1,0:T(8,128)(2,1)S(1)} %get-tuple-element.70), channel_id=1, source_target_pairs={{0,8},{2,10},{4,12},{6,14},{8,0},{10,2},{12,4},{14,6},{1,9},{3,11}... | collective-permute-start | bytes 344072 | tf_op jit(solution)/shard_map/ppermute | solution.py:22
  8.9 1.4 %collective-permute-start.2 = (bf16[24,3584]{1,0:T(8,128)(2,1)S(1)}, bf16[24,3584]{1,0:T(8,128)(2,1)S(1)}, u32[]{:S(2)}, u32[]{:S(2)}) collective-permute-start(bf16[24,3584]{1,0:T(8,128)(2,1)S(1)} %get-tuple-element.69), channel_id=1, source_target_pairs={{0,6},{2,4},{4,2},{6,0},{8,14},{10,12},{12,10},{14,8},{1,7},{3,5},... | collective-permute-start | bytes 516104 | tf_op jit(solution)/shard_map/ppermute | solution.py:22
  10.3 1.3 %collective-permute-start.6 = (bf16[8,3584]{1,0:T(8,128)(2,1)S(1)}, bf16[8,3584]{1,0:T(8,128)(2,1)S(1)}, u32[]{:S(2)}, u32[]{:S(2)}) collective-permute-start(bf16[8,3584]{1,0:T(8,128)(2,1)S(1)} %get-tuple-element.57), channel_id=1, source_target_pairs={{0,12},{2,14},{4,8},{6,10},{8,4},{10,6},{12,0},{14,2},{1,13},{3,15... | collective-permute-start | bytes 172040 | tf_op jit(solution)/shard_map/ppermute | solution.py:22
  11.7 2.4 %collective-permute-start.7 = (bf16[8,3584]{1,0:T(8,128)(2,1)S(1)}, bf16[8,3584]{1,0:T(8,128)(2,1)S(1)}, u32[]{:S(2)}, u32[]{:S(2)}) collective-permute-start(bf16[8,3584]{1,0:T(8,128)(2,1)S(1)} %get-tuple-element.56), channel_id=1, source_target_pairs={{0,14},{2,12},{4,10},{6,8},{8,6},{10,4},{12,2},{14,0},{1,15},{3,13... | collective-permute-start | bytes 172040 | tf_op jit(solution)/shard_map/ppermute | solution.py:22
  14.1 1.8 %collective-permute-start.4 = (bf16[24,3584]{1,0:T(8,128)(2,1)S(1)}, bf16[24,3584]{1,0:T(8,128)(2,1)S(1)}, u32[]{:S(2)}, u32[]{:S(2)}) collective-permute-start(bf16[24,3584]{1,0:T(8,128)(2,1)S(1)} %pad_maximum_fusion.4), channel_id=1, source_target_pairs={{0,2},{2,0},{4,6},{6,4},{8,10},{10,8},{12,14},{14,12},{1,3},{3,1},... | collective-permute-start | bytes 516104 | tf_op jit(solution)/shard_map/ppermute | solution.py:22
  16.0 2.4 %collective-permute-start.5 = (bf16[8,3584]{1,0:T(8,128)(2,1)S(1)}, bf16[8,3584]{1,0:T(8,128)(2,1)S(1)}, u32[]{:S(2)}, u32[]{:S(2)}) collective-permute-start(bf16[8,3584]{1,0:T(8,128)(2,1)S(1)} %get-tuple-element.33), channel_id=1, source_target_pairs={{0,10},{2,8},{4,14},{6,12},{8,2},{10,0},{12,6},{14,4},{1,11},{3,9}... | collective-permute-start | bytes 172040 | tf_op jit(solution)/shard_map/ppermute | solution.py:22
  18.4 4.2 %load.1 = (bf16[1,3584,512]{2,1,0:T(8,128)(2,1)S(1)}, bf16[1,3584,512]{2,1,0:T(8,128)(2,1)S(1)}, bf16[1,512,3584]{2,1,0:T(8,128)(2,1)S(1)}) custom-call(bf16[1,3584,512]{2,1,0:T(8,128)(2,1)} %refs_0_, bf16[1,3584,512]{2,1,0:T(8,128)(2,1)} %refs_1_, bf16[1,512,3584]{2,1,0:T(8,128)(2,1)} %refs_2_), custom_call_target="tpu_custom_call" | custom-call | bytes 11010048 | tf_op jit(solution)/shard_map/load/pallas_call | solution.py:64
  22.6 1.1 %collective-permute-done.4 = bf16[24,3584]{1,0:T(8,128)(2,1)S(1)} collective-permute-done((bf16[24,3584]{1,0:T(8,128)(2,1)S(1)}, bf16[24,3584]{1,0:T(8,128)(2,1)S(1)}, u32[]{:S(2)}, u32[]{:S(2)}) %collective-permute-start.4) | collective-permute-done | bytes 172064 | tf_op jit(solution)/shard_map/ppermute | solution.py:22
  24.4 1.0 %collective-permute-start.10 = (bf16[16,3584]{1,0:T(8,128)(2,1)S(1)}, bf16[16,3584]{1,0:T(8,128)(2,1)S(1)}, u32[]{:S(2)}, u32[]{:S(2)}) collective-permute-start(bf16[16,3584]{1,0:T(8,128)(2,1)S(1)} %pad_maximum_fusion.7), channel_id=1, source_target_pairs={{0,4},{2,6},{4,0},{6,2},{8,12},{10,14},{12,8},{14,10},{1,5},{3,7},... | collective-permute-start | bytes 344072 | tf_op jit(solution)/shard_map/ppermute | solution.py:22
  25.4 0.8 %collective-permute-done.8.peer = bf16[64,3584]{1,0:T(8,128)(2,1)S(1)} collective-permute-done((bf16[64,3584]{1,0:T(8,128)(2,1)S(1)}, bf16[64,3584]{1,0:T(8,128)(2,1)S(1)}, u32[]{:S(2)}, u32[]{:S(2)}) %collective-permute-start.8) | collective-permute-done | bytes 458784 | tf_op jit(solution)/shard_map/ppermute | solution.py:17
  26.2 1.8 %ffn.1 = (bf16[64,3584]{1,0:T(8,128)(2,1)S(1)}, bf16[64,3584]{1,0:T(8,128)(2,1)S(1)}) custom-call(bf16[64,3584]{1,0:T(8,128)(2,1)S(1)} %constant_dynamic-update-slice_fusion.own, bf16[64,3584]{1,0:T(8,128)(2,1)S(1)} %collective-permute-done.8.peer, s32[1,16]{1,0:T(1,128)S(1)} %copy-done.4, bf16[1,3584,512]{2,1,0:T(8,128)(2,1)S(1)} %get-tuple-element.44.gate, ...), custom_call_target="tpu_custom_call" | custom-call | flops 1409286144 | bytes 11010048 | tf_op jit(solution)/shard_map/ffn/pallas_call | solution.py:115
  28.6 1.3 %collective-permute-done.10 = bf16[16,3584]{1,0:T(8,128)(2,1)S(1)} collective-permute-done((bf16[16,3584]{1,0:T(8,128)(2,1)S(1)}, bf16[16,3584]{1,0:T(8,128)(2,1)S(1)}, u32[]{:S(2)}, u32[]{:S(2)}) %collective-permute-start.10) | collective-permute-done | bytes 114720 | tf_op jit(solution)/shard_map/ppermute | solution.py:22
  30.0 0.8 %add_halves.1 = bf16[8,8,3584]{2,1,0:T(8,128)(2,1)} custom-call(bf16[64,3584]{1,0:T(8,128)(2,1)S(1)} %get-tuple-element.53.ours, bf16[64,3584]{1,0:T(8,128)(2,1)S(1)} %collective-permute-done.9.other), custom_call_target="tpu_custom_call" | custom-call | flops 229376 | bytes 1376256 | tf_op jit(solution)/shard_map/add_halves/pallas_call | solution.py:143
  30.8 4.6 %all-to-all-start = ((bf16[8,8,3584]{2,1,0:T(8,128)(2,1)}), bf16[8,8,3584]{2,1,0:T(8,128)(2,1)S(1)}, u32[]{:S(2)}, u32[]{:S(2)}) async-start(bf16[8,8,3584]{2,1,0:T(8,128)(2,1)} %add_halves.1), calls=%async_computation | async-start | bytes 917504 | tf_op jit(solution)/shard_map/all_to_all | solution.py:338
  35.4 1.6 %collective-permute-start.11 = (bf16[40,3584]{1,0:T(8,128)(2,1)S(1)}, bf16[40,3584]{1,0:T(8,128)(2,1)S(1)}, u32[]{:S(2)}, u32[]{:S(2)}) collective-permute-start(bf16[40,3584]{1,0:T(8,128)(2,1)S(1)} %pad_maximum_fusion.1.refs_1_), channel_id=1, source_target_pairs={{0,16},{16,0},{1,17},{17,1},{2,18},{18,2},{3,19},{19,3},{4,20},{20... | collective-permute-start | bytes 860168 | tf_op jit(solution)/shard_map/ppermute | solution.py:22
  37.0 7.0 %collective-permute-done.11.refs_2_ = bf16[40,3584]{1,0:T(8,128)(2,1)S(1)} collective-permute-done((bf16[40,3584]{1,0:T(8,128)(2,1)S(1)}, bf16[40,3584]{1,0:T(8,128)(2,1)S(1)}, u32[]{:S(2)}, u32[]{:S(2)}) %collective-permute-start.11) | collective-permute-done | bytes 286752 | tf_op jit(solution)/shard_map/ppermute | solution.py:22
  44.0 0.6 %half_logits.1 = (f32[128,128]{1,0:T(8,128)S(1)}, f32[128,128]{1,0:T(8,128)S(1)}) custom-call(bf16[128,3584]{1,0:T(8,128)(2,1)S(1)} %copy-done.1, bf16[128,3584]{1,0:T(8,128)(2,1)S(1)} %collective-permute-done.peer_tokens, bf16[48,3584]{1,0:T(8,128)(2,1)S(1)} %pad_maximum_fusion.refs_0_, bf16[40,3584]{1,0:T(8,128)(2,1)S(1)} %pad_maximum_fusion.1.refs_1_, ...), custom_call_target="tpu_custom_call" | custom-call | flops 234881024 | bytes 2752512 | tf_op jit(solution)/shard_map/half_logits/pallas_call | solution.py:179
  44.9 1.1 %collective-permute-done.12.refs_1_ = f32[128,128]{1,0:T(8,128)S(1)} collective-permute-done((f32[128,128]{1,0:T(8,128)S(1)}, f32[128,128]{1,0:T(8,128)S(1)}, u32[]{:S(2)}, u32[]{:S(2)}) %collective-permute-start.12) | collective-permute-done | bytes 65568 | tf_op jit(solution)/shard_map/ppermute | solution.py:17
  46.0 1.0 %router_terms.1 = (bf16[128,64]{1,0:T(8,128)(2,1)S(1)}, f32[1,128]{1,0:T(1,128)}) custom-call(s32[8,128]{1,0:T(8,128)S(1)} %bitcast.45, s32[8,128]{1,0:T(8,128)S(1)} %bitcast.46, s32[1,128]{1,0:T(1,128)S(1)} %bitcast.47, f32[256,128]{1,0:T(8,128)S(1)} %bitcast.44, f32[128,128]{1,0:T(8,128)S(1)} %get-tuple-element.50.refs_0_, ...), custom_call_target="tpu_custom_call" | custom-call | flops 983040 | bytes 393216 | tf_op jit(solution)/shard_map/router_terms/pallas_call | solution.py:232
  47.0 1.7 %all-to-all-done = bf16[8,8,3584]{2,1,0:T(8,128)(2,1)S(1)} async-done(((bf16[8,8,3584]{2,1,0:T(8,128)(2,1)}), bf16[8,8,3584]{2,1,0:T(8,128)(2,1)S(1)}, u32[]{:S(2)}, u32[]{:S(2)}) %all-to-all-start) | async-done | bytes 458784 | tf_op jit(solution)/shard_map/all_to_all | solution.py:338
  48.7 1.1 %combine.1 = bf16[128,3584]{1,0:T(8,128)(2,1)} custom-call(bf16[128,64]{1,0:T(8,128)(2,1)S(1)} %get-tuple-element.52.weights, bf16[64,3584]{1,0:T(8,128)(2,1)S(1)} %bitcast.43), custom_call_target="tpu_custom_call" | custom-call | flops 58720256 | bytes 917504 | tf_op jit(solution)/shard_map/combine/pallas_call | solution.py:264
  (48 shorter events, 1.6 us)
Async XLA Ops:
  0.6 0.9 %copy-start = (bf16[32,3584]{1,0:T(8,128)(2,1)S(1)}, bf16[32,3584]{1,0:T(8,128)(2,1)}, u32[]{:S(2)}) copy-start(bf16[32,3584]{1,0:T(8,128)(2,1)} %param.11) | copy-start | bytes 688132
  3.1 11.0 %collective-permute-start.1 = (bf16[24,3584]{1,0:T(8,128)(2,1)S(1)}, bf16[24,3584]{1,0:T(8,128)(2,1)S(1)}, u32[]{:S(2)}, u32[]{:S(2)}) collective-permute-start(bf16[24,3584]{1,0:T(8,128)(2,1)S(1)} %get-tuple-element.68), channel_id=1, source_target_pairs={{0,4},{2,6},{4,0},{6,2},{8,12},{10,14},{12,8},{14,10},{1,5},{3,7},... | collective-permute-start | bytes 516104 | tf_op jit(solution)/shard_map/ppermute | solution.py:22
  6.2 7.8 %collective-permute-start.3 = (bf16[16,3584]{1,0:T(8,128)(2,1)S(1)}, bf16[16,3584]{1,0:T(8,128)(2,1)S(1)}, u32[]{:S(2)}, u32[]{:S(2)}) collective-permute-start(bf16[16,3584]{1,0:T(8,128)(2,1)S(1)} %get-tuple-element.70), channel_id=1, source_target_pairs={{0,8},{2,10},{4,12},{6,14},{8,0},{10,2},{12,4},{14,6},{1,9},{3,11}... | collective-permute-start | bytes 344072 | tf_op jit(solution)/shard_map/ppermute | solution.py:22
  8.9 14.9 %collective-permute-start.2 = (bf16[24,3584]{1,0:T(8,128)(2,1)S(1)}, bf16[24,3584]{1,0:T(8,128)(2,1)S(1)}, u32[]{:S(2)}, u32[]{:S(2)}) collective-permute-start(bf16[24,3584]{1,0:T(8,128)(2,1)S(1)} %get-tuple-element.69), channel_id=1, source_target_pairs={{0,6},{2,4},{4,2},{6,0},{8,14},{10,12},{12,10},{14,8},{1,7},{3,5},... | collective-permute-start | bytes 516104 | tf_op jit(solution)/shard_map/ppermute | solution.py:22
  10.3 13.9 %collective-permute-start.6 = (bf16[8,3584]{1,0:T(8,128)(2,1)S(1)}, bf16[8,3584]{1,0:T(8,128)(2,1)S(1)}, u32[]{:S(2)}, u32[]{:S(2)}) collective-permute-start(bf16[8,3584]{1,0:T(8,128)(2,1)S(1)} %get-tuple-element.57), channel_id=1, source_target_pairs={{0,12},{2,14},{4,8},{6,10},{8,4},{10,6},{12,0},{14,2},{1,13},{3,15... | collective-permute-start | bytes 172040 | tf_op jit(solution)/shard_map/ppermute | solution.py:22
  11.7 12.6 %collective-permute-start.7 = (bf16[8,3584]{1,0:T(8,128)(2,1)S(1)}, bf16[8,3584]{1,0:T(8,128)(2,1)S(1)}, u32[]{:S(2)}, u32[]{:S(2)}) collective-permute-start(bf16[8,3584]{1,0:T(8,128)(2,1)S(1)} %get-tuple-element.56), channel_id=1, source_target_pairs={{0,14},{2,12},{4,10},{6,8},{8,6},{10,4},{12,2},{14,0},{1,15},{3,13... | collective-permute-start | bytes 172040 | tf_op jit(solution)/shard_map/ppermute | solution.py:22
  14.1 9.6 %collective-permute-start.4 = (bf16[24,3584]{1,0:T(8,128)(2,1)S(1)}, bf16[24,3584]{1,0:T(8,128)(2,1)S(1)}, u32[]{:S(2)}, u32[]{:S(2)}) collective-permute-start(bf16[24,3584]{1,0:T(8,128)(2,1)S(1)} %pad_maximum_fusion.4), channel_id=1, source_target_pairs={{0,2},{2,0},{4,6},{6,4},{8,10},{10,8},{12,14},{14,12},{1,3},{3,1},... | collective-permute-start | bytes 516104 | tf_op jit(solution)/shard_map/ppermute | solution.py:22
  16.0 10.2 %copy-start.4 = (s32[1,16]{1,0:T(1,128)S(1)}, s32[1,16]{1,0:T(1,128)}, u32[]{:S(2)}) copy-start(s32[1,16]{1,0:T(1,128)} %occupancy.1) | copy-start | bytes 196
  16.0 8.3 %collective-permute-start.5 = (bf16[8,3584]{1,0:T(8,128)(2,1)S(1)}, bf16[8,3584]{1,0:T(8,128)(2,1)S(1)}, u32[]{:S(2)}, u32[]{:S(2)}) collective-permute-start(bf16[8,3584]{1,0:T(8,128)(2,1)S(1)} %get-tuple-element.33), channel_id=1, source_target_pairs={{0,10},{2,8},{4,14},{6,12},{8,2},{10,0},{12,6},{14,4},{1,11},{3,9}... | collective-permute-start | bytes 172040 | tf_op jit(solution)/shard_map/ppermute | solution.py:22
  24.3 4.0 %copy-start.1 = (bf16[128,3584]{1,0:T(8,128)(2,1)S(1)}, bf16[128,3584]{1,0:T(8,128)(2,1)}, u32[]{:S(2)}) copy-start(bf16[128,3584]{1,0:T(8,128)(2,1)} %own_tokens.1) | copy-start | bytes 2752516
  24.3 1.9 %collective-permute-start.8 = (bf16[64,3584]{1,0:T(8,128)(2,1)S(1)}, bf16[64,3584]{1,0:T(8,128)(2,1)S(1)}, u32[]{:S(2)}, u32[]{:S(2)}) collective-permute-start(bf16[64,3584]{1,0:T(8,128)(2,1)S(1)} %constant_dynamic-update-slice_fusion.own), channel_id=1, source_target_pairs={{0,1},{1,0},{2,3},{3,2},{4,5},{5,4},{6,7},{7,6},{8,9},{9,8},{10,11... | collective-permute-start | bytes 1376264 | tf_op jit(solution)/shard_map/ppermute | solution.py:17
  24.4 5.6 %collective-permute-start.10 = (bf16[16,3584]{1,0:T(8,128)(2,1)S(1)}, bf16[16,3584]{1,0:T(8,128)(2,1)S(1)}, u32[]{:S(2)}, u32[]{:S(2)}) collective-permute-start(bf16[16,3584]{1,0:T(8,128)(2,1)S(1)} %pad_maximum_fusion.7), channel_id=1, source_target_pairs={{0,4},{2,6},{4,0},{6,2},{8,12},{10,14},{12,8},{14,10},{1,5},{3,7},... | collective-permute-start | bytes 344072 | tf_op jit(solution)/shard_map/ppermute | solution.py:22
  28.0 16.8 %copy-start.6 = (f32[128,256]{1,0:T(8,128)S(1)}, f32[128,256]{1,0:T(8,128)}, u32[]{:S(2)}) copy-start(f32[128,256]{1,0:T(8,128)} %param.15) | copy-start | bytes 393220
  28.0 18.0 %copy-start.2 = (s32[128,8]{0,1:T(8,128)S(1)}, s32[128,8]{0,1:T(8,128)}, u32[]{:S(2)}) copy-start(s32[128,8]{0,1:T(8,128)} %param.16) | copy-start | bytes 12292
  28.0 18.0 %copy-start.3 = (s32[128,8]{0,1:T(8,128)S(1)}, s32[128,8]{0,1:T(8,128)}, u32[]{:S(2)}) copy-start(s32[128,8]{0,1:T(8,128)} %param.17) | copy-start | bytes 12292
  28.0 18.0 %copy-start.5 = (s32[128]{0:T(128)S(1)}, s32[128]{0:T(128)}, u32[]{:S(2)}) copy-start(s32[128]{0:T(128)} %param.19) | copy-start | bytes 1540
  28.0 1.9 %collective-permute-start.9 = (bf16[64,3584]{1,0:T(8,128)(2,1)S(1)}, bf16[64,3584]{1,0:T(8,128)(2,1)S(1)}, u32[]{:S(2)}, u32[]{:S(2)}) collective-permute-start(bf16[64,3584]{1,0:T(8,128)(2,1)S(1)} %get-tuple-element.47), channel_id=1, source_target_pairs={{0,1},{1,0},{2,3},{3,2},{4,5},{5,4},{6,7},{7,6},{8,9},{9,8},{10,11... | collective-permute-start | bytes 1376264 | tf_op jit(solution)/shard_map/ppermute | solution.py:17
  28.2 8.8 %collective-permute-start = (bf16[128,3584]{1,0:T(8,128)(2,1)S(1)}, bf16[128,3584]{1,0:T(8,128)(2,1)S(1)}, u32[]{:S(2)}, u32[]{:S(2)}) collective-permute-start(bf16[128,3584]{1,0:T(8,128)(2,1)S(1)} %copy-done.1), channel_id=1, source_target_pairs={{0,1},{1,0},{2,3},{3,2},{4,5},{5,4},{6,7},{7,6},{8,9},{9,8},{10,11... | collective-permute-start | bytes 2752520 | tf_op jit(solution)/shard_map/ppermute | solution.py:17
  30.8 17.9 %all-to-all-start = ((bf16[8,8,3584]{2,1,0:T(8,128)(2,1)}), bf16[8,8,3584]{2,1,0:T(8,128)(2,1)S(1)}, u32[]{:S(2)}, u32[]{:S(2)}) async-start(bf16[8,8,3584]{2,1,0:T(8,128)(2,1)} %add_halves.1), calls=%async_computation | async-start | bytes 917504 | tf_op jit(solution)/shard_map/all_to_all | solution.py:338
  35.4 8.6 %collective-permute-start.11 = (bf16[40,3584]{1,0:T(8,128)(2,1)S(1)}, bf16[40,3584]{1,0:T(8,128)(2,1)S(1)}, u32[]{:S(2)}, u32[]{:S(2)}) collective-permute-start(bf16[40,3584]{1,0:T(8,128)(2,1)S(1)} %pad_maximum_fusion.1.refs_1_), channel_id=1, source_target_pairs={{0,16},{16,0},{1,17},{17,1},{2,18},{18,2},{3,19},{19,3},{4,20},{20... | collective-permute-start | bytes 860168 | tf_op jit(solution)/shard_map/ppermute | solution.py:22
  44.7 1.3 %collective-permute-start.12 = (f32[128,128]{1,0:T(8,128)S(1)}, f32[128,128]{1,0:T(8,128)S(1)}, u32[]{:S(2)}, u32[]{:S(2)}) collective-permute-start(f32[128,128]{1,0:T(8,128)S(1)} %get-tuple-element.51), channel_id=1, source_target_pairs={{0,1},{1,0},{2,3},{3,2},{4,5},{5,4},{6,7},{7,6},{8,9},{9,8},{10,11... | collective-permute-start | bytes 196616 | tf_op jit(solution)/shard_map/ppermute | solution.py:17

commit v7 on v6

--- a/solution.py
+++ b/solution.py
@@ -309,7 +309,7 @@
             block = lax.dynamic_index_in_dim(outgoing, at ^ d, 0, keepdims=False)
             along = [mine] if d in (2, 3) else [piece] if d < 5 else []
             send[d] = jnp.concatenate([block] + along, axis=0)
-        for d, before in ((4, 0), (2, 0), (3, 0), (6, 0), (7, 0), (5, 4), (1, 2)):
+        for d, before in ((4, 0), (2, 0), (3, 0), (6, 0), (7, 0), (5, 4), (1, 3)):
             if before:
                 blocks[before], send[d] = lax.optimization_barrier((blocks[before], send[d]))
             if d == 1:

time: 50.1 us -> 49.5 us (0.988)
  waiting for transfers between devices: 13.5 us -> 12.8 us
    ppermute x9, starting transfers between devices: 17.8 us -> 18.4 us  [across(): return lax.ppermute(value, axis, [(s, s ^ distance) for s in range(size)])]
    all_to_all x1, starting transfers between devices: 4.58 us -> 4.01 us  [per_device(): lax.all_to_all(summed, 'expert', split_axis=0, concat_axis=0, tiled=True)]
  transfers between devices with their start and end apart: 14 -> 14, of which waited for: 7 -> 8; matrix products, arithmetic and copies ran while one was open for 0% -> 1% of each run, Pallas kernels for 17% -> 17%
where the time goes in v7:
time: 49.5 us; the launch traced here: 49.2 us
  starting transfers between devices  23.1 us (47%)
  waiting for transfers between devices  12.8 us (26%)
  Pallas kernels  9.65 us (19%)
  matrix products  1.45 us (3%)
  between operations  0.98 us (2%)
  other arithmetic  0.88 us (2%)
    ppermute x9, starting transfers between devices, across(): return lax.ppermute(value, axis, [(s, s ^ distance) for s in range(size)])  18.4 us
    ppermute x9, waiting for transfers between devices, across(): return lax.ppermute(value, axis, [(s, s ^ distance) for s in range(size)])  9.5 us
    pallas_call x1, Pallas kernels, load(): pl.pallas_call(load_kernel, out_shape=tuple((jax.ShapeDtypeStruct(w.shape...  4.23 us
    all_to_all x1, starting transfers between devices, per_device(): lax.all_to_all(summed, 'expert', split_axis=0, concat_axis=0, tiled=True)  4.01 us
    pallas_call x1, Pallas kernels, ffn(): pl.pallas_call(functools.partial(ffn_kernel, parts, relative), out_shape=...  1.81 us
    all_to_all x1, waiting for transfers between devices, per_device(): lax.all_to_all(summed, 'expert', split_axis=0, concat_axis=0, tiled=True)  1.73 us
    ppermute x4, waiting for transfers between devices, swap_cores(): return lax.ppermute(value, 'tensor', SWAP)  1.53 us
    dot_general x1, matrix products, per_device(): jnp.dot(hits.astype(jnp.bfloat16), tokens, preferred_element_type=jnp.flo...  1.45 us
  transfers between devices with their start and end apart: 14, of which 8 were waited for; matrix products, arithmetic and copies ran while one was open for 1% of the time, Pallas kernels for 17%

profile of v7, /device:TPU:0, one launch (start us, length us, event | category | flops | bytes accessed | tf_op | source)
XLA Modules:
  0.0 49.2 jit_solution(14308577973319092570)
XLA Ops:
  0.7 0.8 %add_select_fusion = s32[8,128]{1,0:T(8,128)S(1)} fusion(s32[128,8]{0,1:T(8,128)} %param.17, s32[128,8]{0,1:T(8,128)} %param.16), kind=kLoop, calls=%fused_computation.48 | loop fusion | flops 6144 | bytes 12288 | tf_op jit(solution)/shard_map/jit(_where)/select_n | solution.py:42
  1.6 1.5 %fusion = bf16[8,8,3584]{2,1,0:T(8,128)(2,1)S(1)} fusion(bf16[128,3584]{1,0:T(8,128)(2,1)} %own_tokens.1, s32[128]{0:T(128)S(1)} %get-tuple-element.73, s32[128]{0:T(128)S(1)} %get-tuple-element.74, s32[128]{0:T(128)S(1)} %get-tuple-element.75, s32[128]{0:T(128)S(1)} %get-tuple-element.76, s32[128]{0:T(128)S(1)} %get-tuple-element.77, ...), kind=kOutput, calls=%fused_computation.1 | convolution fusion | flops 59072512 | bytes 1380352 | tf_op jit(solution)/shard_map/dot_general | solution.py:300
  3.1 4.0 %collective-permute-start.2 = (bf16[24,3584]{1,0:T(8,128)(2,1)S(1)}, bf16[24,3584]{1,0:T(8,128)(2,1)S(1)}, u32[]{:S(2)}, u32[]{:S(2)}) collective-permute-start(bf16[24,3584]{1,0:T(8,128)(2,1)S(1)} %get-tuple-element.69), channel_id=1, source_target_pairs={{0,6},{2,4},{4,2},{6,0},{8,14},{10,12},{12,10},{14,8},{1,7},{3,5},... | collective-permute-start | bytes 516104 | tf_op jit(solution)/shard_map/ppermute | solution.py:22
  7.2 2.7 %collective-permute-start.3 = (bf16[16,3584]{1,0:T(8,128)(2,1)S(1)}, bf16[16,3584]{1,0:T(8,128)(2,1)S(1)}, u32[]{:S(2)}, u32[]{:S(2)}) collective-permute-start(bf16[16,3584]{1,0:T(8,128)(2,1)S(1)} %get-tuple-element.70), channel_id=1, source_target_pairs={{0,8},{2,10},{4,12},{6,14},{8,0},{10,2},{12,4},{14,6},{1,9},{3,11}... | collective-permute-start | bytes 344072 | tf_op jit(solution)/shard_map/ppermute | solution.py:22
  9.9 0.4 collective-permute-start.1
  10.3 1.3 %collective-permute-start.6 = (bf16[8,3584]{1,0:T(8,128)(2,1)S(1)}, bf16[8,3584]{1,0:T(8,128)(2,1)S(1)}, u32[]{:S(2)}, u32[]{:S(2)}) collective-permute-start(bf16[8,3584]{1,0:T(8,128)(2,1)S(1)} %get-tuple-element.57), channel_id=1, source_target_pairs={{0,12},{2,14},{4,8},{6,10},{8,4},{10,6},{12,0},{14,2},{1,13},{3,15... | collective-permute-start | bytes 172040 | tf_op jit(solution)/shard_map/ppermute | solution.py:22
  11.7 2.4 %collective-permute-start.7 = (bf16[8,3584]{1,0:T(8,128)(2,1)S(1)}, bf16[8,3584]{1,0:T(8,128)(2,1)S(1)}, u32[]{:S(2)}, u32[]{:S(2)}) collective-permute-start(bf16[8,3584]{1,0:T(8,128)(2,1)S(1)} %get-tuple-element.56), channel_id=1, source_target_pairs={{0,14},{2,12},{4,10},{6,8},{8,6},{10,4},{12,2},{14,0},{1,15},{3,13... | collective-permute-start | bytes 172040 | tf_op jit(solution)/shard_map/ppermute | solution.py:22
  14.4 0.4 collective-permute-done.2
  14.9 2.0 %collective-permute-start.4 = (bf16[24,3584]{1,0:T(8,128)(2,1)S(1)}, bf16[24,3584]{1,0:T(8,128)(2,1)S(1)}, u32[]{:S(2)}, u32[]{:S(2)}) collective-permute-start(bf16[24,3584]{1,0:T(8,128)(2,1)S(1)} %pad_maximum_fusion.4), channel_id=1, source_target_pairs={{0,2},{2,0},{4,6},{6,4},{8,10},{10,8},{12,14},{14,12},{1,3},{3,1},... | collective-permute-start | bytes 516104 | tf_op jit(solution)/shard_map/ppermute | solution.py:22
  16.9 2.5 %collective-permute-start.5 = (bf16[8,3584]{1,0:T(8,128)(2,1)S(1)}, bf16[8,3584]{1,0:T(8,128)(2,1)S(1)}, u32[]{:S(2)}, u32[]{:S(2)}) collective-permute-start(bf16[8,3584]{1,0:T(8,128)(2,1)S(1)} %get-tuple-element.33), channel_id=1, source_target_pairs={{0,10},{2,8},{4,14},{6,12},{8,2},{10,0},{12,6},{14,4},{1,11},{3,9}... | collective-permute-start | bytes 172040 | tf_op jit(solution)/shard_map/ppermute | solution.py:22
  19.4 4.2 %load.1 = (bf16[1,3584,512]{2,1,0:T(8,128)(2,1)S(1)}, bf16[1,3584,512]{2,1,0:T(8,128)(2,1)S(1)}, bf16[1,512,3584]{2,1,0:T(8,128)(2,1)S(1)}) custom-call(bf16[1,3584,512]{2,1,0:T(8,128)(2,1)} %refs_0_, bf16[1,3584,512]{2,1,0:T(8,128)(2,1)} %refs_1_, bf16[1,512,3584]{2,1,0:T(8,128)(2,1)} %refs_2_), custom_call_target="tpu_custom_call" | custom-call | bytes 11010048 | tf_op jit(solution)/shard_map/load/pallas_call | solution.py:64
  23.7 0.4 collective-permute-done.5
  24.3 1.4 %collective-permute-start.10 = (bf16[16,3584]{1,0:T(8,128)(2,1)S(1)}, bf16[16,3584]{1,0:T(8,128)(2,1)S(1)}, u32[]{:S(2)}, u32[]{:S(2)}) collective-permute-start(bf16[16,3584]{1,0:T(8,128)(2,1)S(1)} %pad_maximum_fusion.7), channel_id=1, source_target_pairs={{0,4},{2,6},{4,0},{6,2},{8,12},{10,14},{12,8},{14,10},{1,5},{3,7},... | collective-permute-start | bytes 344072 | tf_op jit(solution)/shard_map/ppermute | solution.py:22
  26.1 1.8 %ffn.1 = (bf16[64,3584]{1,0:T(8,128)(2,1)S(1)}, bf16[64,3584]{1,0:T(8,128)(2,1)S(1)}) custom-call(bf16[64,3584]{1,0:T(8,128)(2,1)S(1)} %constant_dynamic-update-slice_fusion.own, bf16[64,3584]{1,0:T(8,128)(2,1)S(1)} %collective-permute-done.8.peer, s32[1,16]{1,0:T(1,128)S(1)} %copy-done.4, bf16[1,3584,512]{2,1,0:T(8,128)(2,1)S(1)} %get-tuple-element.44.gate, ...), custom_call_target="tpu_custom_call" | custom-call | flops 1409286144 | bytes 11010048 | tf_op jit(solution)/shard_map/ffn/pallas_call | solution.py:115
  28.5 1.3 %collective-permute-done.10 = bf16[16,3584]{1,0:T(8,128)(2,1)S(1)} collective-permute-done((bf16[16,3584]{1,0:T(8,128)(2,1)S(1)}, bf16[16,3584]{1,0:T(8,128)(2,1)S(1)}, u32[]{:S(2)}, u32[]{:S(2)}) %collective-permute-start.10) | collective-permute-done | bytes 114720 | tf_op jit(solution)/shard_map/ppermute | solution.py:22
  29.9 0.8 %add_halves.1 = bf16[8,8,3584]{2,1,0:T(8,128)(2,1)} custom-call(bf16[64,3584]{1,0:T(8,128)(2,1)S(1)} %get-tuple-element.53.ours, bf16[64,3584]{1,0:T(8,128)(2,1)S(1)} %collective-permute-done.9.other), custom_call_target="tpu_custom_call" | custom-call | flops 229376 | bytes 1376256 | tf_op jit(solution)/shard_map/add_halves/pallas_call | solution.py:143
  30.7 4.0 %all-to-all-start = ((bf16[8,8,3584]{2,1,0:T(8,128)(2,1)}), bf16[8,8,3584]{2,1,0:T(8,128)(2,1)S(1)}, u32[]{:S(2)}, u32[]{:S(2)}) async-start(bf16[8,8,3584]{2,1,0:T(8,128)(2,1)} %add_halves.1), calls=%async_computation | async-start | bytes 917504 | tf_op jit(solution)/shard_map/all_to_all | solution.py:338
  34.8 1.6 %collective-permute-start.11 = (bf16[40,3584]{1,0:T(8,128)(2,1)S(1)}, bf16[40,3584]{1,0:T(8,128)(2,1)S(1)}, u32[]{:S(2)}, u32[]{:S(2)}) collective-permute-start(bf16[40,3584]{1,0:T(8,128)(2,1)S(1)} %pad_maximum_fusion.1.refs_1_), channel_id=1, source_target_pairs={{0,16},{16,0},{1,17},{17,1},{2,18},{18,2},{3,19},{19,3},{4,20},{20... | collective-permute-start | bytes 860168 | tf_op jit(solution)/shard_map/ppermute | solution.py:22
  36.4 7.0 %collective-permute-done.11.refs_2_ = bf16[40,3584]{1,0:T(8,128)(2,1)S(1)} collective-permute-done((bf16[40,3584]{1,0:T(8,128)(2,1)S(1)}, bf16[40,3584]{1,0:T(8,128)(2,1)S(1)}, u32[]{:S(2)}, u32[]{:S(2)}) %collective-permute-start.11) | collective-permute-done | bytes 286752 | tf_op jit(solution)/shard_map/ppermute | solution.py:22
  43.4 0.6 %half_logits.1 = (f32[128,128]{1,0:T(8,128)S(1)}, f32[128,128]{1,0:T(8,128)S(1)}) custom-call(bf16[128,3584]{1,0:T(8,128)(2,1)S(1)} %copy-done.1, bf16[128,3584]{1,0:T(8,128)(2,1)S(1)} %collective-permute-done.peer_tokens, bf16[48,3584]{1,0:T(8,128)(2,1)S(1)} %pad_maximum_fusion.refs_0_, bf16[40,3584]{1,0:T(8,128)(2,1)S(1)} %pad_maximum_fusion.1.refs_1_, ...), custom_call_target="tpu_custom_call" | custom-call | flops 234881024 | bytes 2752512 | tf_op jit(solution)/shard_map/half_logits/pallas_call | solution.py:179
  44.2 1.1 %collective-permute-done.12.refs_1_ = f32[128,128]{1,0:T(8,128)S(1)} collective-permute-done((f32[128,128]{1,0:T(8,128)S(1)}, f32[128,128]{1,0:T(8,128)S(1)}, u32[]{:S(2)}, u32[]{:S(2)}) %collective-permute-start.12) | collective-permute-done | bytes 65568 | tf_op jit(solution)/shard_map/ppermute | solution.py:17
  45.3 1.0 %router_terms.1 = (bf16[128,64]{1,0:T(8,128)(2,1)S(1)}, f32[1,128]{1,0:T(1,128)}) custom-call(s32[8,128]{1,0:T(8,128)S(1)} %bitcast.45, s32[8,128]{1,0:T(8,128)S(1)} %bitcast.46, s32[1,128]{1,0:T(1,128)S(1)} %bitcast.47, f32[256,128]{1,0:T(8,128)S(1)} %bitcast.44, f32[128,128]{1,0:T(8,128)S(1)} %get-tuple-element.50.refs_0_, ...), custom_call_target="tpu_custom_call" | custom-call | flops 983040 | bytes 393216 | tf_op jit(solution)/shard_map/router_terms/pallas_call | solution.py:232
  46.3 1.7 %all-to-all-done = bf16[8,8,3584]{2,1,0:T(8,128)(2,1)S(1)} async-done(((bf16[8,8,3584]{2,1,0:T(8,128)(2,1)}), bf16[8,8,3584]{2,1,0:T(8,128)(2,1)S(1)}, u32[]{:S(2)}, u32[]{:S(2)}) %all-to-all-start) | async-done | bytes 458784 | tf_op jit(solution)/shard_map/all_to_all | solution.py:338
  48.1 1.1 %combine.1 = bf16[128,3584]{1,0:T(8,128)(2,1)} custom-call(bf16[128,64]{1,0:T(8,128)(2,1)S(1)} %get-tuple-element.52.weights, bf16[64,3584]{1,0:T(8,128)(2,1)S(1)} %bitcast.43), custom_call_target="tpu_custom_call" | custom-call | flops 58720256 | bytes 917504 | tf_op jit(solution)/shard_map/combine/pallas_call | solution.py:264
  (48 shorter events, 1.9 us)
Async XLA Ops:
  0.6 0.9 %copy-start = (bf16[32,3584]{1,0:T(8,128)(2,1)S(1)}, bf16[32,3584]{1,0:T(8,128)(2,1)}, u32[]{:S(2)}) copy-start(bf16[32,3584]{1,0:T(8,128)(2,1)} %param.11) | copy-start | bytes 688132
  3.1 11.7 %collective-permute-start.2 = (bf16[24,3584]{1,0:T(8,128)(2,1)S(1)}, bf16[24,3584]{1,0:T(8,128)(2,1)S(1)}, u32[]{:S(2)}, u32[]{:S(2)}) collective-permute-start(bf16[24,3584]{1,0:T(8,128)(2,1)S(1)} %get-tuple-element.69), channel_id=1, source_target_pairs={{0,6},{2,4},{4,2},{6,0},{8,14},{10,12},{12,10},{14,8},{1,7},{3,5},... | collective-permute-start | bytes 516104 | tf_op jit(solution)/shard_map/ppermute | solution.py:22
  7.2 7.2 %collective-permute-start.3 = (bf16[16,3584]{1,0:T(8,128)(2,1)S(1)}, bf16[16,3584]{1,0:T(8,128)(2,1)S(1)}, u32[]{:S(2)}, u32[]{:S(2)}) collective-permute-start(bf16[16,3584]{1,0:T(8,128)(2,1)S(1)} %get-tuple-element.70), channel_id=1, source_target_pairs={{0,8},{2,10},{4,12},{6,14},{8,0},{10,2},{12,4},{14,6},{1,9},{3,11}... | collective-permute-start | bytes 344072 | tf_op jit(solution)/shard_map/ppermute | solution.py:22
  9.9 13.8 %collective-permute-start.1 = (bf16[24,3584]{1,0:T(8,128)(2,1)S(1)}, bf16[24,3584]{1,0:T(8,128)(2,1)S(1)}, u32[]{:S(2)}, u32[]{:S(2)}) collective-permute-start(bf16[24,3584]{1,0:T(8,128)(2,1)S(1)} %get-tuple-element.68), channel_id=1, source_target_pairs={{0,4},{2,6},{4,0},{6,2},{8,12},{10,14},{12,8},{14,10},{1,5},{3,7},... | collective-permute-start | bytes 516104 | tf_op jit(solution)/shard_map/ppermute | solution.py:22
  10.3 13.8 %collective-permute-start.6 = (bf16[8,3584]{1,0:T(8,128)(2,1)S(1)}, bf16[8,3584]{1,0:T(8,128)(2,1)S(1)}, u32[]{:S(2)}, u32[]{:S(2)}) collective-permute-start(bf16[8,3584]{1,0:T(8,128)(2,1)S(1)} %get-tuple-element.57), channel_id=1, source_target_pairs={{0,12},{2,14},{4,8},{6,10},{8,4},{10,6},{12,0},{14,2},{1,13},{3,15... | collective-permute-start | bytes 172040 | tf_op jit(solution)/shard_map/ppermute | solution.py:22
  11.7 12.5 %collective-permute-start.7 = (bf16[8,3584]{1,0:T(8,128)(2,1)S(1)}, bf16[8,3584]{1,0:T(8,128)(2,1)S(1)}, u32[]{:S(2)}, u32[]{:S(2)}) collective-permute-start(bf16[8,3584]{1,0:T(8,128)(2,1)S(1)} %get-tuple-element.56), channel_id=1, source_target_pairs={{0,14},{2,12},{4,10},{6,8},{8,6},{10,4},{12,2},{14,0},{1,15},{3,13... | collective-permute-start | bytes 172040 | tf_op jit(solution)/shard_map/ppermute | solution.py:22
  14.9 8.8 %collective-permute-start.4 = (bf16[24,3584]{1,0:T(8,128)(2,1)S(1)}, bf16[24,3584]{1,0:T(8,128)(2,1)S(1)}, u32[]{:S(2)}, u32[]{:S(2)}) collective-permute-start(bf16[24,3584]{1,0:T(8,128)(2,1)S(1)} %pad_maximum_fusion.4), channel_id=1, source_target_pairs={{0,2},{2,0},{4,6},{6,4},{8,10},{10,8},{12,14},{14,12},{1,3},{3,1},... | collective-permute-start | bytes 516104 | tf_op jit(solution)/shard_map/ppermute | solution.py:22
  16.9 9.2 %copy-start.4 = (s32[1,16]{1,0:T(1,128)S(1)}, s32[1,16]{1,0:T(1,128)}, u32[]{:S(2)}) copy-start(s32[1,16]{1,0:T(1,128)} %occupancy.1) | copy-start | bytes 196
  16.9 7.3 %collective-permute-start.5 = (bf16[8,3584]{1,0:T(8,128)(2,1)S(1)}, bf16[8,3584]{1,0:T(8,128)(2,1)S(1)}, u32[]{:S(2)}, u32[]{:S(2)}) collective-permute-start(bf16[8,3584]{1,0:T(8,128)(2,1)S(1)} %get-tuple-element.33), channel_id=1, source_target_pairs={{0,10},{2,8},{4,14},{6,12},{8,2},{10,0},{12,6},{14,4},{1,11},{3,9}... | collective-permute-start | bytes 172040 | tf_op jit(solution)/shard_map/ppermute | solution.py:22
  24.2 4.0 %copy-start.1 = (bf16[128,3584]{1,0:T(8,128)(2,1)S(1)}, bf16[128,3584]{1,0:T(8,128)(2,1)}, u32[]{:S(2)}) copy-start(bf16[128,3584]{1,0:T(8,128)(2,1)} %own_tokens.1) | copy-start | bytes 2752516
  24.2 1.9 %collective-permute-start.8 = (bf16[64,3584]{1,0:T(8,128)(2,1)S(1)}, bf16[64,3584]{1,0:T(8,128)(2,1)S(1)}, u32[]{:S(2)}, u32[]{:S(2)}) collective-permute-start(bf16[64,3584]{1,0:T(8,128)(2,1)S(1)} %constant_dynamic-update-slice_fusion.own), channel_id=1, source_target_pairs={{0,1},{1,0},{2,3},{3,2},{4,5},{5,4},{6,7},{7,6},{8,9},{9,8},{10,11... | collective-permute-start | bytes 1376264 | tf_op jit(solution)/shard_map/ppermute | solution.py:17
  24.3 5.6 %collective-permute-start.10 = (bf16[16,3584]{1,0:T(8,128)(2,1)S(1)}, bf16[16,3584]{1,0:T(8,128)(2,1)S(1)}, u32[]{:S(2)}, u32[]{:S(2)}) collective-permute-start(bf16[16,3584]{1,0:T(8,128)(2,1)S(1)} %pad_maximum_fusion.7), channel_id=1, source_target_pairs={{0,4},{2,6},{4,0},{6,2},{8,12},{10,14},{12,8},{14,10},{1,5},{3,7},... | collective-permute-start | bytes 344072 | tf_op jit(solution)/shard_map/ppermute | solution.py:22
  27.9 16.2 %copy-start.6 = (f32[128,256]{1,0:T(8,128)S(1)}, f32[128,256]{1,0:T(8,128)}, u32[]{:S(2)}) copy-start(f32[128,256]{1,0:T(8,128)} %param.15) | copy-start | bytes 393220
  27.9 17.4 %copy-start.2 = (s32[128,8]{0,1:T(8,128)S(1)}, s32[128,8]{0,1:T(8,128)}, u32[]{:S(2)}) copy-start(s32[128,8]{0,1:T(8,128)} %param.16) | copy-start | bytes 12292
  27.9 17.4 %copy-start.3 = (s32[128,8]{0,1:T(8,128)S(1)}, s32[128,8]{0,1:T(8,128)}, u32[]{:S(2)}) copy-start(s32[128,8]{0,1:T(8,128)} %param.17) | copy-start | bytes 12292
  27.9 17.4 %copy-start.5 = (s32[128]{0:T(128)S(1)}, s32[128]{0:T(128)}, u32[]{:S(2)}) copy-start(s32[128]{0:T(128)} %param.19) | copy-start | bytes 1540
  28.0 1.9 %collective-permute-start.9 = (bf16[64,3584]{1,0:T(8,128)(2,1)S(1)}, bf16[64,3584]{1,0:T(8,128)(2,1)S(1)}, u32[]{:S(2)}, u32[]{:S(2)}) collective-permute-start(bf16[64,3584]{1,0:T(8,128)(2,1)S(1)} %get-tuple-element.47), channel_id=1, source_target_pairs={{0,1},{1,0},{2,3},{3,2},{4,5},{5,4},{6,7},{7,6},{8,9},{9,8},{10,11... | collective-permute-start | bytes 1376264 | tf_op jit(solution)/shard_map/ppermute | solution.py:17
  28.1 8.2 %collective-permute-start = (bf16[128,3584]{1,0:T(8,128)(2,1)S(1)}, bf16[128,3584]{1,0:T(8,128)(2,1)S(1)}, u32[]{:S(2)}, u32[]{:S(2)}) collective-permute-start(bf16[128,3584]{1,0:T(8,128)(2,1)S(1)} %copy-done.1), channel_id=1, source_target_pairs={{0,1},{1,0},{2,3},{3,2},{4,5},{5,4},{6,7},{7,6},{8,9},{9,8},{10,11... | collective-permute-start | bytes 2752520 | tf_op jit(solution)/shard_map/ppermute | solution.py:17
  30.7 17.3 %all-to-all-start = ((bf16[8,8,3584]{2,1,0:T(8,128)(2,1)}), bf16[8,8,3584]{2,1,0:T(8,128)(2,1)S(1)}, u32[]{:S(2)}, u32[]{:S(2)}) async-start(bf16[8,8,3584]{2,1,0:T(8,128)(2,1)} %add_halves.1), calls=%async_computation | async-start | bytes 917504 | tf_op jit(solution)/shard_map/all_to_all | solution.py:338
  34.8 8.6 %collective-permute-start.11 = (bf16[40,3584]{1,0:T(8,128)(2,1)S(1)}, bf16[40,3584]{1,0:T(8,128)(2,1)S(1)}, u32[]{:S(2)}, u32[]{:S(2)}) collective-permute-start(bf16[40,3584]{1,0:T(8,128)(2,1)S(1)} %pad_maximum_fusion.1.refs_1_), channel_id=1, source_target_pairs={{0,16},{16,0},{1,17},{17,1},{2,18},{18,2},{3,19},{19,3},{4,20},{20... | collective-permute-start | bytes 860168 | tf_op jit(solution)/shard_map/ppermute | solution.py:22
  44.0 1.3 %collective-permute-start.12 = (f32[128,128]{1,0:T(8,128)S(1)}, f32[128,128]{1,0:T(8,128)S(1)}, u32[]{:S(2)}, u32[]{:S(2)}) collective-permute-start(f32[128,128]{1,0:T(8,128)S(1)} %get-tuple-element.51), channel_id=1, source_target_pairs={{0,1},{1,0},{2,3},{3,2},{4,5},{5,4},{6,7},{7,6},{8,9},{9,8},{10,11... | collective-permute-start | bytes 196616 | tf_op jit(solution)/shard_map/ppermute | solution.py:17

commit v8 on v7

--- a/solution.py
+++ b/solution.py
@@ -159,14 +159,14 @@
     levels, (out_own, out_peer) = refs[:-2], refs[-2:]
     expert, group = lax.axis_index("expert"), lax.axis_index("groups")
     rows = jnp.concatenate([level[...] for level in levels], axis=0)
-    places = [(expert ^ d) * 16 for d in (0, 2, 3)]
+    places = [(expert ^ d) * 16 for d in (0, 2)]
     for side in range(2):
-        places += [(expert ^ d) * 16 + (group ^ side) * 8 for d in (1, 4, 5, 6, 7)]
+        places += [(expert ^ d) * 16 + (group ^ side) * 8 for d in (1, 3, 4, 5, 6, 7)]
     for tokens, out in ((own_tokens, out_own), (peer_tokens, out_peer)):
         value = dot_rows(rows, tokens[...])
         first = 0
         for n, place in enumerate(places):
-            count = 16 if n < 3 else 8
+            count = 16 if n < 2 else 8
             at = pl.ds(pl.multiple_of(place, 8), count)
             out[at, :] = value[first : first + count]
             first += count
@@ -307,22 +307,22 @@
         send = {}
         for d in range(1, 8):
             block = lax.dynamic_index_in_dim(outgoing, at ^ d, 0, keepdims=False)
-            along = [mine] if d in (2, 3) else [piece] if d < 5 else []
+            along = [mine] if d == 2 else [piece] if d < 5 else []
             send[d] = jnp.concatenate([block] + along, axis=0)
-        for d, before in ((4, 0), (2, 0), (3, 0), (6, 0), (7, 0), (5, 4), (1, 3)):
+        for d, before in ((2, 0), (4, 0), (3, 0), (7, 0), (6, 0), (5, 4), (1, 3)):
             if before:
                 blocks[before], send[d] = lax.optimization_barrier((blocks[before], send[d]))
             if d == 1:
                 send[d] = jnp.concatenate([send[d], blocks[4][CAP:]], axis=0)
             blocks[d] = across(send[d], "expert", d)
-        level_a = jnp.concatenate([mine] + [blocks[d][CAP : CAP + 16] for d in (2, 3)], axis=0)
+        level_a = jnp.concatenate([mine] + [blocks[2][CAP : CAP + 16]], axis=0)
         weights = (gate_weight, up_weight, down_weight)
         blocks[4], *weights = lax.optimization_barrier((blocks[4], *weights))
         held = load(*weights)
         level_b = jnp.concatenate([blocks[4][CAP:], blocks[1][2 * CAP :]], axis=0)
         level_b, *held = lax.optimization_barrier((level_b, *held))
         level_b = jnp.concatenate(
-            [blocks[1][CAP : 2 * CAP], level_b, across(level_b, "expert", 2)], axis=0
+            [blocks[1][CAP : 2 * CAP], blocks[3][CAP:], level_b, across(level_b, "expert", 2)], axis=0
         )
         arrived = jnp.concatenate([blocks[d][:CAP] for d in range(8)], axis=0)
         arrived, *held = lax.optimization_barrier((arrived, *held))

time: 49.5 us -> 49 us (0.990)
  starting transfers between devices: 23.1 us -> 21.7 us
  waiting for transfers between devices: 12.8 us -> 13.7 us
    ppermute x9, waiting for transfers between devices: 9.5 us -> 11.6 us  [across(): return lax.ppermute(value, axis, [(s, s ^ distance) for s in range(size)])]
    ppermute x9, starting transfers between devices: 18.4 us -> 16.5 us  [across(): return lax.ppermute(value, axis, [(s, s ^ distance) for s in range(size)])]
    all_to_all x1, waiting for transfers between devices: 1.73 us -> 0.52 us  [per_device(): lax.all_to_all(summed, 'expert', split_axis=0, concat_axis=0, tiled=True)]
where the time goes in v8:
time: 49 us; the launch traced here: 48.7 us
  starting transfers between devices  21.7 us (44%)
  waiting for transfers between devices  13.7 us (28%)
  Pallas kernels  9.65 us (20%)
  matrix products  1.46 us (3%)
  between operations  0.97 us (2%)
  other arithmetic  0.88 us (2%)
    ppermute x9, starting transfers between devices, across(): return lax.ppermute(value, axis, [(s, s ^ distance) for s in range(size)])  16.5 us
    ppermute x9, waiting for transfers between devices, across(): return lax.ppermute(value, axis, [(s, s ^ distance) for s in range(size)])  11.6 us
    all_to_all x1, starting transfers between devices, per_device(): lax.all_to_all(summed, 'expert', split_axis=0, concat_axis=0, tiled=True)  4.47 us
    pallas_call x1, Pallas kernels, load(): pl.pallas_call(load_kernel, out_shape=tuple((jax.ShapeDtypeStruct(w.shape...  4.23 us
    pallas_call x1, Pallas kernels, ffn(): pl.pallas_call(functools.partial(ffn_kernel, parts, relative), out_shape=...  1.8 us
    ppermute x4, waiting for transfers between devices, swap_cores(): return lax.ppermute(value, 'tensor', SWAP)  1.59 us
    dot_general x1, matrix products, per_device(): jnp.dot(hits.astype(jnp.bfloat16), tokens, preferred_element_type=jnp.flo...  1.46 us
    pallas_call x1, Pallas kernels, combine(): pl.pallas_call(functools.partial(combine_kernel, parts), out_shape=jax.Sh...  1.16 us
  transfers between devices with their start and end apart: 14, of which 8 were waited for; matrix products, arithmetic and copies ran while one was open for 1% of the time, Pallas kernels for 17%

profile of v8, /device:TPU:0, one launch (start us, length us, event | category | flops | bytes accessed | tf_op | source)
XLA Modules:
  0.0 48.7 jit_solution(8298464883261876315)
XLA Ops:
  0.7 0.8 %add_select_fusion = s32[8,128]{1,0:T(8,128)S(1)} fusion(s32[128,8]{0,1:T(8,128)} %param.17, s32[128,8]{0,1:T(8,128)} %param.16), kind=kLoop, calls=%fused_computation.48 | loop fusion | flops 6144 | bytes 12288 | tf_op jit(solution)/shard_map/jit(_where)/select_n | solution.py:42
  1.6 1.5 %fusion = bf16[8,8,3584]{2,1,0:T(8,128)(2,1)S(1)} fusion(bf16[128,3584]{1,0:T(8,128)(2,1)} %own_tokens.1, s32[128]{0:T(128)S(1)} %get-tuple-element.74, s32[128]{0:T(128)S(1)} %get-tuple-element.75, s32[128]{0:T(128)S(1)} %get-tuple-element.76, s32[128]{0:T(128)S(1)} %get-tuple-element.77, s32[128]{0:T(128)S(1)} %get-tuple-element.78, ...), kind=kOutput, calls=%fused_computation.1 | convolution fusion | flops 59072512 | bytes 1380352 | tf_op jit(solution)/shard_map/dot_general | solution.py:300
  3.1 4.1 %collective-permute-start.3 = (bf16[16,3584]{1,0:T(8,128)(2,1)S(1)}, bf16[16,3584]{1,0:T(8,128)(2,1)S(1)}, u32[]{:S(2)}, u32[]{:S(2)}) collective-permute-start(bf16[16,3584]{1,0:T(8,128)(2,1)S(1)} %get-tuple-element.71), channel_id=1, source_target_pairs={{0,8},{2,10},{4,12},{6,14},{8,0},{10,2},{12,4},{14,6},{1,9},{3,11}... | collective-permute-start | bytes 344072 | tf_op jit(solution)/shard_map/ppermute | solution.py:22
  7.2 2.5 %collective-permute-start.2 = (bf16[16,3584]{1,0:T(8,128)(2,1)S(1)}, bf16[16,3584]{1,0:T(8,128)(2,1)S(1)}, u32[]{:S(2)}, u32[]{:S(2)}) collective-permute-start(bf16[16,3584]{1,0:T(8,128)(2,1)S(1)} %get-tuple-element.72), channel_id=1, source_target_pairs={{0,6},{2,4},{4,2},{6,0},{8,14},{10,12},{12,10},{14,8},{1,7},{3,5},... | collective-permute-start | bytes 344072 | tf_op jit(solution)/shard_map/ppermute | solution.py:22
  9.8 0.5 %collective-permute-start.1 = (bf16[24,3584]{1,0:T(8,128)(2,1)S(1)}, bf16[24,3584]{1,0:T(8,128)(2,1)S(1)}, u32[]{:S(2)}, u32[]{:S(2)}) collective-permute-start(bf16[24,3584]{1,0:T(8,128)(2,1)S(1)} %pad_maximum_fusion.2), channel_id=1, source_target_pairs={{0,4},{2,6},{4,0},{6,2},{8,12},{10,14},{12,8},{14,10},{1,5},{3,7},... | collective-permute-start | bytes 516104 | tf_op jit(solution)/shard_map/ppermute | solution.py:22
  10.3 1.3 %collective-permute-start.6 = (bf16[8,3584]{1,0:T(8,128)(2,1)S(1)}, bf16[8,3584]{1,0:T(8,128)(2,1)S(1)}, u32[]{:S(2)}, u32[]{:S(2)}) collective-permute-start(bf16[8,3584]{1,0:T(8,128)(2,1)S(1)} %get-tuple-element.57), channel_id=1, source_target_pairs={{0,12},{2,14},{4,8},{6,10},{8,4},{10,6},{12,0},{14,2},{1,13},{3,15... | collective-permute-start | bytes 172040 | tf_op jit(solution)/shard_map/ppermute | solution.py:22
  11.7 2.4 %collective-permute-start.7 = (bf16[8,3584]{1,0:T(8,128)(2,1)S(1)}, bf16[8,3584]{1,0:T(8,128)(2,1)S(1)}, u32[]{:S(2)}, u32[]{:S(2)}) collective-permute-start(bf16[8,3584]{1,0:T(8,128)(2,1)S(1)} %get-tuple-element.56), channel_id=1, source_target_pairs={{0,14},{2,12},{4,10},{6,8},{8,6},{10,4},{12,2},{14,0},{1,15},{3,13... | collective-permute-start | bytes 172040 | tf_op jit(solution)/shard_map/ppermute | solution.py:22
  14.1 1.3 %collective-permute-done.2 = bf16[16,3584]{1,0:T(8,128)(2,1)S(1)} collective-permute-done((bf16[16,3584]{1,0:T(8,128)(2,1)S(1)}, bf16[16,3584]{1,0:T(8,128)(2,1)S(1)}, u32[]{:S(2)}, u32[]{:S(2)}) %collective-permute-start.2) | collective-permute-done | bytes 114720 | tf_op jit(solution)/shard_map/ppermute | solution.py:22
  15.4 1.1 %collective-permute-start.4 = (bf16[24,3584]{1,0:T(8,128)(2,1)S(1)}, bf16[24,3584]{1,0:T(8,128)(2,1)S(1)}, u32[]{:S(2)}, u32[]{:S(2)}) collective-permute-start(bf16[24,3584]{1,0:T(8,128)(2,1)S(1)} %pad_maximum_fusion.3), channel_id=1, source_target_pairs={{0,2},{2,0},{4,6},{6,4},{8,10},{10,8},{12,14},{14,12},{1,3},{3,1},... | collective-permute-start | bytes 516104 | tf_op jit(solution)/shard_map/ppermute | solution.py:22
  16.5 1.6 %collective-permute-start.5 = (bf16[8,3584]{1,0:T(8,128)(2,1)S(1)}, bf16[8,3584]{1,0:T(8,128)(2,1)S(1)}, u32[]{:S(2)}, u32[]{:S(2)}) collective-permute-start(bf16[8,3584]{1,0:T(8,128)(2,1)S(1)} %get-tuple-element.33), channel_id=1, source_target_pairs={{0,10},{2,8},{4,14},{6,12},{8,2},{10,0},{12,6},{14,4},{1,11},{3,9}... | collective-permute-start | bytes 172040 | tf_op jit(solution)/shard_map/ppermute | solution.py:22
  18.1 4.2 %load.1 = (bf16[1,3584,512]{2,1,0:T(8,128)(2,1)S(1)}, bf16[1,3584,512]{2,1,0:T(8,128)(2,1)S(1)}, bf16[1,512,3584]{2,1,0:T(8,128)(2,1)S(1)}) custom-call(bf16[1,3584,512]{2,1,0:T(8,128)(2,1)} %refs_0_, bf16[1,3584,512]{2,1,0:T(8,128)(2,1)} %refs_1_, bf16[1,512,3584]{2,1,0:T(8,128)(2,1)} %refs_2_), custom_call_target="tpu_custom_call" | custom-call | bytes 11010048 | tf_op jit(solution)/shard_map/load/pallas_call | solution.py:64
  23.3 1.4 %collective-permute-start.10 = (bf16[16,3584]{1,0:T(8,128)(2,1)S(1)}, bf16[16,3584]{1,0:T(8,128)(2,1)S(1)}, u32[]{:S(2)}, u32[]{:S(2)}) collective-permute-start(bf16[16,3584]{1,0:T(8,128)(2,1)S(1)} %pad_maximum_fusion.7), channel_id=1, source_target_pairs={{0,4},{2,6},{4,0},{6,2},{8,12},{10,14},{12,8},{14,10},{1,5},{3,7},... | collective-permute-start | bytes 344072 | tf_op jit(solution)/shard_map/ppermute | solution.py:22
  24.7 0.5 collective-permute-done.8.peer
  25.1 1.8 %ffn.1 = (bf16[64,3584]{1,0:T(8,128)(2,1)S(1)}, bf16[64,3584]{1,0:T(8,128)(2,1)S(1)}) custom-call(bf16[64,3584]{1,0:T(8,128)(2,1)S(1)} %constant_dynamic-update-slice_fusion.own, bf16[64,3584]{1,0:T(8,128)(2,1)S(1)} %collective-permute-done.8.peer, s32[1,16]{1,0:T(1,128)S(1)} %copy-done.4, bf16[1,3584,512]{2,1,0:T(8,128)(2,1)S(1)} %get-tuple-element.44.gate, ...), custom_call_target="tpu_custom_call" | custom-call | flops 1409286144 | bytes 11010048 | tf_op jit(solution)/shard_map/ffn/pallas_call | solution.py:115
  27.5 1.3 %collective-permute-done.10 = bf16[16,3584]{1,0:T(8,128)(2,1)S(1)} collective-permute-done((bf16[16,3584]{1,0:T(8,128)(2,1)S(1)}, bf16[16,3584]{1,0:T(8,128)(2,1)S(1)}, u32[]{:S(2)}, u32[]{:S(2)}) %collective-permute-start.10) | collective-permute-done | bytes 114720 | tf_op jit(solution)/shard_map/ppermute | solution.py:22
  28.9 0.8 %add_halves.1 = bf16[8,8,3584]{2,1,0:T(8,128)(2,1)} custom-call(bf16[64,3584]{1,0:T(8,128)(2,1)S(1)} %get-tuple-element.53.ours, bf16[64,3584]{1,0:T(8,128)(2,1)S(1)} %collective-permute-done.9.other), custom_call_target="tpu_custom_call" | custom-call | flops 229376 | bytes 1376256 | tf_op jit(solution)/shard_map/add_halves/pallas_call | solution.py:143
  29.8 4.5 %all-to-all-start = ((bf16[8,8,3584]{2,1,0:T(8,128)(2,1)}), bf16[8,8,3584]{2,1,0:T(8,128)(2,1)S(1)}, u32[]{:S(2)}, u32[]{:S(2)}) async-start(bf16[8,8,3584]{2,1,0:T(8,128)(2,1)} %add_halves.1), calls=%async_computation | async-start | bytes 917504 | tf_op jit(solution)/shard_map/all_to_all | solution.py:338
  34.2 1.6 %collective-permute-start.11 = (bf16[48,3584]{1,0:T(8,128)(2,1)S(1)}, bf16[48,3584]{1,0:T(8,128)(2,1)S(1)}, u32[]{:S(2)}, u32[]{:S(2)}) collective-permute-start(bf16[48,3584]{1,0:T(8,128)(2,1)S(1)} %pad_maximum_fusion.refs_1_), channel_id=1, source_target_pairs={{0,16},{16,0},{1,17},{17,1},{2,18},{18,2},{3,19},{19,3},{4,20},{20... | collective-permute-start | bytes 1032200 | tf_op jit(solution)/shard_map/ppermute | solution.py:22
  35.8 8.2 %collective-permute-done.11.refs_2_ = bf16[48,3584]{1,0:T(8,128)(2,1)S(1)} collective-permute-done((bf16[48,3584]{1,0:T(8,128)(2,1)S(1)}, bf16[48,3584]{1,0:T(8,128)(2,1)S(1)}, u32[]{:S(2)}, u32[]{:S(2)}) %collective-permute-start.11) | collective-permute-done | bytes 344096 | tf_op jit(solution)/shard_map/ppermute | solution.py:22
  44.1 0.6 %half_logits.1 = (f32[128,128]{1,0:T(8,128)S(1)}, f32[128,128]{1,0:T(8,128)S(1)}) custom-call(bf16[128,3584]{1,0:T(8,128)(2,1)S(1)} %copy-done.1, bf16[128,3584]{1,0:T(8,128)(2,1)S(1)} %collective-permute-done.peer_tokens, bf16[32,3584]{1,0:T(8,128)(2,1)S(1)} %pad_maximum_fusion.1.refs_0_, bf16[48,3584]{1,0:T(8,128)(2,1)S(1)} %pad_maximum_fusion.refs_1_, ...), custom_call_target="tpu_custom_call" | custom-call | flops 234881024 | bytes 2752512 | tf_op jit(solution)/shard_map/half_logits/pallas_call | solution.py:179
  44.9 1.1 %collective-permute-done.12.refs_1_ = f32[128,128]{1,0:T(8,128)S(1)} collective-permute-done((f32[128,128]{1,0:T(8,128)S(1)}, f32[128,128]{1,0:T(8,128)S(1)}, u32[]{:S(2)}, u32[]{:S(2)}) %collective-permute-start.12) | collective-permute-done | bytes 65568 | tf_op jit(solution)/shard_map/ppermute | solution.py:17
  46.0 1.0 %router_terms.1 = (bf16[128,64]{1,0:T(8,128)(2,1)S(1)}, f32[1,128]{1,0:T(1,128)}) custom-call(s32[8,128]{1,0:T(8,128)S(1)} %bitcast.45, s32[8,128]{1,0:T(8,128)S(1)} %bitcast.46, s32[1,128]{1,0:T(1,128)S(1)} %bitcast.47, f32[256,128]{1,0:T(8,128)S(1)} %bitcast.44, f32[128,128]{1,0:T(8,128)S(1)} %get-tuple-element.50.refs_0_, ...), custom_call_target="tpu_custom_call" | custom-call | flops 983040 | bytes 393216 | tf_op jit(solution)/shard_map/router_terms/pallas_call | solution.py:232
  47.0 0.5 %all-to-all-done = bf16[8,8,3584]{2,1,0:T(8,128)(2,1)S(1)} async-done(((bf16[8,8,3584]{2,1,0:T(8,128)(2,1)}), bf16[8,8,3584]{2,1,0:T(8,128)(2,1)S(1)}, u32[]{:S(2)}, u32[]{:S(2)}) %all-to-all-start) | async-done | bytes 458784 | tf_op jit(solution)/shard_map/all_to_all | solution.py:338
  47.6 1.2 %combine.1 = bf16[128,3584]{1,0:T(8,128)(2,1)} custom-call(bf16[128,64]{1,0:T(8,128)(2,1)S(1)} %get-tuple-element.52.weights, bf16[64,3584]{1,0:T(8,128)(2,1)S(1)} %bitcast.43), custom_call_target="tpu_custom_call" | custom-call | flops 58720256 | bytes 917504 | tf_op jit(solution)/shard_map/combine/pallas_call | solution.py:264
  (47 shorter events, 1.9 us)
Async XLA Ops:
  0.6 0.9 %copy-start = (bf16[32,3584]{1,0:T(8,128)(2,1)S(1)}, bf16[32,3584]{1,0:T(8,128)(2,1)}, u32[]{:S(2)}) copy-start(bf16[32,3584]{1,0:T(8,128)(2,1)} %param.11) | copy-start | bytes 688132
  3.1 11.0 %collective-permute-start.3 = (bf16[16,3584]{1,0:T(8,128)(2,1)S(1)}, bf16[16,3584]{1,0:T(8,128)(2,1)S(1)}, u32[]{:S(2)}, u32[]{:S(2)}) collective-permute-start(bf16[16,3584]{1,0:T(8,128)(2,1)S(1)} %get-tuple-element.71), channel_id=1, source_target_pairs={{0,8},{2,10},{4,12},{6,14},{8,0},{10,2},{12,4},{14,6},{1,9},{3,11}... | collective-permute-start | bytes 344072 | tf_op jit(solution)/shard_map/ppermute | solution.py:22
  7.2 8.1 %collective-permute-start.2 = (bf16[16,3584]{1,0:T(8,128)(2,1)S(1)}, bf16[16,3584]{1,0:T(8,128)(2,1)S(1)}, u32[]{:S(2)}, u32[]{:S(2)}) collective-permute-start(bf16[16,3584]{1,0:T(8,128)(2,1)S(1)} %get-tuple-element.72), channel_id=1, source_target_pairs={{0,6},{2,4},{4,2},{6,0},{8,14},{10,12},{12,10},{14,8},{1,7},{3,5},... | collective-permute-start | bytes 344072 | tf_op jit(solution)/shard_map/ppermute | solution.py:22
  9.8 13.0 %collective-permute-start.1 = (bf16[24,3584]{1,0:T(8,128)(2,1)S(1)}, bf16[24,3584]{1,0:T(8,128)(2,1)S(1)}, u32[]{:S(2)}, u32[]{:S(2)}) collective-permute-start(bf16[24,3584]{1,0:T(8,128)(2,1)S(1)} %pad_maximum_fusion.2), channel_id=1, source_target_pairs={{0,4},{2,6},{4,0},{6,2},{8,12},{10,14},{12,8},{14,10},{1,5},{3,7},... | collective-permute-start | bytes 516104 | tf_op jit(solution)/shard_map/ppermute | solution.py:22
  10.3 12.9 %collective-permute-start.6 = (bf16[8,3584]{1,0:T(8,128)(2,1)S(1)}, bf16[8,3584]{1,0:T(8,128)(2,1)S(1)}, u32[]{:S(2)}, u32[]{:S(2)}) collective-permute-start(bf16[8,3584]{1,0:T(8,128)(2,1)S(1)} %get-tuple-element.57), channel_id=1, source_target_pairs={{0,12},{2,14},{4,8},{6,10},{8,4},{10,6},{12,0},{14,2},{1,13},{3,15... | collective-permute-start | bytes 172040 | tf_op jit(solution)/shard_map/ppermute | solution.py:22
  11.7 11.5 %collective-permute-start.7 = (bf16[8,3584]{1,0:T(8,128)(2,1)S(1)}, bf16[8,3584]{1,0:T(8,128)(2,1)S(1)}, u32[]{:S(2)}, u32[]{:S(2)}) collective-permute-start(bf16[8,3584]{1,0:T(8,128)(2,1)S(1)} %get-tuple-element.56), channel_id=1, source_target_pairs={{0,14},{2,12},{4,10},{6,8},{8,6},{10,4},{12,2},{14,0},{1,15},{3,13... | collective-permute-start | bytes 172040 | tf_op jit(solution)/shard_map/ppermute | solution.py:22
  15.4 7.4 %collective-permute-start.4 = (bf16[24,3584]{1,0:T(8,128)(2,1)S(1)}, bf16[24,3584]{1,0:T(8,128)(2,1)S(1)}, u32[]{:S(2)}, u32[]{:S(2)}) collective-permute-start(bf16[24,3584]{1,0:T(8,128)(2,1)S(1)} %pad_maximum_fusion.3), channel_id=1, source_target_pairs={{0,2},{2,0},{4,6},{6,4},{8,10},{10,8},{12,14},{14,12},{1,3},{3,1},... | collective-permute-start | bytes 516104 | tf_op jit(solution)/shard_map/ppermute | solution.py:22
  16.5 8.6 %copy-start.4 = (s32[1,16]{1,0:T(1,128)S(1)}, s32[1,16]{1,0:T(1,128)}, u32[]{:S(2)}) copy-start(s32[1,16]{1,0:T(1,128)} %occupancy.1) | copy-start | bytes 196
  16.5 6.7 %collective-permute-start.5 = (bf16[8,3584]{1,0:T(8,128)(2,1)S(1)}, bf16[8,3584]{1,0:T(8,128)(2,1)S(1)}, u32[]{:S(2)}, u32[]{:S(2)}) collective-permute-start(bf16[8,3584]{1,0:T(8,128)(2,1)S(1)} %get-tuple-element.33), channel_id=1, source_target_pairs={{0,10},{2,8},{4,14},{6,12},{8,2},{10,0},{12,6},{14,4},{1,11},{3,9}... | collective-permute-start | bytes 172040 | tf_op jit(solution)/shard_map/ppermute | solution.py:22
  23.2 4.0 %copy-start.1 = (bf16[128,3584]{1,0:T(8,128)(2,1)S(1)}, bf16[128,3584]{1,0:T(8,128)(2,1)}, u32[]{:S(2)}) copy-start(bf16[128,3584]{1,0:T(8,128)(2,1)} %own_tokens.1) | copy-start | bytes 2752516
  23.2 1.9 %collective-permute-start.8 = (bf16[64,3584]{1,0:T(8,128)(2,1)S(1)}, bf16[64,3584]{1,0:T(8,128)(2,1)S(1)}, u32[]{:S(2)}, u32[]{:S(2)}) collective-permute-start(bf16[64,3584]{1,0:T(8,128)(2,1)S(1)} %constant_dynamic-update-slice_fusion.own), channel_id=1, source_target_pairs={{0,1},{1,0},{2,3},{3,2},{4,5},{5,4},{6,7},{7,6},{8,9},{9,8},{10,11... | collective-permute-start | bytes 1376264 | tf_op jit(solution)/shard_map/ppermute | solution.py:17
  23.3 5.6 %collective-permute-start.10 = (bf16[16,3584]{1,0:T(8,128)(2,1)S(1)}, bf16[16,3584]{1,0:T(8,128)(2,1)S(1)}, u32[]{:S(2)}, u32[]{:S(2)}) collective-permute-start(bf16[16,3584]{1,0:T(8,128)(2,1)S(1)} %pad_maximum_fusion.7), channel_id=1, source_target_pairs={{0,4},{2,6},{4,0},{6,2},{8,12},{10,14},{12,8},{14,10},{1,5},{3,7},... | collective-permute-start | bytes 344072 | tf_op jit(solution)/shard_map/ppermute | solution.py:22
  26.9 17.9 %copy-start.6 = (f32[128,256]{1,0:T(8,128)S(1)}, f32[128,256]{1,0:T(8,128)}, u32[]{:S(2)}) copy-start(f32[128,256]{1,0:T(8,128)} %param.15) | copy-start | bytes 393220
  26.9 19.1 %copy-start.2 = (s32[128,8]{0,1:T(8,128)S(1)}, s32[128,8]{0,1:T(8,128)}, u32[]{:S(2)}) copy-start(s32[128,8]{0,1:T(8,128)} %param.16) | copy-start | bytes 12292
  26.9 19.1 %copy-start.3 = (s32[128,8]{0,1:T(8,128)S(1)}, s32[128,8]{0,1:T(8,128)}, u32[]{:S(2)}) copy-start(s32[128,8]{0,1:T(8,128)} %param.17) | copy-start | bytes 12292
  27.0 19.1 %copy-start.5 = (s32[128]{0:T(128)S(1)}, s32[128]{0:T(128)}, u32[]{:S(2)}) copy-start(s32[128]{0:T(128)} %param.19) | copy-start | bytes 1540
  27.0 1.9 %collective-permute-start.9 = (bf16[64,3584]{1,0:T(8,128)(2,1)S(1)}, bf16[64,3584]{1,0:T(8,128)(2,1)S(1)}, u32[]{:S(2)}, u32[]{:S(2)}) collective-permute-start(bf16[64,3584]{1,0:T(8,128)(2,1)S(1)} %get-tuple-element.47), channel_id=1, source_target_pairs={{0,1},{1,0},{2,3},{3,2},{4,5},{5,4},{6,7},{7,6},{8,9},{9,8},{10,11... | collective-permute-start | bytes 1376264 | tf_op jit(solution)/shard_map/ppermute | solution.py:17
  27.2 8.6 %collective-permute-start = (bf16[128,3584]{1,0:T(8,128)(2,1)S(1)}, bf16[128,3584]{1,0:T(8,128)(2,1)S(1)}, u32[]{:S(2)}, u32[]{:S(2)}) collective-permute-start(bf16[128,3584]{1,0:T(8,128)(2,1)S(1)} %copy-done.1), channel_id=1, source_target_pairs={{0,1},{1,0},{2,3},{3,2},{4,5},{5,4},{6,7},{7,6},{8,9},{9,8},{10,11... | collective-permute-start | bytes 2752520 | tf_op jit(solution)/shard_map/ppermute | solution.py:17
  29.8 17.8 %all-to-all-start = ((bf16[8,8,3584]{2,1,0:T(8,128)(2,1)}), bf16[8,8,3584]{2,1,0:T(8,128)(2,1)S(1)}, u32[]{:S(2)}, u32[]{:S(2)}) async-start(bf16[8,8,3584]{2,1,0:T(8,128)(2,1)} %add_halves.1), calls=%async_computation | async-start | bytes 917504 | tf_op jit(solution)/shard_map/all_to_all | solution.py:338
  34.2 9.8 %collective-permute-start.11 = (bf16[48,3584]{1,0:T(8,128)(2,1)S(1)}, bf16[48,3584]{1,0:T(8,128)(2,1)S(1)}, u32[]{:S(2)}, u32[]{:S(2)}) collective-permute-start(bf16[48,3584]{1,0:T(8,128)(2,1)S(1)} %pad_maximum_fusion.refs_1_), channel_id=1, source_target_pairs={{0,16},{16,0},{1,17},{17,1},{2,18},{18,2},{3,19},{19,3},{4,20},{20... | collective-permute-start | bytes 1032200 | tf_op jit(solution)/shard_map/ppermute | solution.py:22
  44.7 1.3 %collective-permute-start.12 = (f32[128,128]{1,0:T(8,128)S(1)}, f32[128,128]{1,0:T(8,128)S(1)}, u32[]{:S(2)}, u32[]{:S(2)}) collective-permute-start(f32[128,128]{1,0:T(8,128)S(1)} %get-tuple-element.51), channel_id=1, source_target_pairs={{0,1},{1,0},{2,3},{3,2},{4,5},{5,4},{6,7},{7,6},{8,9},{9,8},{10,11... | collective-permute-start | bytes 196616 | tf_op jit(solution)/shard_map/ppermute | solution.py:17

commit v9 on v8

--- a/solution.py
+++ b/solution.py
@@ -309,7 +309,7 @@
             block = lax.dynamic_index_in_dim(outgoing, at ^ d, 0, keepdims=False)
             along = [mine] if d == 2 else [piece] if d < 5 else []
             send[d] = jnp.concatenate([block] + along, axis=0)
-        for d, before in ((2, 0), (4, 0), (3, 0), (7, 0), (6, 0), (5, 4), (1, 3)):
+        for d, before in ((4, 0), (2, 0), (3, 0), (6, 0), (7, 0), (5, 4), (1, 3)):
             if before:
                 blocks[before], send[d] = lax.optimization_barrier((blocks[before], send[d]))
             if d == 1:

time: 49 us -> 49 us (level)
  no operation moved by 1% of the time
where the time goes in v9:
time: 49 us; the launch traced here: 48.7 us
  starting transfers between devices  21.7 us (44%)
  waiting for transfers between devices  13.7 us (28%)
  Pallas kernels  9.65 us (20%)
  matrix products  1.46 us (3%)
  between operations  0.97 us (2%)
  other arithmetic  0.88 us (2%)
    ppermute x9, starting transfers between devices, across(): return lax.ppermute(value, axis, [(s, s ^ distance) for s in range(size)])  16.5 us
    ppermute x9, waiting for transfers between devices, across(): return lax.ppermute(value, axis, [(s, s ^ distance) for s in range(size)])  11.6 us
    all_to_all x1, starting transfers between devices, per_device(): lax.all_to_all(summed, 'expert', split_axis=0, concat_axis=0, tiled=True)  4.47 us
    pallas_call x1, Pallas kernels, load(): pl.pallas_call(load_kernel, out_shape=tuple((jax.ShapeDtypeStruct(w.shape...  4.23 us
    pallas_call x1, Pallas kernels, ffn(): pl.pallas_call(functools.partial(ffn_kernel, parts, relative), out_shape=...  1.8 us
    ppermute x4, waiting for transfers between devices, swap_cores(): return lax.ppermute(value, 'tensor', SWAP)  1.59 us
    dot_general x1, matrix products, per_device(): jnp.dot(hits.astype(jnp.bfloat16), tokens, preferred_element_type=jnp.flo...  1.46 us
    pallas_call x1, Pallas kernels, combine(): pl.pallas_call(functools.partial(combine_kernel, parts), out_shape=jax.Sh...  1.16 us
  transfers between devices with their start and end apart: 14, of which 8 were waited for; matrix products, arithmetic and copies ran while one was open for 1% of the time, Pallas kernels for 17%

profile of v9, /device:TPU:0, one launch (start us, length us, event | category | flops | bytes accessed | tf_op | source)
XLA Modules:
  0.0 48.7 jit_solution(8298464883261876315)
XLA Ops:
  0.7 0.8 %add_select_fusion = s32[8,128]{1,0:T(8,128)S(1)} fusion(s32[128,8]{0,1:T(8,128)} %param.17, s32[128,8]{0,1:T(8,128)} %param.16), kind=kLoop, calls=%fused_computation.48 | loop fusion | flops 6144 | bytes 12288 | tf_op jit(solution)/shard_map/jit(_where)/select_n | solution.py:42
  1.6 1.5 %fusion = bf16[8,8,3584]{2,1,0:T(8,128)(2,1)S(1)} fusion(bf16[128,3584]{1,0:T(8,128)(2,1)} %own_tokens.1, s32[128]{0:T(128)S(1)} %get-tuple-element.74, s32[128]{0:T(128)S(1)} %get-tuple-element.75, s32[128]{0:T(128)S(1)} %get-tuple-element.76, s32[128]{0:T(128)S(1)} %get-tuple-element.77, s32[128]{0:T(128)S(1)} %get-tuple-element.78, ...), kind=kOutput, calls=%fused_computation.1 | convolution fusion | flops 59072512 | bytes 1380352 | tf_op jit(solution)/shard_map/dot_general | solution.py:300
  3.1 4.1 %collective-permute-start.3 = (bf16[16,3584]{1,0:T(8,128)(2,1)S(1)}, bf16[16,3584]{1,0:T(8,128)(2,1)S(1)}, u32[]{:S(2)}, u32[]{:S(2)}) collective-permute-start(bf16[16,3584]{1,0:T(8,128)(2,1)S(1)} %get-tuple-element.71), channel_id=1, source_target_pairs={{0,8},{2,10},{4,12},{6,14},{8,0},{10,2},{12,4},{14,6},{1,9},{3,11}... | collective-permute-start | bytes 344072 | tf_op jit(solution)/shard_map/ppermute | solution.py:22
  7.2 2.5 %collective-permute-start.2 = (bf16[16,3584]{1,0:T(8,128)(2,1)S(1)}, bf16[16,3584]{1,0:T(8,128)(2,1)S(1)}, u32[]{:S(2)}, u32[]{:S(2)}) collective-permute-start(bf16[16,3584]{1,0:T(8,128)(2,1)S(1)} %get-tuple-element.72), channel_id=1, source_target_pairs={{0,6},{2,4},{4,2},{6,0},{8,14},{10,12},{12,10},{14,8},{1,7},{3,5},... | collective-permute-start | bytes 344072 | tf_op jit(solution)/shard_map/ppermute | solution.py:22
  9.8 0.5 %collective-permute-start.1 = (bf16[24,3584]{1,0:T(8,128)(2,1)S(1)}, bf16[24,3584]{1,0:T(8,128)(2,1)S(1)}, u32[]{:S(2)}, u32[]{:S(2)}) collective-permute-start(bf16[24,3584]{1,0:T(8,128)(2,1)S(1)} %pad_maximum_fusion.2), channel_id=1, source_target_pairs={{0,4},{2,6},{4,0},{6,2},{8,12},{10,14},{12,8},{14,10},{1,5},{3,7},... | collective-permute-start | bytes 516104 | tf_op jit(solution)/shard_map/ppermute | solution.py:22
  10.3 1.3 %collective-permute-start.6 = (bf16[8,3584]{1,0:T(8,128)(2,1)S(1)}, bf16[8,3584]{1,0:T(8,128)(2,1)S(1)}, u32[]{:S(2)}, u32[]{:S(2)}) collective-permute-start(bf16[8,3584]{1,0:T(8,128)(2,1)S(1)} %get-tuple-element.57), channel_id=1, source_target_pairs={{0,12},{2,14},{4,8},{6,10},{8,4},{10,6},{12,0},{14,2},{1,13},{3,15... | collective-permute-start | bytes 172040 | tf_op jit(solution)/shard_map/ppermute | solution.py:22
  11.7 2.4 %collective-permute-start.7 = (bf16[8,3584]{1,0:T(8,128)(2,1)S(1)}, bf16[8,3584]{1,0:T(8,128)(2,1)S(1)}, u32[]{:S(2)}, u32[]{:S(2)}) collective-permute-start(bf16[8,3584]{1,0:T(8,128)(2,1)S(1)} %get-tuple-element.56), channel_id=1, source_target_pairs={{0,14},{2,12},{4,10},{6,8},{8,6},{10,4},{12,2},{14,0},{1,15},{3,13... | collective-permute-start | bytes 172040 | tf_op jit(solution)/shard_map/ppermute | solution.py:22
  14.1 1.3 %collective-permute-done.2 = bf16[16,3584]{1,0:T(8,128)(2,1)S(1)} collective-permute-done((bf16[16,3584]{1,0:T(8,128)(2,1)S(1)}, bf16[16,3584]{1,0:T(8,128)(2,1)S(1)}, u32[]{:S(2)}, u32[]{:S(2)}) %collective-permute-start.2) | collective-permute-done | bytes 114720 | tf_op jit(solution)/shard_map/ppermute | solution.py:22
  15.4 1.1 %collective-permute-start.4 = (bf16[24,3584]{1,0:T(8,128)(2,1)S(1)}, bf16[24,3584]{1,0:T(8,128)(2,1)S(1)}, u32[]{:S(2)}, u32[]{:S(2)}) collective-permute-start(bf16[24,3584]{1,0:T(8,128)(2,1)S(1)} %pad_maximum_fusion.3), channel_id=1, source_target_pairs={{0,2},{2,0},{4,6},{6,4},{8,10},{10,8},{12,14},{14,12},{1,3},{3,1},... | collective-permute-start | bytes 516104 | tf_op jit(solution)/shard_map/ppermute | solution.py:22
  16.5 1.6 %collective-permute-start.5 = (bf16[8,3584]{1,0:T(8,128)(2,1)S(1)}, bf16[8,3584]{1,0:T(8,128)(2,1)S(1)}, u32[]{:S(2)}, u32[]{:S(2)}) collective-permute-start(bf16[8,3584]{1,0:T(8,128)(2,1)S(1)} %get-tuple-element.33), channel_id=1, source_target_pairs={{0,10},{2,8},{4,14},{6,12},{8,2},{10,0},{12,6},{14,4},{1,11},{3,9}... | collective-permute-start | bytes 172040 | tf_op jit(solution)/shard_map/ppermute | solution.py:22
  18.1 4.2 %load.1 = (bf16[1,3584,512]{2,1,0:T(8,128)(2,1)S(1)}, bf16[1,3584,512]{2,1,0:T(8,128)(2,1)S(1)}, bf16[1,512,3584]{2,1,0:T(8,128)(2,1)S(1)}) custom-call(bf16[1,3584,512]{2,1,0:T(8,128)(2,1)} %refs_0_, bf16[1,3584,512]{2,1,0:T(8,128)(2,1)} %refs_1_, bf16[1,512,3584]{2,1,0:T(8,128)(2,1)} %refs_2_), custom_call_target="tpu_custom_call" | custom-call | bytes 11010048 | tf_op jit(solution)/shard_map/load/pallas_call | solution.py:64
  23.3 1.4 %collective-permute-start.10 = (bf16[16,3584]{1,0:T(8,128)(2,1)S(1)}, bf16[16,3584]{1,0:T(8,128)(2,1)S(1)}, u32[]{:S(2)}, u32[]{:S(2)}) collective-permute-start(bf16[16,3584]{1,0:T(8,128)(2,1)S(1)} %pad_maximum_fusion.7), channel_id=1, source_target_pairs={{0,4},{2,6},{4,0},{6,2},{8,12},{10,14},{12,8},{14,10},{1,5},{3,7},... | collective-permute-start | bytes 344072 | tf_op jit(solution)/shard_map/ppermute | solution.py:22
  24.7 0.5 collective-permute-done.8.peer
  25.1 1.8 %ffn.1 = (bf16[64,3584]{1,0:T(8,128)(2,1)S(1)}, bf16[64,3584]{1,0:T(8,128)(2,1)S(1)}) custom-call(bf16[64,3584]{1,0:T(8,128)(2,1)S(1)} %constant_dynamic-update-slice_fusion.own, bf16[64,3584]{1,0:T(8,128)(2,1)S(1)} %collective-permute-done.8.peer, s32[1,16]{1,0:T(1,128)S(1)} %copy-done.4, bf16[1,3584,512]{2,1,0:T(8,128)(2,1)S(1)} %get-tuple-element.44.gate, ...), custom_call_target="tpu_custom_call" | custom-call | flops 1409286144 | bytes 11010048 | tf_op jit(solution)/shard_map/ffn/pallas_call | solution.py:115
  27.5 1.3 %collective-permute-done.10 = bf16[16,3584]{1,0:T(8,128)(2,1)S(1)} collective-permute-done((bf16[16,3584]{1,0:T(8,128)(2,1)S(1)}, bf16[16,3584]{1,0:T(8,128)(2,1)S(1)}, u32[]{:S(2)}, u32[]{:S(2)}) %collective-permute-start.10) | collective-permute-done | bytes 114720 | tf_op jit(solution)/shard_map/ppermute | solution.py:22
  28.9 0.8 %add_halves.1 = bf16[8,8,3584]{2,1,0:T(8,128)(2,1)} custom-call(bf16[64,3584]{1,0:T(8,128)(2,1)S(1)} %get-tuple-element.53.ours, bf16[64,3584]{1,0:T(8,128)(2,1)S(1)} %collective-permute-done.9.other), custom_call_target="tpu_custom_call" | custom-call | flops 229376 | bytes 1376256 | tf_op jit(solution)/shard_map/add_halves/pallas_call | solution.py:143
  29.8 4.5 %all-to-all-start = ((bf16[8,8,3584]{2,1,0:T(8,128)(2,1)}), bf16[8,8,3584]{2,1,0:T(8,128)(2,1)S(1)}, u32[]{:S(2)}, u32[]{:S(2)}) async-start(bf16[8,8,3584]{2,1,0:T(8,128)(2,1)} %add_halves.1), calls=%async_computation | async-start | bytes 917504 | tf_op jit(solution)/shard_map/all_to_all | solution.py:338
  34.2 1.6 %collective-permute-start.11 = (bf16[48,3584]{1,0:T(8,128)(2,1)S(1)}, bf16[48,3584]{1,0:T(8,128)(2,1)S(1)}, u32[]{:S(2)}, u32[]{:S(2)}) collective-permute-start(bf16[48,3584]{1,0:T(8,128)(2,1)S(1)} %pad_maximum_fusion.refs_1_), channel_id=1, source_target_pairs={{0,16},{16,0},{1,17},{17,1},{2,18},{18,2},{3,19},{19,3},{4,20},{20... | collective-permute-start | bytes 1032200 | tf_op jit(solution)/shard_map/ppermute | solution.py:22
  35.8 8.2 %collective-permute-done.11.refs_2_ = bf16[48,3584]{1,0:T(8,128)(2,1)S(1)} collective-permute-done((bf16[48,3584]{1,0:T(8,128)(2,1)S(1)}, bf16[48,3584]{1,0:T(8,128)(2,1)S(1)}, u32[]{:S(2)}, u32[]{:S(2)}) %collective-permute-start.11) | collective-permute-done | bytes 344096 | tf_op jit(solution)/shard_map/ppermute | solution.py:22
  44.1 0.6 %half_logits.1 = (f32[128,128]{1,0:T(8,128)S(1)}, f32[128,128]{1,0:T(8,128)S(1)}) custom-call(bf16[128,3584]{1,0:T(8,128)(2,1)S(1)} %copy-done.1, bf16[128,3584]{1,0:T(8,128)(2,1)S(1)} %collective-permute-done.peer_tokens, bf16[32,3584]{1,0:T(8,128)(2,1)S(1)} %pad_maximum_fusion.1.refs_0_, bf16[48,3584]{1,0:T(8,128)(2,1)S(1)} %pad_maximum_fusion.refs_1_, ...), custom_call_target="tpu_custom_call" | custom-call | flops 234881024 | bytes 2752512 | tf_op jit(solution)/shard_map/half_logits/pallas_call | solution.py:179
  44.9 1.1 %collective-permute-done.12.refs_1_ = f32[128,128]{1,0:T(8,128)S(1)} collective-permute-done((f32[128,128]{1,0:T(8,128)S(1)}, f32[128,128]{1,0:T(8,128)S(1)}, u32[]{:S(2)}, u32[]{:S(2)}) %collective-permute-start.12) | collective-permute-done | bytes 65568 | tf_op jit(solution)/shard_map/ppermute | solution.py:17
  46.0 1.0 %router_terms.1 = (bf16[128,64]{1,0:T(8,128)(2,1)S(1)}, f32[1,128]{1,0:T(1,128)}) custom-call(s32[8,128]{1,0:T(8,128)S(1)} %bitcast.45, s32[8,128]{1,0:T(8,128)S(1)} %bitcast.46, s32[1,128]{1,0:T(1,128)S(1)} %bitcast.47, f32[256,128]{1,0:T(8,128)S(1)} %bitcast.44, f32[128,128]{1,0:T(8,128)S(1)} %get-tuple-element.50.refs_0_, ...), custom_call_target="tpu_custom_call" | custom-call | flops 983040 | bytes 393216 | tf_op jit(solution)/shard_map/router_terms/pallas_call | solution.py:232
  47.0 0.5 %all-to-all-done = bf16[8,8,3584]{2,1,0:T(8,128)(2,1)S(1)} async-done(((bf16[8,8,3584]{2,1,0:T(8,128)(2,1)}), bf16[8,8,3584]{2,1,0:T(8,128)(2,1)S(1)}, u32[]{:S(2)}, u32[]{:S(2)}) %all-to-all-start) | async-done | bytes 458784 | tf_op jit(solution)/shard_map/all_to_all | solution.py:338
  47.6 1.2 %combine.1 = bf16[128,3584]{1,0:T(8,128)(2,1)} custom-call(bf16[128,64]{1,0:T(8,128)(2,1)S(1)} %get-tuple-element.52.weights, bf16[64,3584]{1,0:T(8,128)(2,1)S(1)} %bitcast.43), custom_call_target="tpu_custom_call" | custom-call | flops 58720256 | bytes 917504 | tf_op jit(solution)/shard_map/combine/pallas_call | solution.py:264
  (47 shorter events, 1.9 us)
Async XLA Ops:
  0.6 0.9 %copy-start = (bf16[32,3584]{1,0:T(8,128)(2,1)S(1)}, bf16[32,3584]{1,0:T(8,128)(2,1)}, u32[]{:S(2)}) copy-start(bf16[32,3584]{1,0:T(8,128)(2,1)} %param.11) | copy-start | bytes 688132
  3.1 11.0 %collective-permute-start.3 = (bf16[16,3584]{1,0:T(8,128)(2,1)S(1)}, bf16[16,3584]{1,0:T(8,128)(2,1)S(1)}, u32[]{:S(2)}, u32[]{:S(2)}) collective-permute-start(bf16[16,3584]{1,0:T(8,128)(2,1)S(1)} %get-tuple-element.71), channel_id=1, source_target_pairs={{0,8},{2,10},{4,12},{6,14},{8,0},{10,2},{12,4},{14,6},{1,9},{3,11}... | collective-permute-start | bytes 344072 | tf_op jit(solution)/shard_map/ppermute | solution.py:22
  7.2 8.1 %collective-permute-start.2 = (bf16[16,3584]{1,0:T(8,128)(2,1)S(1)}, bf16[16,3584]{1,0:T(8,128)(2,1)S(1)}, u32[]{:S(2)}, u32[]{:S(2)}) collective-permute-start(bf16[16,3584]{1,0:T(8,128)(2,1)S(1)} %get-tuple-element.72), channel_id=1, source_target_pairs={{0,6},{2,4},{4,2},{6,0},{8,14},{10,12},{12,10},{14,8},{1,7},{3,5},... | collective-permute-start | bytes 344072 | tf_op jit(solution)/shard_map/ppermute | solution.py:22
  9.8 13.0 %collective-permute-start.1 = (bf16[24,3584]{1,0:T(8,128)(2,1)S(1)}, bf16[24,3584]{1,0:T(8,128)(2,1)S(1)}, u32[]{:S(2)}, u32[]{:S(2)}) collective-permute-start(bf16[24,3584]{1,0:T(8,128)(2,1)S(1)} %pad_maximum_fusion.2), channel_id=1, source_target_pairs={{0,4},{2,6},{4,0},{6,2},{8,12},{10,14},{12,8},{14,10},{1,5},{3,7},... | collective-permute-start | bytes 516104 | tf_op jit(solution)/shard_map/ppermute | solution.py:22
  10.3 12.9 %collective-permute-start.6 = (bf16[8,3584]{1,0:T(8,128)(2,1)S(1)}, bf16[8,3584]{1,0:T(8,128)(2,1)S(1)}, u32[]{:S(2)}, u32[]{:S(2)}) collective-permute-start(bf16[8,3584]{1,0:T(8,128)(2,1)S(1)} %get-tuple-element.57), channel_id=1, source_target_pairs={{0,12},{2,14},{4,8},{6,10},{8,4},{10,6},{12,0},{14,2},{1,13},{3,15... | collective-permute-start | bytes 172040 | tf_op jit(solution)/shard_map/ppermute | solution.py:22
  11.7 11.5 %collective-permute-start.7 = (bf16[8,3584]{1,0:T(8,128)(2,1)S(1)}, bf16[8,3584]{1,0:T(8,128)(2,1)S(1)}, u32[]{:S(2)}, u32[]{:S(2)}) collective-permute-start(bf16[8,3584]{1,0:T(8,128)(2,1)S(1)} %get-tuple-element.56), channel_id=1, source_target_pairs={{0,14},{2,12},{4,10},{6,8},{8,6},{10,4},{12,2},{14,0},{1,15},{3,13... | collective-permute-start | bytes 172040 | tf_op jit(solution)/shard_map/ppermute | solution.py:22
  15.4 7.4 %collective-permute-start.4 = (bf16[24,3584]{1,0:T(8,128)(2,1)S(1)}, bf16[24,3584]{1,0:T(8,128)(2,1)S(1)}, u32[]{:S(2)}, u32[]{:S(2)}) collective-permute-start(bf16[24,3584]{1,0:T(8,128)(2,1)S(1)} %pad_maximum_fusion.3), channel_id=1, source_target_pairs={{0,2},{2,0},{4,6},{6,4},{8,10},{10,8},{12,14},{14,12},{1,3},{3,1},... | collective-permute-start | bytes 516104 | tf_op jit(solution)/shard_map/ppermute | solution.py:22
  16.5 8.6 %copy-start.4 = (s32[1,16]{1,0:T(1,128)S(1)}, s32[1,16]{1,0:T(1,128)}, u32[]{:S(2)}) copy-start(s32[1,16]{1,0:T(1,128)} %occupancy.1) | copy-start | bytes 196
  16.5 6.7 %collective-permute-start.5 = (bf16[8,3584]{1,0:T(8,128)(2,1)S(1)}, bf16[8,3584]{1,0:T(8,128)(2,1)S(1)}, u32[]{:S(2)}, u32[]{:S(2)}) collective-permute-start(bf16[8,3584]{1,0:T(8,128)(2,1)S(1)} %get-tuple-element.33), channel_id=1, source_target_pairs={{0,10},{2,8},{4,14},{6,12},{8,2},{10,0},{12,6},{14,4},{1,11},{3,9}... | collective-permute-start | bytes 172040 | tf_op jit(solution)/shard_map/ppermute | solution.py:22
  23.2 4.0 %copy-start.1 = (bf16[128,3584]{1,0:T(8,128)(2,1)S(1)}, bf16[128,3584]{1,0:T(8,128)(2,1)}, u32[]{:S(2)}) copy-start(bf16[128,3584]{1,0:T(8,128)(2,1)} %own_tokens.1) | copy-start | bytes 2752516
  23.2 1.9 %collective-permute-start.8 = (bf16[64,3584]{1,0:T(8,128)(2,1)S(1)}, bf16[64,3584]{1,0:T(8,128)(2,1)S(1)}, u32[]{:S(2)}, u32[]{:S(2)}) collective-permute-start(bf16[64,3584]{1,0:T(8,128)(2,1)S(1)} %constant_dynamic-update-slice_fusion.own), channel_id=1, source_target_pairs={{0,1},{1,0},{2,3},{3,2},{4,5},{5,4},{6,7},{7,6},{8,9},{9,8},{10,11... | collective-permute-start | bytes 1376264 | tf_op jit(solution)/shard_map/ppermute | solution.py:17
  23.3 5.6 %collective-permute-start.10 = (bf16[16,3584]{1,0:T(8,128)(2,1)S(1)}, bf16[16,3584]{1,0:T(8,128)(2,1)S(1)}, u32[]{:S(2)}, u32[]{:S(2)}) collective-permute-start(bf16[16,3584]{1,0:T(8,128)(2,1)S(1)} %pad_maximum_fusion.7), channel_id=1, source_target_pairs={{0,4},{2,6},{4,0},{6,2},{8,12},{10,14},{12,8},{14,10},{1,5},{3,7},... | collective-permute-start | bytes 344072 | tf_op jit(solution)/shard_map/ppermute | solution.py:22
  26.9 17.9 %copy-start.6 = (f32[128,256]{1,0:T(8,128)S(1)}, f32[128,256]{1,0:T(8,128)}, u32[]{:S(2)}) copy-start(f32[128,256]{1,0:T(8,128)} %param.15) | copy-start | bytes 393220
  26.9 19.1 %copy-start.2 = (s32[128,8]{0,1:T(8,128)S(1)}, s32[128,8]{0,1:T(8,128)}, u32[]{:S(2)}) copy-start(s32[128,8]{0,1:T(8,128)} %param.16) | copy-start | bytes 12292
  26.9 19.1 %copy-start.3 = (s32[128,8]{0,1:T(8,128)S(1)}, s32[128,8]{0,1:T(8,128)}, u32[]{:S(2)}) copy-start(s32[128,8]{0,1:T(8,128)} %param.17) | copy-start | bytes 12292
  27.0 19.1 %copy-start.5 = (s32[128]{0:T(128)S(1)}, s32[128]{0:T(128)}, u32[]{:S(2)}) copy-start(s32[128]{0:T(128)} %param.19) | copy-start | bytes 1540
  27.0 1.9 %collective-permute-start.9 = (bf16[64,3584]{1,0:T(8,128)(2,1)S(1)}, bf16[64,3584]{1,0:T(8,128)(2,1)S(1)}, u32[]{:S(2)}, u32[]{:S(2)}) collective-permute-start(bf16[64,3584]{1,0:T(8,128)(2,1)S(1)} %get-tuple-element.47), channel_id=1, source_target_pairs={{0,1},{1,0},{2,3},{3,2},{4,5},{5,4},{6,7},{7,6},{8,9},{9,8},{10,11... | collective-permute-start | bytes 1376264 | tf_op jit(solution)/shard_map/ppermute | solution.py:17
  27.2 8.6 %collective-permute-start = (bf16[128,3584]{1,0:T(8,128)(2,1)S(1)}, bf16[128,3584]{1,0:T(8,128)(2,1)S(1)}, u32[]{:S(2)}, u32[]{:S(2)}) collective-permute-start(bf16[128,3584]{1,0:T(8,128)(2,1)S(1)} %copy-done.1), channel_id=1, source_target_pairs={{0,1},{1,0},{2,3},{3,2},{4,5},{5,4},{6,7},{7,6},{8,9},{9,8},{10,11... | collective-permute-start | bytes 2752520 | tf_op jit(solution)/shard_map/ppermute | solution.py:17
  29.8 17.8 %all-to-all-start = ((bf16[8,8,3584]{2,1,0:T(8,128)(2,1)}), bf16[8,8,3584]{2,1,0:T(8,128)(2,1)S(1)}, u32[]{:S(2)}, u32[]{:S(2)}) async-start(bf16[8,8,3584]{2,1,0:T(8,128)(2,1)} %add_halves.1), calls=%async_computation | async-start | bytes 917504 | tf_op jit(solution)/shard_map/all_to_all | solution.py:338
  34.2 9.8 %collective-permute-start.11 = (bf16[48,3584]{1,0:T(8,128)(2,1)S(1)}, bf16[48,3584]{1,0:T(8,128)(2,1)S(1)}, u32[]{:S(2)}, u32[]{:S(2)}) collective-permute-start(bf16[48,3584]{1,0:T(8,128)(2,1)S(1)} %pad_maximum_fusion.refs_1_), channel_id=1, source_target_pairs={{0,16},{16,0},{1,17},{17,1},{2,18},{18,2},{3,19},{19,3},{4,20},{20... | collective-permute-start | bytes 1032200 | tf_op jit(solution)/shard_map/ppermute | solution.py:22
  44.7 1.3 %collective-permute-start.12 = (f32[128,128]{1,0:T(8,128)S(1)}, f32[128,128]{1,0:T(8,128)S(1)}, u32[]{:S(2)}, u32[]{:S(2)}) collective-permute-start(f32[128,128]{1,0:T(8,128)S(1)} %get-tuple-element.51), channel_id=1, source_target_pairs={{0,1},{1,0},{2,3},{3,2},{4,5},{5,4},{6,7},{7,6},{8,9},{9,8},{10,11... | collective-permute-start | bytes 196616 | tf_op jit(solution)/shard_map/ppermute | solution.py:17
